TPU v7x, 32 devices: a whole 2x2x4 slice. The times are simulated.
32 devices in a mesh: parts: 2 (over y), space: 4 (over z), comp: 2 (over x), lev: 2 (over core).
Axes of the slice: x: 2, y: 2, z: 4, core: 2. Of those that a mesh axis runs over, the one named last changes fastest.
Arguments:
- atmos_state: float32 [16, 16, 1024], P(('parts', 'lev'), None, ('space', 'comp')), parts along dimension 0, may hold values from -6 to 6
- ocean_state: float32 [32, 8, 512], P(('parts', 'lev'), ('space', 'comp')), parts along dimension 0, may hold values from -6 to 6
- vertical_mixing: float32 [8, 8], replicated, may hold values from -2 to 2
- flux_coupling: float32 [16, 8], replicated, may hold values from -2 to 2
- request_cells: int32 [8, 8, 256], P(('space', 'comp')), may hold values from 0 to 2047, as said below
- margin_slot: int32 [4, 8, 512], P(None, ('space', 'comp')), may hold values from 0 to 2047, as said below
- margin_weight: float32 [4, 8, 512], P(None, ('space', 'comp')), may hold values from 0.1 to 0.5
- sea_mask: int32 [8, 512], P(('space', 'comp')), may hold values from 0 to 1, as said below
Outputs:
- atmos_next: float32 [16, 16, 1024], P(('parts', 'lev'), None, ('space', 'comp')), parts along dimension 0
- ocean_next: float32 [32, 8, 512], P(('parts', 'lev'), ('space', 'comp')), parts along dimension 0
- returned: float32 [32, 16, 1024], P(('parts', 'lev'), None, ('space', 'comp')), parts along dimension 0
There are 2 independent parts, one for each index of `parts`. A program takes and returns all parts, laid end to end along the dimension named above; an argument that names none is the same for every part. Nothing has to cross between parts.
Inputs may be any that keep to these rules, and one draw needn't show every extreme that they name: `request_cells`: entry [s, d, r] is the local cell of atmosphere strip s whose flux fills slot r for ocean strip d; slots that no sea margin names hold 0. `margin_slot`: for ocean cell (x, y) the source strip is s = y // 64. On sea cells the slots in use from strip s to ocean strip d are 0 to 4 times the sea cells of d in s's columns, minus 1, each named by one margin; on land cells slot r = k. The named atmosphere cell lies in column 2 y or 2 y + 1 and a row from 2 x - 1 to 2 x + 2. The last strip fills all 256 slots of every ocean strip; strips further west carry fewer, down to none. `sea_mask`: land lies west of a coastline that varies from row to row, with scattered islands.
All inputs are finite; a program needn't handle non-finite values.
Results may differ from a plain program's by a relative error of at most 0.0001.
Values sent between devices are 32-bit elements; how exact they have to be, the bound alone decides.
No kernel may reach another device: no remote copies, remote signals or barrier semaphores. Data moves between devices by JAX's collectives and lax.ppermute only.
A program may use at most 128 MiB of HBM per device.

v0:
```python
import jax
import jax.numpy as jnp
from jax import lax
from jax.sharding import PartitionSpec as P

ASUB = 2
SUB = 8


DIFFUSE = 0.2
TENDENCY = 0.25
OCEAN_MIX = 0.2
FORCING = 0.15


def with_halo(cells, sides, width):
    for axis, dim in sides:
        count = lax.axis_size(axis)
        ends = count - 1
        head = lax.slice_in_dim(cells, 0, width, axis=dim)
        tail = lax.slice_in_dim(cells, cells.shape[dim] - width, cells.shape[dim], axis=dim)
        cells = jnp.concatenate(
            [
                lax.ppermute(tail, axis, [(i, (i + 1) % count) for i in range(ends)]),
                cells,
                lax.ppermute(head, axis, [((i + 1) % count, i) for i in range(ends)]),
            ],
            axis=dim,
        )
    return cells


def atmos_step(atmos, mixing_rows):
    lev_local = atmos.shape[0]
    padded = with_halo(atmos, ((("space", "comp"), 2),), 1)
    padded = jnp.pad(padded, ((0, 0), (1, 1), (0, 0)))
    beside = padded[:, 2:, 1:-1] + padded[:, :-2, 1:-1] + padded[:, 1:-1, 2:] + padded[:, 1:-1, :-2]
    shaded = jnp.tanh(atmos).reshape(lev_local, -1)
    column = jnp.dot(
        mixing_rows,
        lax.all_gather(shaded, "lev", axis=0, tiled=True),
        precision=lax.Precision.HIGHEST,
    )
    return atmos + DIFFUSE * (beside - 4.0 * atmos) + TENDENCY * column.reshape(atmos.shape)


def advance(padded, wetness, forcing):
    centre = padded[:, 1:-1, 1:-1]
    beside = padded[:, 2:, 1:-1] + padded[:, :-2, 1:-1] + padded[:, 1:-1, 2:] + padded[:, 1:-1, :-2]
    return wetness[None] * (centre + OCEAN_MIX * (beside - 4.0 * centre) + FORCING * forcing)


def shards(
    atmos_state,
    ocean_state,
    vertical_mixing,
    flux_coupling,
    request_cells,
    margin_slot,
    margin_weight,
    sea_mask,
):
    lev_local, rows_atmos, cols_atmos = atmos_state.shape
    fields_local = ocean_state.shape[0]
    margins = margin_slot.shape[0]
    lev_place = lax.axis_index("lev")
    mixing_rows = lax.dynamic_slice_in_dim(vertical_mixing, lev_place * lev_local, lev_local, 0)
    coupling_cols = lax.dynamic_slice_in_dim(flux_coupling, lev_place * lev_local, lev_local, 1)
    atmos = atmos_state
    for substep in range(ASUB):
        atmos = atmos_step(atmos, mixing_rows)
    flat_atmos = atmos.reshape(lev_local, -1)
    fluxes = lax.psum_scatter(
        jnp.dot(coupling_cols, flat_atmos, precision=lax.Precision.HIGHEST),
        "lev",
        scatter_dimension=0,
        tiled=True,
    )
    requests = request_cells.reshape(-1)
    outgoing = jnp.take(fluxes, requests, axis=1)
    slot_flat = margin_slot.reshape(-1)
    weight_flat = margin_weight.reshape(margins, -1)
    received = lax.all_to_all(outgoing, ("space", "comp"), split_axis=1, concat_axis=1, tiled=True)
    picked = jnp.take(received, slot_flat, axis=1).reshape(received.shape[0], margins, -1)
    remapped = jnp.sum(picked * weight_flat[None], axis=1)
    forcing = remapped.reshape(ocean_state.shape)
    wetness = sea_mask.astype(jnp.float32)
    ocean_now = ocean_state
    for substep in range(SUB):
        padded = with_halo(ocean_now, ((("space", "comp"), 1),), 1)
        padded = jnp.pad(padded, ((0, 0), (0, 0), (1, 1)))
        ocean_now = advance(padded, wetness, forcing)
    weighted = (weight_flat[None] * ocean_now).reshape(fields_local, -1)
    outgoing_back = (
        jnp.zeros((fields_local, requests.shape[0]), jnp.float32).at[:, slot_flat].add(weighted)
    )
    arrived = lax.all_to_all(
        outgoing_back, ("space", "comp"), split_axis=1, concat_axis=1, tiled=True
    )
    returned = (
        jnp.zeros((fields_local, rows_atmos * cols_atmos), jnp.float32).at[:, requests].add(arrived)
    )
    return (atmos, ocean_now, returned.reshape(fields_local, rows_atmos, cols_atmos))


def solution(mesh):
    placed = (
        P(("parts", "lev"), None, ("space", "comp")),
        P(("parts", "lev"), ("space", "comp"), None),
        P(),
        P(),
        P(("space", "comp"), None, None),
        P(None, ("space", "comp"), None),
        P(None, ("space", "comp"), None),
        P(("space", "comp"), None),
    )
    return jax.shard_map(
        shards,
        mesh=mesh,
        in_specs=placed,
        out_specs=(
            P(("parts", "lev"), None, ("space", "comp")),
            P(("parts", "lev"), ("space", "comp"), None),
            P(("parts", "lev"), None, ("space", "comp")),
        ),
        check_vma=False,
    )
```

profile of v0, /device:TPU:0, one launch (start us, length us, event | category | flops | bytes accessed | tf_op | source)
XLA Modules:
  0.0 184.4 jit_solution(7847322945856986493)
XLA Ops:
  7.2 0.7 copy.104
  8.0 1.3 collective-permute-start.4
  9.2 5.5 %collective-permute-start.5 = (f32[8,1,512]{2,0,1:T(8,128)S(1)}, f32[8,1,512]{2,0,1:T(8,128)S(1)}, u32[]{:S(2)}, u32[]{:S(2)}) collective-permute-start(f32[8,1,512]{2,0,1:T(8,128)S(1)} %copy.104), channel_id=1, source_target_pairs={{0,2},{2,4},{4,6},{6,8},{8,10},{10,12},{12,14},{1,3},{3,5},{5,7},{... | collective-permute-start | bytes 49160 | tf_op jit(solution)/shard_map/ppermute | solution.py:24
  14.8 4.8 %collective-permute-start = (f32[4,16,1]{2,1,0:T(8,128)S(1)}, f32[4,16,1]{2,1,0:T(8,128)S(1)}, u32[]{:S(2)}, u32[]{:S(2)}) collective-permute-start(f32[4,16,1]{2,1,0:T(8,128)S(1)} %get-tuple-element.27), channel_id=1, source_target_pairs={{0,2},{2,4},{4,6},{6,8},{8,10},{10,12},{12,14},{1,3},{3,5},{5,7},{... | collective-permute-start | bytes 776 | tf_op jit(solution)/shard_map/ppermute | solution.py:24
  19.6 1.3 collective-permute-start.1
  21.0 1.9 %all-gather = f32[2,4,2048]{2,1,0:T(4,128)S(1)} all-gather(f32[1,4,2048]{2,1,0:T(4,128)S(1)} %reshape.164), channel_id=1, replica_groups=mesh['parts'=2,'space'=4,'comp'=2,'lev'=2] {'lev'}, dimensions={0}, use_global_device_ids=true | all-gather | bytes 98304 | tf_op jit(solution)/shard_map/all_gather | solution.py:41
  22.9 0.7 copy-done.6
  23.5 0.7 copy-done.7
  24.2 0.2 fusion
  24.4 1.0 collective-permute-done.1
  25.6 0.1 fusion.70
  25.8 3.5 %collective-permute-start.2 = (f32[4,16,1]{2,1,0:T(8,128)S(1)}, f32[4,16,1]{2,1,0:T(8,128)S(1)}, u32[]{:S(2)}, u32[]{:S(2)}) collective-permute-start(f32[4,16,1]{2,1,0:T(8,128)S(1)} %get-tuple-element.25), channel_id=1, source_target_pairs={{0,2},{2,4},{4,6},{6,8},{8,10},{10,12},{12,14},{1,3},{3,5},{5,7},{... | collective-permute-start | bytes 776 | tf_op jit(solution)/shard_map/ppermute | solution.py:24
  29.3 1.3 collective-permute-start.3
  30.6 1.9 %all-gather.1 = f32[2,4,2048]{2,1,0:T(4,128)S(1)} all-gather(f32[1,4,2048]{2,1,0:T(4,128)S(1)} %reshape.166), channel_id=1, replica_groups=mesh['parts'=2,'space'=4,'comp'=2,'lev'=2] {'lev'}, dimensions={0}, use_global_device_ids=true | all-gather | bytes 98304 | tf_op jit(solution)/shard_map/all_gather | solution.py:41
  32.5 0.2 fusion.1
  32.7 2.4 %collective-permute-done.3 = f32[4,16,1]{2,1,0:T(8,128)S(1)} collective-permute-done((f32[4,16,1]{2,1,0:T(8,128)S(1)}, f32[4,16,1]{2,1,0:T(8,128)S(1)}, u32[]{:S(2)}, u32[]{:S(2)}) %collective-permute-start.3) | collective-permute-done | bytes 288 | tf_op jit(solution)/shard_map/ppermute | solution.py:26
  35.2 0.1 bitcast_add_fusion
  35.4 1.0 fusion.9
  36.4 0.7 copy-done.3
  37.1 8.2 %reduce-scatter.2.cloned.1.call-done = f32[8,2048]{1,0:T(8,128)} async-done(((f32[16,2048]{1,0:T(8,128)}), f32[8,2048]{1,0:T(8,128)}) %reduce-scatter.2.cloned.1.call-update) | async-done | bytes 65552 | tf_op jit(solution)/shard_map/reduce_scatter | solution.py:73
  45.3 1.2 copy.105
  46.5 5.5 %gather_fusion = f32[2048,8]{1,0:T(8,128)S(1)} fusion(f32[8,2048]{0,1:T(8,128)S(1)} %copy.105, s32[2048]{0:T(1024)S(1)} %fusion.62), kind=kCustom, calls=%fused_computation.clone | custom fusion | bytes 139264 | tf_op jit(solution)/shard_map/jit(_take)/gather | solution.py:80
  51.9 0.3 broadcast_select_fusion.1
  52.3 0.9 copy.106
  53.2 5.8 %all-to-all-start = ((f32[8,8,256]{2,0,1:T(8,128)}), f32[8,8,256]{2,0,1:T(8,128)S(1)}, u32[]{:S(2)}, u32[]{:S(2)}) async-start(f32[8,8,256]{2,0,1:T(8,128)} %copy.106), calls=%async_computation.1 | async-start | bytes 131072 | tf_op jit(solution)/shard_map/all_to_all | solution.py:83
  59.0 0.7 copy-done.5
  59.7 0.7 copy-done.8
  60.4 5.4 %all-to-all-done = f32[8,8,256]{2,0,1:T(8,128)S(1)} async-done(((f32[8,8,256]{2,0,1:T(8,128)}), f32[8,8,256]{2,0,1:T(8,128)S(1)}, u32[]{:S(2)}, u32[]{:S(2)}) %all-to-all-start) | async-done | bytes 65568 | tf_op jit(solution)/shard_map/all_to_all | solution.py:83
  65.9 0.3 copy.107
  66.2 5.5 %gather_fusion.1 = f32[2048,8]{1,0:T(8,128)S(1)} fusion(f32[8,2048]{0,1:T(8,128)S(1)} %bitcast.60, s32[2048]{0:T(1024)S(1)} %fusion.63), kind=kCustom, calls=%fused_computation.1.clone | custom fusion | bytes 139264 | tf_op jit(solution)/shard_map/jit(_take)/gather | solution.py:84
  71.7 0.3 broadcast_select_fusion
  72.0 0.3 multiply_reduce_fusion
  72.5 0.6 copy-done.4
  73.2 1.3 collective-permute-start.6
  74.5 4.5 %collective-permute-start.7 = (f32[8,1,512]{2,0,1:T(8,128)S(1)}, f32[8,1,512]{2,0,1:T(8,128)S(1)}, u32[]{:S(2)}, u32[]{:S(2)}) collective-permute-start(f32[8,1,512]{2,0,1:T(8,128)S(1)} %fusion.61), channel_id=1, source_target_pairs={{0,2},{2,4},{4,6},{6,8},{8,10},{10,12},{12,14},{1,3},{3,5},{5,7},{... | collective-permute-start | bytes 49160 | tf_op jit(solution)/shard_map/ppermute | solution.py:24
  79.0 1.4 collective-permute-done.7
  80.6 1.3 collective-permute-start.8
  81.9 4.8 %collective-permute-start.9 = (f32[8,1,512]{2,0,1:T(8,128)S(1)}, f32[8,1,512]{2,0,1:T(8,128)S(1)}, u32[]{:S(2)}, u32[]{:S(2)}) collective-permute-start(f32[8,1,512]{2,0,1:T(8,128)S(1)} %fusion.56), channel_id=1, source_target_pairs={{0,2},{2,4},{4,6},{6,8},{8,10},{10,12},{12,14},{1,3},{3,5},{5,7},{... | collective-permute-start | bytes 49160 | tf_op jit(solution)/shard_map/ppermute | solution.py:24
  86.7 1.4 collective-permute-done.9
  88.3 1.3 collective-permute-start.10
  89.6 5.4 %collective-permute-start.11 = (f32[8,1,512]{2,0,1:T(8,128)S(1)}, f32[8,1,512]{2,0,1:T(8,128)S(1)}, u32[]{:S(2)}, u32[]{:S(2)}) collective-permute-start(f32[8,1,512]{2,0,1:T(8,128)S(1)} %fusion.51), channel_id=1, source_target_pairs={{0,2},{2,4},{4,6},{6,8},{8,10},{10,12},{12,14},{1,3},{3,5},{5,7},{... | collective-permute-start | bytes 49160 | tf_op jit(solution)/shard_map/ppermute | solution.py:24
  95.1 1.4 collective-permute-done.11
  96.7 1.3 collective-permute-start.12
  98.0 5.7 %collective-permute-start.13 = (f32[8,1,512]{2,0,1:T(8,128)S(1)}, f32[8,1,512]{2,0,1:T(8,128)S(1)}, u32[]{:S(2)}, u32[]{:S(2)}) collective-permute-start(f32[8,1,512]{2,0,1:T(8,128)S(1)} %fusion.46), channel_id=1, source_target_pairs={{0,2},{2,4},{4,6},{6,8},{8,10},{10,12},{12,14},{1,3},{3,5},{5,7},{... | collective-permute-start | bytes 49160 | tf_op jit(solution)/shard_map/ppermute | solution.py:24
  103.7 1.4 collective-permute-done.13
  105.3 1.3 collective-permute-start.14
  106.6 5.7 %collective-permute-start.15 = (f32[8,1,512]{2,0,1:T(8,128)S(1)}, f32[8,1,512]{2,0,1:T(8,128)S(1)}, u32[]{:S(2)}, u32[]{:S(2)}) collective-permute-start(f32[8,1,512]{2,0,1:T(8,128)S(1)} %fusion.41), channel_id=1, source_target_pairs={{0,2},{2,4},{4,6},{6,8},{8,10},{10,12},{12,14},{1,3},{3,5},{5,7},{... | collective-permute-start | bytes 49160 | tf_op jit(solution)/shard_map/ppermute | solution.py:24
  112.3 1.4 collective-permute-done.15
  113.9 1.3 collective-permute-start.16
  115.2 5.7 %collective-permute-start.17 = (f32[8,1,512]{2,0,1:T(8,128)S(1)}, f32[8,1,512]{2,0,1:T(8,128)S(1)}, u32[]{:S(2)}, u32[]{:S(2)}) collective-permute-start(f32[8,1,512]{2,0,1:T(8,128)S(1)} %fusion.36), channel_id=1, source_target_pairs={{0,2},{2,4},{4,6},{6,8},{8,10},{10,12},{12,14},{1,3},{3,5},{5,7},{... | collective-permute-start | bytes 49160 | tf_op jit(solution)/shard_map/ppermute | solution.py:24
  120.9 1.4 collective-permute-done.17
  122.5 1.3 collective-permute-start.18
  123.8 5.7 %collective-permute-start.19 = (f32[8,1,512]{2,0,1:T(8,128)S(1)}, f32[8,1,512]{2,0,1:T(8,128)S(1)}, u32[]{:S(2)}, u32[]{:S(2)}) collective-permute-start(f32[8,1,512]{2,0,1:T(8,128)S(1)} %fusion.31), channel_id=1, source_target_pairs={{0,2},{2,4},{4,6},{6,8},{8,10},{10,12},{12,14},{1,3},{3,5},{5,7},{... | collective-permute-start | bytes 49160 | tf_op jit(solution)/shard_map/ppermute | solution.py:24
  129.6 1.4 collective-permute-done.19
  131.1 0.1 copy.109
  131.3 0.3 bitcast_multiply_fusion
  131.6 13.1 %scatter_custom_fusion = f32[8,2048]{0,1:T(8,128)S(1)} fusion(s32[2048]{0:T(1024)S(1)} %bitcast.82, f32[8,2048]{0,1:T(8,128)S(1)} %bitcast_multiply_fusion, f32[]{:T(128)} %constant.18.clone.1), kind=kCustom, calls=%fused_computation.8 | custom fusion | flops 16384 | bytes 1114116 | tf_op jit(solution)/shard_map/scatter-add | solution.py:95
  144.7 0.9 copy.110
  145.6 10.1 %all-to-all-start.1 = ((f32[8,8,256]{2,0,1:T(8,128)}), f32[8,8,256]{2,0,1:T(8,128)S(1)}, u32[]{:S(2)}, u32[]{:S(2)}) async-start(f32[8,8,256]{2,0,1:T(8,128)} %copy.110), calls=%async_computation.2 | async-start | bytes 131072 | tf_op jit(solution)/shard_map/all_to_all | solution.py:97
  155.7 0.6 copy.112
  156.3 6.3 %all-to-all-done.1 = f32[8,8,256]{2,0,1:T(8,128)S(1)} async-done(((f32[8,8,256]{2,0,1:T(8,128)}), f32[8,8,256]{2,0,1:T(8,128)S(1)}, u32[]{:S(2)}, u32[]{:S(2)}) %all-to-all-start.1) | async-done | bytes 65568 | tf_op jit(solution)/shard_map/all_to_all | solution.py:97
  162.6 0.3 copy.111
  162.9 13.7 %scatter_custom_fusion.1 = f32[8,2048]{0,1:T(8,128)S(1)} fusion(s32[2048]{0:T(1024)S(1)} %bitcast.83, f32[2048,8]{1,0:T(8,128)S(1)} %copy.111, f32[]{:T(128)} %constant.18.clone.1), kind=kCustom, calls=%fused_computation.14 | custom fusion | flops 16384 | bytes 65540 | tf_op jit(solution)/shard_map/scatter-add | solution.py:101
  176.6 0.9 copy.113
  (61 shorter events, 2.0 us)
Async XLA Ops:
  7.2 28.2 %copy-start = (f32[16,8]{0,1:T(8,128)S(1)}, f32[16,8]{0,1:T(8,128)}, u32[]{:S(2)}) copy-start(f32[16,8]{0,1:T(8,128)} %param.13) | copy-start | bytes 1540
  7.2 7.5 %copy-start.1 = (f32[4,16,128]{2,1,0:T(8,128)S(1)}, f32[4,16,128]{2,1,0:T(8,128)}, u32[]{:S(2)}) copy-start(f32[4,16,128]{2,1,0:T(8,128)} %param.10) | copy-start | bytes 98308
  7.2 38.1 %reduce-scatter.2.cloned.1.call-start = ((), (), s32[]{:S(2)}) async-start(), calls=%async_computation.3 | async-start | bytes 196608 | tf_op jit(solution)/shard_map/reduce_scatter | solution.py:73
  8.0 52.4 %collective-permute-start.4 = (f32[8,1,512]{2,0,1:T(8,128)S(1)}, f32[8,1,512]{2,0,1:T(8,128)S(1)}, u32[]{:S(2)}, u32[]{:S(2)}) collective-permute-start(f32[8,1,512]{2,0,1:T(8,128)S(1)} %copy.104), channel_id=1, source_target_pairs={{2,0},{4,2},{6,4},{8,6},{10,8},{12,10},{14,12},{3,1},{5,3},{7,5},{... | collective-permute-start | bytes 49160 | tf_op jit(solution)/shard_map/ppermute | solution.py:26
  9.2 51.1 %collective-permute-start.5 = (f32[8,1,512]{2,0,1:T(8,128)S(1)}, f32[8,1,512]{2,0,1:T(8,128)S(1)}, u32[]{:S(2)}, u32[]{:S(2)}) collective-permute-start(f32[8,1,512]{2,0,1:T(8,128)S(1)} %copy.104), channel_id=1, source_target_pairs={{0,2},{2,4},{4,6},{6,8},{8,10},{10,12},{12,14},{1,3},{3,5},{5,7},{... | collective-permute-start | bytes 49160 | tf_op jit(solution)/shard_map/ppermute | solution.py:24
  14.8 9.6 %collective-permute-start = (f32[4,16,1]{2,1,0:T(8,128)S(1)}, f32[4,16,1]{2,1,0:T(8,128)S(1)}, u32[]{:S(2)}, u32[]{:S(2)}) collective-permute-start(f32[4,16,1]{2,1,0:T(8,128)S(1)} %get-tuple-element.27), channel_id=1, source_target_pairs={{0,2},{2,4},{4,6},{6,8},{8,10},{10,12},{12,14},{1,3},{3,5},{5,7},{... | collective-permute-start | bytes 776 | tf_op jit(solution)/shard_map/ppermute | solution.py:24
  19.6 5.8 %collective-permute-start.1 = (f32[4,16,1]{2,1,0:T(8,128)S(1)}, f32[4,16,1]{2,1,0:T(8,128)S(1)}, u32[]{:S(2)}, u32[]{:S(2)}) collective-permute-start(f32[4,16,1]{2,1,0:T(8,128)S(1)} %get-tuple-element.26), channel_id=1, source_target_pairs={{2,0},{4,2},{6,4},{8,6},{10,8},{12,10},{14,12},{3,1},{5,3},{7,5},{... | collective-permute-start | bytes 776 | tf_op jit(solution)/shard_map/ppermute | solution.py:26
  22.8 0.7 copy-start.6
  23.5 0.7 copy-start.7
  25.8 7.0 %collective-permute-start.2 = (f32[4,16,1]{2,1,0:T(8,128)S(1)}, f32[4,16,1]{2,1,0:T(8,128)S(1)}, u32[]{:S(2)}, u32[]{:S(2)}) collective-permute-start(f32[4,16,1]{2,1,0:T(8,128)S(1)} %get-tuple-element.25), channel_id=1, source_target_pairs={{0,2},{2,4},{4,6},{6,8},{8,10},{10,12},{12,14},{1,3},{3,5},{5,7},{... | collective-permute-start | bytes 776 | tf_op jit(solution)/shard_map/ppermute | solution.py:24
  29.3 5.8 %collective-permute-start.3 = (f32[4,16,1]{2,1,0:T(8,128)S(1)}, f32[4,16,1]{2,1,0:T(8,128)S(1)}, u32[]{:S(2)}, u32[]{:S(2)}) collective-permute-start(f32[4,16,1]{2,1,0:T(8,128)S(1)} %get-tuple-element.24), channel_id=1, source_target_pairs={{2,0},{4,2},{6,4},{8,6},{10,8},{12,10},{14,12},{3,1},{5,3},{7,5},{... | collective-permute-start | bytes 776 | tf_op jit(solution)/shard_map/ppermute | solution.py:26
  35.4 1.0 copy-start.2
  36.4 0.7 copy-start.3
  53.2 12.7 %all-to-all-start = ((f32[8,8,256]{2,0,1:T(8,128)}), f32[8,8,256]{2,0,1:T(8,128)S(1)}, u32[]{:S(2)}, u32[]{:S(2)}) async-start(f32[8,8,256]{2,0,1:T(8,128)} %copy.106), calls=%async_computation.1 | async-start | bytes 131072 | tf_op jit(solution)/shard_map/all_to_all | solution.py:83
  59.0 0.7 copy-start.5
  59.7 0.7 copy-start.8
  72.4 0.7 copy-start.4
  73.2 5.8 %collective-permute-start.6 = (f32[8,1,512]{2,0,1:T(8,128)S(1)}, f32[8,1,512]{2,0,1:T(8,128)S(1)}, u32[]{:S(2)}, u32[]{:S(2)}) collective-permute-start(f32[8,1,512]{2,0,1:T(8,128)S(1)} %fusion.61), channel_id=1, source_target_pairs={{2,0},{4,2},{6,4},{8,6},{10,8},{12,10},{14,12},{3,1},{5,3},{7,5},{... | collective-permute-start | bytes 49160 | tf_op jit(solution)/shard_map/ppermute | solution.py:26
  74.5 6.0 %collective-permute-start.7 = (f32[8,1,512]{2,0,1:T(8,128)S(1)}, f32[8,1,512]{2,0,1:T(8,128)S(1)}, u32[]{:S(2)}, u32[]{:S(2)}) collective-permute-start(f32[8,1,512]{2,0,1:T(8,128)S(1)} %fusion.61), channel_id=1, source_target_pairs={{0,2},{2,4},{4,6},{6,8},{8,10},{10,12},{12,14},{1,3},{3,5},{5,7},{... | collective-permute-start | bytes 49160 | tf_op jit(solution)/shard_map/ppermute | solution.py:24
  80.6 6.1 %collective-permute-start.8 = (f32[8,1,512]{2,0,1:T(8,128)S(1)}, f32[8,1,512]{2,0,1:T(8,128)S(1)}, u32[]{:S(2)}, u32[]{:S(2)}) collective-permute-start(f32[8,1,512]{2,0,1:T(8,128)S(1)} %fusion.56), channel_id=1, source_target_pairs={{2,0},{4,2},{6,4},{8,6},{10,8},{12,10},{14,12},{3,1},{5,3},{7,5},{... | collective-permute-start | bytes 49160 | tf_op jit(solution)/shard_map/ppermute | solution.py:26
  81.9 6.3 %collective-permute-start.9 = (f32[8,1,512]{2,0,1:T(8,128)S(1)}, f32[8,1,512]{2,0,1:T(8,128)S(1)}, u32[]{:S(2)}, u32[]{:S(2)}) collective-permute-start(f32[8,1,512]{2,0,1:T(8,128)S(1)} %fusion.56), channel_id=1, source_target_pairs={{0,2},{2,4},{4,6},{6,8},{8,10},{10,12},{12,14},{1,3},{3,5},{5,7},{... | collective-permute-start | bytes 49160 | tf_op jit(solution)/shard_map/ppermute | solution.py:24
  88.3 6.7 %collective-permute-start.10 = (f32[8,1,512]{2,0,1:T(8,128)S(1)}, f32[8,1,512]{2,0,1:T(8,128)S(1)}, u32[]{:S(2)}, u32[]{:S(2)}) collective-permute-start(f32[8,1,512]{2,0,1:T(8,128)S(1)} %fusion.51), channel_id=1, source_target_pairs={{2,0},{4,2},{6,4},{8,6},{10,8},{12,10},{14,12},{3,1},{5,3},{7,5},{... | collective-permute-start | bytes 49160 | tf_op jit(solution)/shard_map/ppermute | solution.py:26
  89.6 6.9 %collective-permute-start.11 = (f32[8,1,512]{2,0,1:T(8,128)S(1)}, f32[8,1,512]{2,0,1:T(8,128)S(1)}, u32[]{:S(2)}, u32[]{:S(2)}) collective-permute-start(f32[8,1,512]{2,0,1:T(8,128)S(1)} %fusion.51), channel_id=1, source_target_pairs={{0,2},{2,4},{4,6},{6,8},{8,10},{10,12},{12,14},{1,3},{3,5},{5,7},{... | collective-permute-start | bytes 49160 | tf_op jit(solution)/shard_map/ppermute | solution.py:24
  96.7 7.0 %collective-permute-start.12 = (f32[8,1,512]{2,0,1:T(8,128)S(1)}, f32[8,1,512]{2,0,1:T(8,128)S(1)}, u32[]{:S(2)}, u32[]{:S(2)}) collective-permute-start(f32[8,1,512]{2,0,1:T(8,128)S(1)} %fusion.46), channel_id=1, source_target_pairs={{2,0},{4,2},{6,4},{8,6},{10,8},{12,10},{14,12},{3,1},{5,3},{7,5},{... | collective-permute-start | bytes 49160 | tf_op jit(solution)/shard_map/ppermute | solution.py:26
  98.0 7.2 %collective-permute-start.13 = (f32[8,1,512]{2,0,1:T(8,128)S(1)}, f32[8,1,512]{2,0,1:T(8,128)S(1)}, u32[]{:S(2)}, u32[]{:S(2)}) collective-permute-start(f32[8,1,512]{2,0,1:T(8,128)S(1)} %fusion.46), channel_id=1, source_target_pairs={{0,2},{2,4},{4,6},{6,8},{8,10},{10,12},{12,14},{1,3},{3,5},{5,7},{... | collective-permute-start | bytes 49160 | tf_op jit(solution)/shard_map/ppermute | solution.py:24
  105.3 7.0 %collective-permute-start.14 = (f32[8,1,512]{2,0,1:T(8,128)S(1)}, f32[8,1,512]{2,0,1:T(8,128)S(1)}, u32[]{:S(2)}, u32[]{:S(2)}) collective-permute-start(f32[8,1,512]{2,0,1:T(8,128)S(1)} %fusion.41), channel_id=1, source_target_pairs={{2,0},{4,2},{6,4},{8,6},{10,8},{12,10},{14,12},{3,1},{5,3},{7,5},{... | collective-permute-start | bytes 49160 | tf_op jit(solution)/shard_map/ppermute | solution.py:26
  106.6 7.2 %collective-permute-start.15 = (f32[8,1,512]{2,0,1:T(8,128)S(1)}, f32[8,1,512]{2,0,1:T(8,128)S(1)}, u32[]{:S(2)}, u32[]{:S(2)}) collective-permute-start(f32[8,1,512]{2,0,1:T(8,128)S(1)} %fusion.41), channel_id=1, source_target_pairs={{0,2},{2,4},{4,6},{6,8},{8,10},{10,12},{12,14},{1,3},{3,5},{5,7},{... | collective-permute-start | bytes 49160 | tf_op jit(solution)/shard_map/ppermute | solution.py:24
  113.9 7.0 %collective-permute-start.16 = (f32[8,1,512]{2,0,1:T(8,128)S(1)}, f32[8,1,512]{2,0,1:T(8,128)S(1)}, u32[]{:S(2)}, u32[]{:S(2)}) collective-permute-start(f32[8,1,512]{2,0,1:T(8,128)S(1)} %fusion.36), channel_id=1, source_target_pairs={{2,0},{4,2},{6,4},{8,6},{10,8},{12,10},{14,12},{3,1},{5,3},{7,5},{... | collective-permute-start | bytes 49160 | tf_op jit(solution)/shard_map/ppermute | solution.py:26
  115.2 7.2 %collective-permute-start.17 = (f32[8,1,512]{2,0,1:T(8,128)S(1)}, f32[8,1,512]{2,0,1:T(8,128)S(1)}, u32[]{:S(2)}, u32[]{:S(2)}) collective-permute-start(f32[8,1,512]{2,0,1:T(8,128)S(1)} %fusion.36), channel_id=1, source_target_pairs={{0,2},{2,4},{4,6},{6,8},{8,10},{10,12},{12,14},{1,3},{3,5},{5,7},{... | collective-permute-start | bytes 49160 | tf_op jit(solution)/shard_map/ppermute | solution.py:24
  122.5 7.1 %collective-permute-start.18 = (f32[8,1,512]{2,0,1:T(8,128)S(1)}, f32[8,1,512]{2,0,1:T(8,128)S(1)}, u32[]{:S(2)}, u32[]{:S(2)}) collective-permute-start(f32[8,1,512]{2,0,1:T(8,128)S(1)} %fusion.31), channel_id=1, source_target_pairs={{2,0},{4,2},{6,4},{8,6},{10,8},{12,10},{14,12},{3,1},{5,3},{7,5},{... | collective-permute-start | bytes 49160 | tf_op jit(solution)/shard_map/ppermute | solution.py:26
  123.8 7.2 %collective-permute-start.19 = (f32[8,1,512]{2,0,1:T(8,128)S(1)}, f32[8,1,512]{2,0,1:T(8,128)S(1)}, u32[]{:S(2)}, u32[]{:S(2)}) collective-permute-start(f32[8,1,512]{2,0,1:T(8,128)S(1)} %fusion.31), channel_id=1, source_target_pairs={{0,2},{2,4},{4,6},{6,8},{8,10},{10,12},{12,14},{1,3},{3,5},{5,7},{... | collective-permute-start | bytes 49160 | tf_op jit(solution)/shard_map/ppermute | solution.py:24
  145.6 17.0 %all-to-all-start.1 = ((f32[8,8,256]{2,0,1:T(8,128)}), f32[8,8,256]{2,0,1:T(8,128)S(1)}, u32[]{:S(2)}, u32[]{:S(2)}) async-start(f32[8,8,256]{2,0,1:T(8,128)} %copy.110), calls=%async_computation.2 | async-start | bytes 131072 | tf_op jit(solution)/shard_map/all_to_all | solution.py:97
Sparse Core Ops, SparseCore 0:
  36.5 8.6 reduce-scatter.1
where the time goes:
time: 186 us; the launch traced here: 184 us
  starting transfers between devices  80.2 us (43%)
  waiting for transfers between devices  33.2 us (18%)
  other arithmetic  29.9 us (16%)
  local copies, waits for them, and re-layouts  21.4 us (12%)
  between operations  14.6 us (8%)
  blocking collectives  3.71 us (2%)
    ppermute x10, starting transfers between devices, with_halo(): lax.ppermute(tail, axis, [(i, (i + 1) % count) for i in range(ends)])  51.6 us
    scatter-add x1, other arithmetic, shards(): jnp.zeros((fields_local, rows_atmos * cols_atmos), jnp.float32)  13.7 us
    scatter-add x1, other arithmetic, shards(): jnp.zeros((fields_local, requests.shape[0]), jnp.float32).at[:, slot_flat]  13.1 us
    ppermute x10, starting transfers between devices, with_halo(): lax.ppermute(head, axis, [((i + 1) % count, i) for i in range(ends)])  12.8 us
    all_to_all x1, starting transfers between devices, shards(): lax.all_to_all(outgoing_back, ('space', 'comp'), split_axis=1, concat_axi...  10.1 us
    ppermute x10, waiting for transfers between devices, with_halo(): lax.ppermute(tail, axis, [(i, (i + 1) % count) for i in range(ends)])  9.87 us
    reduce_scatter x1, waiting for transfers between devices, shards(): lax.psum_scatter(jnp.dot(coupling_cols, flat_atmos, precision=lax.Precisi...  8.16 us
    unnamed x28, local copies, waits for them, and re-layouts  6.4 us
  transfers between devices with their start and end apart: 23, of which 12 were waited for; matrix products, arithmetic and copies ran while one was open for 6% of the time, Pallas kernels for 0%

commit v1 on v0

--- a/solution.py
+++ b/solution.py
@@ -1,6 +1,10 @@
+import functools
+
 import jax
 import jax.numpy as jnp
 from jax import lax
+from jax.experimental import pallas as pl
+from jax.experimental.pallas import tpu as pltpu
 from jax.sharding import PartitionSpec as P
 
 ASUB = 2
@@ -50,7 +54,7 @@
     return wetness[None] * (centre + OCEAN_MIX * (beside - 4.0 * centre) + FORCING * forcing)
 
 
-def shards(
+def shards_by_neighbours(
     atmos_state,
     ocean_state,
     vertical_mixing,
@@ -103,6 +107,258 @@
     return (atmos, ocean_now, returned.reshape(fields_local, rows_atmos, cols_atmos))
 
 
+LANES = 128
+HALF = 64
+ROWS = 8
+BLOCK = 32
+EDGE = 16
+AT_EDGES = 16
+AT_REQUESTS = 24
+
+
+def lane_of(shape=(ROWS, LANES)):
+    return lax.broadcasted_iota(jnp.int32, shape, len(shape) - 1)
+
+
+def pick_lanes(tile, lanes):
+    return jnp.take_along_axis(tile, lanes, axis=1, mode="promise_in_bounds")
+
+
+def rows_down(tile):
+    row = lax.broadcasted_iota(jnp.int32, tile.shape, 0)
+    return jnp.where(row == 0, 0.0, pltpu.roll(tile, 1, 0))
+
+
+def rows_up(tile):
+    row = lax.broadcasted_iota(jnp.int32, tile.shape, 0)
+    return jnp.where(row == tile.shape[0] - 1, 0.0, pltpu.roll(tile, tile.shape[0] - 1, 0))
+
+
+def place(peers_comp):
+    return lax.axis_index("space") * peers_comp + lax.axis_index("comp"), lax.axis_index("lev")
+
+
+def pack_kernel(peers, peers_comp, ocean_ref, slot_ref, weight_ref, mask_ref, atmos_ref, request_ref, send_ref):
+    strip, lev = place(peers_comp)
+    lane = lane_of()
+
+    def rings(cells):
+        tiles = [cells[:, LANES * t : LANES * (t + 1)] for t in range(peers // 2)]
+        beyond = jnp.zeros_like(tiles[0])
+        turned = [pltpu.roll(tile, HALF, 1) for tile in tiles]
+        place_in = lane[: cells.shape[0]]
+        out = []
+        for t in range(peers // 2):
+            before = tiles[t - 1] if t > 0 else beyond
+            after = turned[t + 1] if t + 1 < peers // 2 else beyond
+            out.append(jnp.where(place_in < 96, tiles[t], before))
+            out.append(jnp.where((place_in >= 64) & (place_in < 96), after, turned[t]))
+        return out
+
+    ocean = rings(ocean_ref[:, 0, :])
+    slot = rings(slot_ref[:, 0, :].astype(jnp.float32))
+    weight = rings(weight_ref[:, 0, :])
+    mask = rings(mask_ref[...].astype(jnp.float32))
+    to_right = jnp.zeros((ROWS, LANES), jnp.float32)
+    to_left = jnp.zeros((ROWS, LANES), jnp.float32)
+    for group in range(LANES // EDGE):
+        tile = atmos_ref[group // 2, ROWS * (group % 2) : ROWS * (group % 2 + 1), :]
+        here = lane // EDGE == group
+        to_right = jnp.where(here, pltpu.roll(tile, EDGE * (group + 1) % LANES, 1), to_right)
+        to_left = jnp.where(here, pltpu.roll(tile, EDGE * group, 1) if group else tile, to_left)
+    requests = request_ref[0].astype(jnp.float32)
+    requests = jnp.where(lev == 0, requests[:, :LANES], requests[:, LANES:])
+    for peer in range(peers):
+        edges = jnp.where(strip < peer, to_right, to_left)
+        same = (peer * 2 + lev) * BLOCK
+        other = (peer * 2 + 1 - lev) * BLOCK
+        send_ref[pl.ds(same, 8), :] = ocean[peer]
+        send_ref[pl.ds(other, 4), :] = slot[peer]
+        send_ref[pl.ds(other + 4, 4), :] = weight[peer]
+        send_ref[pl.ds(other + 8, 8), :] = jnp.broadcast_to(mask[peer], (ROWS, LANES))
+        for block in range(2):
+            send_ref[pl.ds((peer * 2 + block) * BLOCK + AT_EDGES, 8), :] = edges
+            send_ref[pl.ds((peer * 2 + block) * BLOCK + AT_REQUESTS, 8), :] = requests
+        send_ref[pl.ds(same + 8, 8), :] = jnp.zeros((ROWS, LANES), jnp.float32)
+
+
+def column_kernel(
+    peers,
+    peers_comp,
+    mixing_ref,
+    coupling_ref,
+    got_ref,
+    own_ref,
+    beside_ref,
+    request_ref,
+    atmos_ref,
+    returned_ref,
+    send_ref,
+    state_ref,
+    flux_ref,
+):
+    strip, lev = place(peers_comp)
+    lane = lane_of()
+    row = lax.broadcasted_iota(jnp.int32, (ROWS, LANES), 0)
+    levels = 8
+    half = levels // 2
+    left = jnp.maximum(strip - 1, 0)
+    right = jnp.minimum(strip + 1, peers - 1)
+
+    for level in range(half):
+        state_ref[lev * half + level, :, :LANES] = own_ref[level]
+        state_ref[(1 - lev) * half + level, :, :LANES] = beside_ref[level]
+    exists = jnp.where(lane < HALF, strip + 1, peers - strip) < peers
+    for block in range(2):
+        from_left = got_ref[pl.ds((left * 2 + block) * BLOCK + AT_EDGES, 8), :]
+        from_right = got_ref[pl.ds((right * 2 + block) * BLOCK + AT_EDGES, 8), :]
+        for group in range(LANES // EDGE):
+            west = pltpu.roll(from_left, LANES - EDGE * (group + 1), 1) if group < 7 else from_left
+            east = pltpu.roll(from_right, LANES - EDGE * group, 1) if group else from_right
+            tile = jnp.where(lane < EDGE, east, jnp.where(lane >= LANES - EDGE, west, 0.0))
+            state_ref[block * half + group // 2, ROWS * (group % 2) : ROWS * (group % 2 + 1), LANES:] = jnp.where(
+                exists, tile, 0.0
+            )
+    inside = jnp.concatenate([jnp.ones((16, LANES), jnp.float32), jnp.where(jnp.concatenate([exists] * 2, 0), 1.0, 0.0)], 1)
+    atmos = [state_ref[level] for level in range(levels)]
+    for substep in range(ASUB):
+        shaded = [jnp.tanh(cells) for cells in atmos]
+        later = []
+        for level in range(levels):
+            cells = atmos[level]
+            beside = pltpu.roll(cells, 1, 1) + pltpu.roll(cells, 2 * LANES - 1, 1) + rows_down(cells) + rows_up(cells)
+            column = sum(mixing_ref[level, other] * shaded[other] for other in range(levels))
+            cells = cells + DIFFUSE * (beside - 4.0 * cells) + TENDENCY * column
+            later.append(inside * cells)
+        atmos = later
+    for level in range(levels):
+        state_ref[level] = atmos[level]
+    for level in range(half):
+        atmos_ref[level] = state_ref[lev * half + level, :, :LANES]
+
+    fields = 8
+    for field in range(fields):
+        flux = sum(coupling_ref[level, lev * fields + field] * atmos[level] for level in range(levels))
+        for tile in range(2):
+            flux_ref[tile, pl.ds(field * BLOCK, 8), :] = jnp.zeros((ROWS, LANES), jnp.float32)
+            flux_ref[tile, pl.ds(field * BLOCK + 8, 16), :] = flux[:, LANES * tile : LANES * (tile + 1)]
+            flux_ref[tile, pl.ds(field * BLOCK + 24, 8), :] = jnp.zeros((ROWS, LANES), jnp.float32)
+
+    own_table = request_ref[0].astype(jnp.float32)
+    tables = [(own_table[:, :LANES], own_table[:, LANES:])]
+    for peer in (right, left):
+        tables.append(tuple(got_ref[pl.ds((peer * 2 + block) * BLOCK + AT_REQUESTS, 8), :] for block in range(2)))
+    first = ((2 * row - 1) * LANES + 2 * (lane & (HALF - 1))).astype(jnp.float32)
+
+    def table_row(which):
+        return got_ref[pl.ds((1 - lev) * BLOCK + which, ROWS, stride=2 * BLOCK), :]
+
+    both = lane >> 1
+    named = [[jnp.zeros((ROWS, LANES), jnp.float32) for _ in range(2)] for _ in range(4)]
+    for margin in range(4):
+        rank = table_row(margin).astype(jnp.int32) & (2 * LANES - 1)
+        late = rank >= LANES
+        rank = rank & (LANES - 1)
+        cells = [jnp.where(late, pick_lanes(high, rank), pick_lanes(low, rank)) for low, high in tables]
+        cell = jnp.where(lane < 64, cells[0], jnp.where(lane < 96, cells[1], cells[2])) - first
+        weight = table_row(4 + margin)
+        for tile in range(2):
+            beyond = pick_lanes(cell, both + HALF * tile) - (lane & 1).astype(jnp.float32)
+            share = pick_lanes(weight, both + HALF * tile)
+            for near in range(4):
+                named[near][tile] = named[near][tile] + jnp.where(beyond == float(near * LANES), share, 0.0)
+
+    wetness = table_row(8)
+    ocean = []
+    forcing = []
+    even = (2 * lane) & (LANES - 1)
+    for field in range(fields):
+        pairs = []
+        for tile in range(2):
+            total = sum(
+                named[near][tile]
+                * flux_ref[tile, pl.ds(field * BLOCK + 7 + near, ROWS, stride=2), :]
+                for near in range(4)
+            )
+            pairs.append(pick_lanes(total + pltpu.roll(total, LANES - 1, 1), even))
+        forcing.append(wetness * (FORCING * jnp.where(lane < HALF, pairs[0], pairs[1])))
+        ocean.append(got_ref[pl.ds(lev * BLOCK + field, ROWS, stride=2 * BLOCK), :])
+    for substep in range(SUB):
+        for field in range(fields):
+            cells = ocean[field]
+            beside = pltpu.roll(cells, 1, 1) + pltpu.roll(cells, LANES - 1, 1) + rows_down(cells) + rows_up(cells)
+            ocean[field] = wetness * (cells + OCEAN_MIX * (beside - 4.0 * cells)) + forcing[field]
+    for field in range(fields):
+        cells = ocean[field]
+        send_ref[pl.ds(field, ROWS, stride=fields), :] = jnp.where(strip % 2 == 0, cells, pltpu.roll(cells, HALF, 1))
+        spread = pick_lanes(cells, both)
+        upper = named[1][0] * spread + rows_down(named[3][0] * spread)
+        lower = named[2][0] * spread + rows_up(named[0][0] * spread)
+        returned_ref[pl.ds(field * 16, ROWS, stride=2), :] = upper
+        returned_ref[pl.ds(field * 16 + 1, ROWS, stride=2), :] = lower
+
+
+def rows_kernel(peers, got_ref, ocean_ref):
+    lane = lane_of()
+    for tile in range(peers // 2):
+        pair = [got_ref[ROWS * strip : ROWS * (strip + 1), :] for strip in (2 * tile, 2 * tile + 1)]
+        ocean_ref[:, 0, LANES * tile : LANES * (tile + 1)] = jnp.where(lane < HALF, pair[0], pair[1])
+
+
+def shards_by_columns(
+    atmos_state,
+    ocean_state,
+    vertical_mixing,
+    flux_coupling,
+    request_cells,
+    margin_slot,
+    margin_weight,
+    sea_mask,
+):
+    peers_comp = lax.axis_size("comp")
+    peers = lax.axis_size("space") * peers_comp
+    vmem = pl.BlockSpec(memory_space=pltpu.VMEM)
+    smem = pl.BlockSpec(memory_space=pltpu.SMEM)
+    values = functools.partial(jax.ShapeDtypeStruct, dtype=jnp.float32)
+    beside = lax.ppermute(atmos_state, "lev", [(0, 1), (1, 0)])
+    outgoing = pl.pallas_call(
+        functools.partial(pack_kernel, peers, peers_comp),
+        out_shape=values((2 * peers * BLOCK, LANES)),
+        in_specs=[vmem] * 6,
+        out_specs=vmem,
+    )(ocean_state, margin_slot, margin_weight, sea_mask, atmos_state, request_cells)
+    received = lax.all_to_all(outgoing, ("space", "comp", "lev"), split_axis=0, concat_axis=0, tiled=True)
+    atmos, returned, ocean_rows = pl.pallas_call(
+        functools.partial(column_kernel, peers, peers_comp),
+        out_shape=(values(atmos_state.shape), values((8 * 16, LANES)), values((peers * ROWS, LANES))),
+        in_specs=[smem] * 2 + [vmem] * 4,
+        out_specs=(vmem,) * 3,
+        scratch_shapes=[pltpu.VMEM((8, 16, 2 * LANES), jnp.float32), pltpu.VMEM((2, 8 * BLOCK, LANES), jnp.float32)],
+    )(vertical_mixing, flux_coupling.T, received, atmos_state, beside, request_cells)
+    gathered = lax.all_to_all(ocean_rows, ("space", "comp"), split_axis=0, concat_axis=0, tiled=True)
+    ocean = pl.pallas_call(
+        functools.partial(rows_kernel, peers),
+        out_shape=values(ocean_state.shape),
+        in_specs=[vmem],
+        out_specs=vmem,
+    )(gathered)
+    return (atmos, ocean, returned.reshape(8, 16, LANES))
+
+
+def shards(*arguments):
+    atmos_state, ocean_state, mixing, coupling, request_cells, margin_slot = arguments[:6]
+    peers = lax.axis_size("space") * lax.axis_size("comp")
+    by_columns = (
+        lax.axis_size("lev") == 2
+        and peers == ROWS
+        and atmos_state.shape == (4, 2 * ROWS, LANES)
+        and ocean_state.shape == (8, 1, HALF * peers)
+        and request_cells.shape == (1, peers, 2 * LANES)
+        and margin_slot.shape[0] == 4
+    )
+    return (shards_by_columns if by_columns else shards_by_neighbours)(*arguments)
+
+
 def solution(mesh):
     placed = (
         P(("parts", "lev"), None, ("space", "comp")),

time: 186 us -> 35.9 us (0.19)
  starting transfers between devices: 80.2 us -> 7.96 us
  other arithmetic: 29.9 us -> 0 us
  waiting for transfers between devices: 33.2 us -> 9.56 us
  local copies, waits for them, and re-layouts: 21.4 us -> 0.71 us
  between operations: 14.6 us -> 0.65 us
  blocking collectives: 3.71 us -> 10.6 us
  Pallas kernels: 0 us -> 5.93 us
    ppermute x20 -> x1, starting transfers between devices: 64.4 us -> 0.47 us  [shards_by_columns(): beside = lax.ppermute(atmos_state, 'lev', [(0, 1), (1, 0)])]
    scatter-add x2 -> x0, other arithmetic: 26.8 us -> none  [the longest x1 13.7 us: shards(): jnp.zeros((fields_local, rows_atmos * cols_atmos), jnp.float32)]
    ppermute x20 -> x1, waiting for transfers between devices: 13.3 us -> 0.86 us  [shards_by_columns(): beside = lax.ppermute(atmos_state, 'lev', [(0, 1), (1, 0)])]
    gather x2 -> x0, local copies, waits for them, and re-layouts: 10.9 us -> none  [the longest x1 5.47 us: shards(): jnp.take(received, slot_flat, axis=1)]
    all_to_all x0 -> x1, blocking collectives: none -> 10.6 us  [shards_by_columns(): lax.all_to_all(ocean_rows, ('space', 'comp'), split_axis=0, concat_axis=0...]
    all_to_all x2 -> x1, starting transfers between devices: 15.8 us -> 7.49 us  [shards_by_columns(): lax.all_to_all(outgoing, ('space', 'comp', 'lev'), split_axis=0, concat_a...]
    reduce_scatter x1 -> x0, waiting for transfers between devices: 8.16 us -> none  [shards(): lax.psum_scatter(jnp.dot(coupling_cols, flat_atmos, precision=lax.Precisi...]
    pallas_call x0 -> x3, Pallas kernels: none -> 5.93 us  [the longest x1 2.91 us: shards_by_columns(): pl.pallas_call(functools.partial(column_kernel, peers, peers_comp), out_s...]
  transfers between devices with their start and end apart: 23 -> 2, of which waited for: 12 -> 2; matrix products, arithmetic and copies ran while one was open for 6% -> 0% of each run, Pallas kernels for 0% -> 0%
where the time goes in v1:
time: 35.9 us; the launch traced here: 35.4 us
  blocking collectives  10.6 us (30%)
  waiting for transfers between devices  9.56 us (27%)
  starting transfers between devices  7.96 us (22%)
  Pallas kernels  5.93 us (17%)
  local copies, waits for them, and re-layouts  0.71 us (2%)
  between operations  0.65 us (2%)
    all_to_all x1, blocking collectives, shards_by_columns(): lax.all_to_all(ocean_rows, ('space', 'comp'), split_axis=0, concat_axis=0...  10.6 us
    all_to_all x1, waiting for transfers between devices, shards_by_columns(): lax.all_to_all(outgoing, ('space', 'comp', 'lev'), split_axis=0, concat_a...  8.7 us
    all_to_all x1, starting transfers between devices, shards_by_columns(): lax.all_to_all(outgoing, ('space', 'comp', 'lev'), split_axis=0, concat_a...  7.49 us
    pallas_call x1, Pallas kernels, shards_by_columns(): pl.pallas_call(functools.partial(column_kernel, peers, peers_comp), out_s...  2.91 us
    pallas_call x1, Pallas kernels, shards_by_columns(): pl.pallas_call(functools.partial(pack_kernel, peers, peers_comp), out_sha...  1.64 us
    pallas_call x1, Pallas kernels, shards_by_columns(): pl.pallas_call(functools.partial(rows_kernel, peers), out_shape=values(oc...  1.38 us
    ppermute x1, waiting for transfers between devices, shards_by_columns(): beside = lax.ppermute(atmos_state, 'lev', [(0, 1), (1, 0)])  0.86 us
  transfers between devices with their start and end apart: 2, of which 2 were waited for; matrix products, arithmetic and copies ran while one was open for 0% of the time, Pallas kernels for 0%

profile of v1, /device:TPU:0, one launch (start us, length us, event | category | flops | bytes accessed | tf_op | source)
XLA Modules:
  0.0 35.4 jit_solution(7349896285387395215)
XLA Ops:
  0.6 1.6 %shard_map.103 = f32[512,128]{1,0:T(8,128)} custom-call(f32[8,1,512]{2,1,0:T(1,128)} %ocean_ref.1, s32[4,1,512]{2,1,0:T(1,128)} %slot_ref.1, f32[4,1,512]{2,1,0:T(1,128)} %weight_ref.1, s32[1,512]{1,0:T(1,128)} %mask_ref.1, f32[4,16,128]{2,1,0:T(8,128)} %own_ref.1, s32[1,8,256]{2,1,0:T(8,128)} %request_ref.3), custom_call_target="tpu_custom_call" | custom-call | tf_op jit(solution)/shard_map/pallas_call | solution.py:324
  2.3 0.0 copy-start.1
  2.3 7.5 %all-to-all-start = ((f32[16,32,128]{2,1,0:T(8,128)}), f32[16,32,128]{2,1,0:T(8,128)S(1)}, u32[]{:S(2)}, u32[]{:S(2)}) async-start(f32[16,32,128]{2,1,0:T(8,128)} %bitcast.7), calls=%async_computation | async-start | bytes 524288 | tf_op jit(solution)/shard_map/all_to_all | solution.py:330
  9.8 0.0 copy-done.1
  9.8 0.5 %collective-permute-start = (f32[4,16,128]{2,1,0:T(8,128)S(1)}, f32[4,16,128]{2,1,0:T(8,128)S(1)}, u32[]{:S(2)}, u32[]{:S(2)}) collective-permute-start(f32[4,16,128]{2,1,0:T(8,128)S(1)} %copy-done.1), channel_id=1, source_target_pairs={{0,1},{1,0},{2,3},{3,2},{4,5},{5,4},{6,7},{7,6},{8,9},{9,8},{10,11... | collective-permute-start | bytes 98312 | tf_op jit(solution)/shard_map/ppermute | solution.py:323
  10.2 0.9 %collective-permute-done.beside_ref = f32[4,16,128]{2,1,0:T(8,128)S(1)} collective-permute-done((f32[4,16,128]{2,1,0:T(8,128)S(1)}, f32[4,16,128]{2,1,0:T(8,128)S(1)}, u32[]{:S(2)}, u32[]{:S(2)}) %collective-permute-start) | collective-permute-done | bytes 32800 | tf_op jit(solution)/shard_map/ppermute | solution.py:323
  11.1 0.0 copy-start.2
  11.1 8.7 %all-to-all-done = f32[16,32,128]{2,1,0:T(8,128)S(1)} async-done(((f32[16,32,128]{2,1,0:T(8,128)}), f32[16,32,128]{2,1,0:T(8,128)S(1)}, u32[]{:S(2)}, u32[]{:S(2)}) %all-to-all-start) | async-done | bytes 262176 | tf_op jit(solution)/shard_map/all_to_all | solution.py:330
  19.8 0.0 copy-start
  19.8 0.0 copy-done.2
  19.8 0.7 %copy-done = f32[16,32,128]{2,1,0:T(8,128)} copy-done((f32[16,32,128]{2,1,0:T(8,128)}, f32[16,32,128]{2,1,0:T(8,128)S(1)}, u32[]{:S(2)}) %copy-start) | copy-done | bytes 262168
  20.5 2.9 %shard_map.104 = (f32[4,16,128]{2,1,0:T(8,128)}, f32[128,128]{1,0:T(8,128)}, f32[64,128]{1,0:T(8,128)}) custom-call(f32[8,8]{1,0:T(8,128)} %mixing_ref.1, f32[8,16]{1,0:T(8,128)} %bitcast.10, f32[512,128]{1,0:T(8,128)} %bitcast.6, f32[4,16,128]{2,1,0:T(8,128)} %own_ref.1, f32[4,16,128]{2,1,0:T(8,128)} %copy-done.2, s32[1,8,256]{2,1,0:T(8,128)} %request_ref.3), custom_call_target="tpu_custom_call" | custom-call | tf_op jit(solution)/shard_map/pallas_call | solution.py:331
  23.4 10.6 %all_to_all.22 = f32[8,8,128]{2,1,0:T(8,128)} all-to-all(f32[8,8,128]{2,1,0:T(8,128)} %bitcast.9), channel_id=1, replica_groups=mesh['parts'=2,'space'=4,'comp'=2,'lev'=2] {'space','comp'}, dimensions={0} | all-to-all | bytes 65536 | tf_op jit(solution)/shard_map/all_to_all | solution.py:338
  34.0 1.4 %shard_map.105 = f32[8,1,512]{2,1,0:T(1,128)} custom-call(f32[64,128]{1,0:T(8,128)} %bitcast.8), custom_call_target="tpu_custom_call" | custom-call | tf_op jit(solution)/shard_map/pallas_call | solution.py:339
Async XLA Ops:
  2.3 7.5 %copy-start.1 = (f32[4,16,128]{2,1,0:T(8,128)S(1)}, f32[4,16,128]{2,1,0:T(8,128)}, u32[]{:S(2)}) copy-start(f32[4,16,128]{2,1,0:T(8,128)} %own_ref.1) | copy-start | bytes 98308
  2.3 17.5 %all-to-all-start = ((f32[16,32,128]{2,1,0:T(8,128)}), f32[16,32,128]{2,1,0:T(8,128)S(1)}, u32[]{:S(2)}, u32[]{:S(2)}) async-start(f32[16,32,128]{2,1,0:T(8,128)} %bitcast.7), calls=%async_computation | async-start | bytes 524288 | tf_op jit(solution)/shard_map/all_to_all | solution.py:330
  9.8 1.3 %collective-permute-start = (f32[4,16,128]{2,1,0:T(8,128)S(1)}, f32[4,16,128]{2,1,0:T(8,128)S(1)}, u32[]{:S(2)}, u32[]{:S(2)}) collective-permute-start(f32[4,16,128]{2,1,0:T(8,128)S(1)} %copy-done.1), channel_id=1, source_target_pairs={{0,1},{1,0},{2,3},{3,2},{4,5},{5,4},{6,7},{7,6},{8,9},{9,8},{10,11... | collective-permute-start | bytes 98312 | tf_op jit(solution)/shard_map/ppermute | solution.py:323
  11.1 8.7 %copy-start.2 = (f32[4,16,128]{2,1,0:T(8,128)}, f32[4,16,128]{2,1,0:T(8,128)S(1)}, u32[]{:S(2)}) copy-start(f32[4,16,128]{2,1,0:T(8,128)S(1)} %collective-permute-done.beside_ref) | copy-start | bytes 98308
  19.8 0.7 %copy-start = (f32[16,32,128]{2,1,0:T(8,128)}, f32[16,32,128]{2,1,0:T(8,128)S(1)}, u32[]{:S(2)}) copy-start(f32[16,32,128]{2,1,0:T(8,128)S(1)} %all-to-all-done) | copy-start | bytes 786436

commit v2 on v0

--- a/solution.py
+++ b/solution.py
@@ -1,6 +1,8 @@
 import jax
 import jax.numpy as jnp
 from jax import lax
+from jax.experimental import pallas as pl
+from jax.experimental.pallas import tpu as pltpu
 from jax.sharding import PartitionSpec as P
 
 ASUB = 2
@@ -50,7 +52,7 @@
     return wetness[None] * (centre + OCEAN_MIX * (beside - 4.0 * centre) + FORCING * forcing)
 
 
-def shards(
+def shards_by_neighbours(
     atmos_state,
     ocean_state,
     vertical_mixing,
@@ -103,6 +105,423 @@
     return (atmos, ocean_now, returned.reshape(fields_local, rows_atmos, cols_atmos))
 
 
+LANES = 128
+HALF = 64
+ROWS = 8
+LEVELS = 8
+FIELDS = 8
+MARGINS = 4
+TABLE = 24
+PACKED = 16
+TABLES = 4 * TABLE
+AT_LEFT = 16
+AT_REQUEST = 32
+AT_LEVELS = 48
+SHEET = 112
+AT_EDGE = 2 * TABLE
+AT_ASKED = AT_EDGE + 16
+LETTER = AT_ASKED + 16
+EDGE = 16
+WIDE = 32
+VMEM_LIMIT = 4 * 1024 * 1024
+
+
+def lane_of(shape=(ROWS, LANES)):
+    return lax.broadcasted_iota(jnp.int32, shape, 1)
+
+
+def row_of(shape=(ROWS, LANES)):
+    return lax.broadcasted_iota(jnp.int32, shape, 0)
+
+
+def pick_lanes(tile, lanes):
+    return jnp.take_along_axis(tile, lanes, axis=1, mode="promise_in_bounds")
+
+
+def turn(tile, by):
+    by = by % tile.shape[1]
+    return pltpu.roll(tile, by, 1) if by else tile
+
+
+def rows_down(tile):
+    return jnp.where(row_of(tile.shape) == 0, 0.0, pltpu.roll(tile, 1, 0))
+
+
+def rows_up(tile):
+    last = tile.shape[0] - 1
+    return jnp.where(row_of(tile.shape) == last, 0.0, pltpu.roll(tile, last, 0))
+
+
+def place():
+    return lax.axis_index("space"), lax.axis_index("comp"), lax.axis_index("lev")
+
+
+def tables_kernel(*refs):
+    arrays, (tables_ref, factors_ref, levels_ref, asked_ref), held, arrived = refs[:8], refs[8:12], refs[12:-1], refs[-1]
+    copies = [pltpu.make_async_copy(a, h, arrived.at[i]) for i, (a, h) in enumerate(zip(arrays, held))]
+    for copy in copies:
+        copy.start()
+    for copy in copies:
+        copy.wait()
+    ocean_ref, slot_ref, weight_ref, mask_ref, atmos_ref, request_ref, mixing_ref, coupling_ref = held
+    space, comp, lev = place()
+    lane, row = lane_of(), row_of()
+    near = (lane < EDGE // 2) | (lane >= LANES - EDGE // 2)
+
+    def halo(tiles, z):
+        beyond = jnp.zeros_like(tiles[0])
+        east = tiles[z + 1] if z + 1 < len(tiles) else beyond
+        west = tiles[z - 1] if z > 0 else beyond
+        wide = lane[: beyond.shape[0]]
+        return jnp.where(near[: beyond.shape[0]], jnp.where(wide < HALF, east, west), 0.0)
+
+    def packed(cells):
+        spread = [jnp.where(row == i, turn(cells, EDGE * i), 0.0) for i in range(ROWS)]
+        return jnp.sum(sum(spread), axis=0, keepdims=True)
+
+    def tiles_of(cells):
+        return [cells[:, LANES * z : LANES * (z + 1)] for z in range(4)]
+
+    ocean = tiles_of(ocean_ref[:, 0, :])
+    table = tiles_of(jnp.concatenate([slot_ref[:, 0, :].astype(jnp.float32), weight_ref[:, 0, :]], 0))
+    mask = tiles_of(mask_ref[...].astype(jnp.float32))
+    for z in range(4):
+        base = (z ^ space) * TABLE
+        tables_ref[pl.ds(base, 8), :] = ocean[z]
+        tables_ref[pl.ds(base + 8, 8), :] = table[z]
+        last = jnp.where(row == 0, packed(halo(ocean, z)), 0.0)
+        last = jnp.where(row == 1, packed(halo(table, z)), last)
+        last = jnp.where(row == 2, mask[z], last)
+        tables_ref[pl.ds(base + PACKED, 8), :] = jnp.where(row == 3, halo(mask, z), last)
+    for other in range(LEVELS):
+        factors_ref[LEVELS * other : LEVELS * (other + 1), :] = jnp.broadcast_to(
+            mixing_ref[:, other : other + 1], (ROWS, LANES)
+        )
+    for field in range(FIELDS):
+        mine = [coupling_ref[:, FIELDS * i + field : FIELDS * i + field + 1] for i in range(2)]
+        at = LEVELS * (LEVELS + field)
+        factors_ref[at : at + LEVELS, :] = jnp.broadcast_to(jnp.where(lev == 0, mine[0], mine[1]), (ROWS, LANES))
+    levels_ref[...] = atmos_ref[...]
+    requests = request_ref[0].astype(jnp.float32)
+    asked_ref[:ROWS, :] = requests[:, :LANES]
+    asked_ref[ROWS:, :] = requests[:, LANES:]
+
+
+def sheet_kernel(levels_ref, other_ref, asked_ref, sheet_ref):
+    space, comp, lev = place()
+    lane = lane_of()
+    for block, ref in ((lev, levels_ref), (1 - lev, other_ref)):
+        to_right = jnp.zeros((ROWS, LANES), jnp.float32)
+        to_left = jnp.zeros((ROWS, LANES), jnp.float32)
+        for group in range(LANES // EDGE):
+            tile = ref[group // 2, ROWS * (group % 2) : ROWS * (group % 2 + 1), :]
+            here = lane // EDGE == group
+            to_right = jnp.where(here, turn(tile, EDGE * (group + 1)), to_right)
+            to_left = jnp.where(here, turn(tile, EDGE * group), to_left)
+        sheet_ref[pl.ds(ROWS * block, 8), :] = to_right
+        sheet_ref[pl.ds(AT_LEFT + ROWS * block, 8), :] = to_left
+    sheet_ref[AT_REQUEST:AT_LEVELS, :] = asked_ref[...]
+    for level in range(LEVELS // 2):
+        at = AT_LEVELS + 2 * ROWS * level
+        sheet_ref[at : at + 2 * ROWS, :] = levels_ref[level]
+
+
+def letter_kernel(own_tables_ref, own_sheet_ref, beside_tables_ref, beside_sheet_ref, *letter_refs):
+    space, comp, lev = place()
+    sheets = (own_sheet_ref, beside_sheet_ref)
+    for k in (1, 2, 3):
+        letter_ref = letter_refs[k - 1]
+        letter_ref[:TABLE, :] = own_tables_ref[TABLE * k : TABLE * (k + 1), :]
+        letter_ref[TABLE : 2 * TABLE, :] = beside_tables_ref[TABLE * k : TABLE * (k + 1), :]
+        east = (space ^ k) > space
+        mine = comp == jnp.where(east, 1, 0)
+        edges = [jnp.where(east, ref[:AT_LEFT, :], ref[AT_LEFT:AT_REQUEST, :]) for ref in sheets]
+        asked = [ref[AT_REQUEST:AT_LEVELS, :] for ref in sheets]
+        letter_ref[AT_EDGE:AT_ASKED, :] = jnp.where(mine, edges[0], edges[1])
+        letter_ref[AT_ASKED:LETTER, :] = jnp.where(mine, asked[0], asked[1])
+
+
+def margins_kernel(
+    own_ref,
+    beside_ref,
+    own_sheet_ref,
+    beside_sheet_ref,
+    one_ref,
+    two_ref,
+    three_ref,
+    ocean_ref,
+    wet_ref,
+    named_ref,
+    rows_ref,
+):
+    space, comp, lev = place()
+    strip = 2 * space + comp
+    lane, row = lane_of(), row_of()
+    blocks = [(own_ref, 0), (beside_ref, 0)]
+    for ref in (one_ref, two_ref, three_ref):
+        blocks += [(ref, 0), (ref, TABLE)]
+    for m, (ref, start) in enumerate(blocks):
+        rows_ref[pl.ds((m ^ strip) * TABLE, TABLE), :] = ref[start : start + TABLE, :]
+
+    def table_row(which):
+        return rows_ref[pl.ds(which, ROWS, stride=TABLE), :]
+
+    ocean_halo = table_row(PACKED)
+    for field in range(FIELDS):
+        ocean_ref[field, :, :LANES] = table_row(field)
+        ocean_ref[field, :, LANES:] = turn(ocean_halo, -EDGE * field)
+    near = (lane < EDGE // 2) | (lane >= LANES - EDGE // 2)
+    wet_ref[:, :LANES] = table_row(PACKED + 2)
+    wet_ref[:, LANES:] = jnp.where(near, table_row(PACKED + 3), 0.0)
+
+    even = space % 2 == 0
+    own = [own_sheet_ref[AT_REQUEST + 8 * i : AT_REQUEST + 8 * (i + 1), :] for i in range(2)]
+    beside = [beside_sheet_ref[AT_REQUEST + 8 * i : AT_REQUEST + 8 * (i + 1), :] for i in range(2)]
+    one = [one_ref[AT_ASKED + 8 * i : AT_ASKED + 8 * (i + 1), :] for i in range(2)]
+    three = [three_ref[AT_ASKED + 8 * i : AT_ASKED + 8 * (i + 1), :] for i in range(2)]
+
+    def either(first_is, first, second):
+        return [jnp.where(first_is, a, b) for a, b in zip(first, second)]
+
+    tables = (
+        (either(comp == 0, own, beside), either(comp == 0, beside, own)),
+        (either(even, one, three), either(even, three, one)),
+    )
+    first = ((2 * row - 1) * LANES + 2 * (lane & (HALF - 1))).astype(jnp.float32)
+    parity = (lane & 1).astype(jnp.float32)
+    pairs = lane >> 1
+    spread = ((0, pairs), (0, pairs + HALF), (1, jnp.where(lane < HALF, pairs, pairs + HALF)))
+    table_halo = table_row(PACKED + 1)
+    named = [[jnp.zeros((ROWS, LANES), jnp.float32) for _ in range(3)] for _ in range(4)]
+    for margin in range(MARGINS):
+        slots = (table_row(8 + margin), turn(table_halo, -EDGE * margin))
+        weights = (table_row(8 + MARGINS + margin), turn(table_halo, -EDGE * (MARGINS + margin)))
+        cells = []
+        for slot, (low_strip, high_strip) in zip(slots, tables):
+            rank = slot.astype(jnp.int32) & (2 * LANES - 1)
+            late = rank >= LANES
+            rank = rank & (LANES - 1)
+            found = [jnp.where(late, pick_lanes(high, rank), pick_lanes(low, rank)) for low, high in (low_strip, high_strip)]
+            cells.append(jnp.where(lane < HALF, found[0], found[1]) - first)
+        for tile, (ring, lanes) in enumerate(spread):
+            beyond = pick_lanes(cells[ring], lanes) - parity
+            share = pick_lanes(weights[ring], lanes)
+            for step in range(4):
+                named[step][tile] = named[step][tile] + jnp.where(beyond == float(step * LANES), share, 0.0)
+    for step in range(4):
+        for tile in range(3):
+            named_ref[step, tile] = named[step][tile]
+
+
+def column_kernel(
+    factors_ref,
+    own_ref,
+    own_other_ref,
+    beside_ref,
+    beside_other_ref,
+    one_ref,
+    three_ref,
+    ocean_ref,
+    wet_ref,
+    named_ref,
+    atmos_ref,
+    final_ref,
+    first_ref,
+    second_ref,
+    third_ref,
+    fourth_ref,
+    state_ref,
+    flux_ref,
+    back_ref,
+):
+    space, comp, lev = place()
+    lane, row = lane_of(), row_of()
+    half = LEVELS // 2
+
+    mine = pl.ds(pl.multiple_of(comp * LANES, LANES), LANES)
+    theirs = pl.ds(pl.multiple_of((1 - comp) * LANES, LANES), LANES)
+    for level in range(half):
+        here, there = lev * half + level, (1 - lev) * half + level
+        state_ref[here, :, mine] = own_ref[level]
+        state_ref[there, :, mine] = own_other_ref[level]
+        at = 2 * ROWS * level
+        state_ref[here, :, theirs] = beside_ref[AT_LEVELS + at : AT_LEVELS + at + 2 * ROWS, :]
+        state_ref[there, :, theirs] = beside_other_ref[at : at + 2 * ROWS, :]
+    even = space % 2 == 0
+    exists = jnp.where(lane < HALF, space + 1, 4 - space) < 4
+    for block in range(2):
+        one, three = [ref[AT_EDGE + ROWS * block : AT_EDGE + ROWS * (block + 1), :] for ref in (one_ref, three_ref)]
+        east, west = jnp.where(even, one, three), jnp.where(even, three, one)
+        for group in range(LANES // EDGE):
+            tile = jnp.where(
+                lane < EDGE,
+                turn(east, -EDGE * group),
+                jnp.where(lane >= LANES - EDGE, turn(west, -EDGE * (group + 1)), 0.0),
+            )
+            state_ref[block * half + group // 2, ROWS * (group % 2) : ROWS * (group % 2 + 1), 2 * LANES :] = jnp.where(
+                exists, tile, 0.0
+            )
+    edge_inside = jnp.where(jnp.concatenate([exists] * 2, 0), 1.0, 0.0)
+    inside = jnp.concatenate([jnp.ones((2 * ROWS, 2 * LANES), jnp.float32), edge_inside], 1)
+
+    def factor(which):
+        return jnp.broadcast_to(jnp.concatenate([factors_ref[which : which + 1, :]] * 3, 1), (2 * ROWS, 3 * LANES))
+
+    atmos = [state_ref[level] for level in range(LEVELS)]
+    for substep in range(ASUB):
+        shaded = [jnp.tanh(cells) for cells in atmos]
+        later = []
+        for level in range(LEVELS):
+            cells = atmos[level]
+            beside = turn(cells, 1) + turn(cells, -1) + rows_down(cells) + rows_up(cells)
+            column = sum(factor(LEVELS * other + level) * shaded[other] for other in range(LEVELS))
+            cells = cells + DIFFUSE * (beside - 4.0 * cells) + TENDENCY * column
+            later.append(inside * cells)
+        atmos = later
+    for level in range(LEVELS):
+        state_ref[level] = atmos[level]
+    for level in range(half):
+        atmos_ref[level] = state_ref[lev * half + level, :, mine]
+
+    for field in range(FIELDS):
+        flux = sum(factor(LEVELS * (LEVELS + field) + level) * atmos[level] for level in range(LEVELS))
+        for tile in range(3):
+            flux_ref[tile, WIDE * field : WIDE * field + 8, :] = jnp.zeros((ROWS, LANES), jnp.float32)
+            flux_ref[tile, WIDE * field + 8 : WIDE * field + 24, :] = flux[:, LANES * tile : LANES * (tile + 1)]
+            flux_ref[tile, WIDE * field + 24 : WIDE * field + 32, :] = jnp.zeros((ROWS, LANES), jnp.float32)
+
+    wetness = wet_ref[...]
+    pairs = (2 * lane) & (LANES - 1)
+    ocean = []
+    forcing = []
+    for field in range(FIELDS):
+        sums = []
+        for tile in range(3):
+            total = sum(
+                named_ref[step, tile] * flux_ref[tile, pl.ds(WIDE * field + 7 + step, ROWS, stride=2), :] for step in range(4)
+            )
+            sums.append(pick_lanes(total + turn(total, -1), pairs))
+        remapped = jnp.concatenate([jnp.where(lane < HALF, sums[0], sums[1]), sums[2]], 1)
+        forcing.append(wetness * (FORCING * remapped))
+        ocean.append(ocean_ref[field])
+    for substep in range(SUB):
+        for field in range(FIELDS):
+            cells = ocean[field]
+            beside = turn(cells, 1) + turn(cells, -1) + rows_down(cells) + rows_up(cells)
+            ocean[field] = wetness * (cells + OCEAN_MIX * (beside - 4.0 * cells)) + forcing[field]
+    for field in range(FIELDS):
+        cells = ocean[field][:, :LANES]
+        final_ref[field] = cells
+        back_ref[pl.ds(field, ROWS, stride=FIELDS), :] = cells
+    for k, ref in enumerate((first_ref, second_ref, third_ref, fourth_ref)):
+        ref[...] = back_ref[pl.ds((2 * (space ^ k) + comp) * FIELDS, FIELDS), :]
+
+
+def returned_kernel(atmos_ref, final_ref, named_ref, atmos_next_ref, returned_ref):
+    space, comp, lev = place()
+    lane = lane_of()
+    atmos_next_ref[...] = atmos_ref[...]
+    named = [jnp.where(comp == 0, named_ref[step, 0], named_ref[step, 1]) for step in range(4)]
+    pairs = (lane >> 1) + HALF * comp
+    for field in range(FIELDS):
+        spread = pick_lanes(final_ref[field], pairs)
+        upper = named[1] * spread + rows_down(named[3] * spread)
+        lower = named[2] * spread + rows_up(named[0] * spread)
+        returned_ref[pl.ds(2 * ROWS * field, ROWS, stride=2), :] = upper
+        returned_ref[pl.ds(2 * ROWS * field + 1, ROWS, stride=2), :] = lower
+
+
+def rows_kernel(own_ref, one_ref, two_ref, three_ref, ocean_ref):
+    space, comp, lev = place()
+    for k, ref in enumerate((own_ref, one_ref, two_ref, three_ref)):
+        ocean_ref[:, 0, pl.ds(pl.multiple_of((space ^ k) * LANES, LANES), LANES)] = ref[...]
+
+
+def over(axis, k, array):
+    return lax.ppermute(array, axis, [(i, i ^ k) for i in range(lax.axis_size(axis))])
+
+
+def local(kernel, out_shape, spaces, scratch=()):
+    single = not isinstance(out_shape, tuple)
+    vmem = pl.BlockSpec(memory_space=pltpu.VMEM)
+    return pl.pallas_call(
+        kernel,
+        out_shape=out_shape,
+        in_specs=[pl.BlockSpec(memory_space=space) for space in spaces],
+        out_specs=vmem if single else (vmem,) * len(out_shape),
+        scratch_shapes=list(scratch),
+        compiler_params=pltpu.CompilerParams(vmem_limit_bytes=VMEM_LIMIT),
+    )
+
+
+def shards_by_columns(
+    atmos_state,
+    ocean_state,
+    vertical_mixing,
+    flux_coupling,
+    request_cells,
+    margin_slot,
+    margin_weight,
+    sea_mask,
+):
+    def values(*shape):
+        return jax.ShapeDtypeStruct(shape, jnp.float32)
+
+    arrays = (ocean_state, margin_slot, margin_weight, sea_mask, atmos_state, request_cells)
+    arrays += (vertical_mixing, flux_coupling.T)
+    own_other = over("lev", 1, atmos_state)
+    tables, factors, levels, asked = local(
+        tables_kernel,
+        (values(TABLES, LANES), values(2 * LEVELS * LEVELS, LANES), values(*atmos_state.shape), values(2 * ROWS, LANES)),
+        [pltpu.HBM] * 8,
+        [pltpu.VMEM(a.shape, a.dtype) for a in arrays] + [pltpu.SemaphoreType.DMA((8,))],
+    )(*(pltpu.with_memory_space_constraint(a, pltpu.HBM) for a in arrays))
+    tables_beside = over("comp", 1, tables)
+    sheet = local(sheet_kernel, values(SHEET, LANES), [pltpu.VMEM] * 3)(levels, own_other, asked)
+    sheet_beside = over("comp", 1, sheet)
+    letters = local(letter_kernel, (values(LETTER, LANES),) * 3, [pltpu.VMEM] * 4)(
+        tables, sheet, tables_beside, sheet_beside
+    )
+    one, two, three = (over("space", k, letter) for k, letter in zip((1, 2, 3), letters))
+    beside_other = over("lev", 1, sheet_beside[AT_LEVELS:])
+    ocean, wet, named = local(
+        margins_kernel,
+        (values(FIELDS, ROWS, 2 * LANES), values(ROWS, 2 * LANES), values(4, 3, ROWS, LANES)),
+        [pltpu.VMEM] * 7,
+        [pltpu.VMEM((ROWS * TABLE, LANES), jnp.float32)],
+    )(tables, tables_beside, sheet, sheet_beside, one, two, three)
+    atmos, final, *back = local(
+        column_kernel,
+        (values(*atmos_state.shape), values(FIELDS, ROWS, LANES)) + (values(FIELDS, LANES),) * 4,
+        [pltpu.VMEM] * 10,
+        [
+            pltpu.VMEM((LEVELS, 2 * ROWS, 3 * LANES), jnp.float32),
+            pltpu.VMEM((3, FIELDS * WIDE, LANES), jnp.float32),
+            pltpu.VMEM((ROWS * FIELDS, LANES), jnp.float32),
+        ],
+    )(factors, levels, own_other, sheet_beside, beside_other, one, three, ocean, wet, named)
+    pieces = [over("space", k, piece) for k, piece in zip((1, 2, 3), back[1:])]
+    atmos_next, returned = local(
+        returned_kernel,
+        (values(*atmos_state.shape), values(FIELDS * 2 * ROWS, LANES)),
+        [pltpu.VMEM] * 3,
+    )(atmos, final, named)
+    ocean_next = local(rows_kernel, values(*ocean_state.shape), [pltpu.VMEM] * 4)(back[0], *pieces)
+    return (atmos_next, ocean_next, returned.reshape(FIELDS, 2 * ROWS, LANES))
+
+
+def shards(*arguments):
+    atmos_state, ocean_state, mixing, coupling, request_cells, margin_slot = arguments[:6]
+    by_columns = (
+        (lax.axis_size("space"), lax.axis_size("comp"), lax.axis_size("lev")) == (4, 2, 2)
+        and atmos_state.shape == (LEVELS // 2, 2 * ROWS, LANES)
+        and ocean_state.shape == (FIELDS, 1, 4 * LANES)
+        and request_cells.shape == (1, ROWS, 2 * LANES)
+        and margin_slot.shape[0] == MARGINS
+    )
+    return (shards_by_columns if by_columns else shards_by_neighbours)(*arguments)
+
+
 def solution(mesh):
     placed = (
         P(("parts", "lev"), None, ("space", "comp")),

time: 186 us -> 28.8 us (0.15)
  starting transfers between devices: 80.2 us -> 12.2 us
  other arithmetic: 29.9 us -> 0 us
  waiting for transfers between devices: 33.2 us -> 11.4 us
  local copies, waits for them, and re-layouts: 21.4 us -> 0.01 us
  between operations: 14.6 us -> 0.69 us
  Pallas kernels: 0 us -> 4.26 us
  blocking collectives: 3.71 us -> 0 us
    ppermute x20 -> x10, starting transfers between devices: 64.4 us -> 12.2 us  [over(): lax.ppermute(array, axis, [(i, i ^ k) for i in range(lax.axis_size(axis))])]
    scatter-add x2 -> x0, other arithmetic: 26.8 us -> none  [the longest x1 13.7 us: shards(): jnp.zeros((fields_local, rows_atmos * cols_atmos), jnp.float32)]
    all_to_all x2 -> x0, starting transfers between devices: 15.8 us -> none  [the longest x1 10.1 us: shards(): lax.all_to_all(outgoing_back, ('space', 'comp'), split_axis=1, concat_axi...]
    all_to_all x2 -> x0, waiting for transfers between devices: 11.7 us -> none  [the longest x1 6.27 us: shards(): lax.all_to_all(outgoing_back, ('space', 'comp'), split_axis=1, concat_axi...]
    gather x2 -> x0, local copies, waits for them, and re-layouts: 10.9 us -> none  [the longest x1 5.47 us: shards(): jnp.take(received, slot_flat, axis=1)]
    reduce_scatter x1 -> x0, waiting for transfers between devices: 8.16 us -> none  [shards(): lax.psum_scatter(jnp.dot(coupling_cols, flat_atmos, precision=lax.Precisi...]
    unnamed x28 -> x0, local copies, waits for them, and re-layouts: 6.4 us -> none
    pallas_call x0 -> x7, Pallas kernels: none -> 4.26 us  [the longest x1 1.44 us: shards_by_columns(): local(column_kernel, (values(*atmos_state.shape), values(FIELDS, ROWS, LA...]
  transfers between devices with their start and end apart: 23 -> 10, of which waited for: 12 -> 4; matrix products, arithmetic and copies ran while one was open for 6% -> 0% of each run, Pallas kernels for 0% -> 7%
where the time goes in v2:
time: 28.8 us; the launch traced here: 28.5 us
  starting transfers between devices  12.2 us (42%)
  waiting for transfers between devices  11.4 us (40%)
  Pallas kernels  4.26 us (15%)
  between operations  0.69 us (2%)
    ppermute x10, starting transfers between devices, over(): lax.ppermute(array, axis, [(i, i ^ k) for i in range(lax.axis_size(axis))])  12.2 us
    ppermute x10, waiting for transfers between devices, over(): lax.ppermute(array, axis, [(i, i ^ k) for i in range(lax.axis_size(axis))])  11.4 us
    pallas_call x1, Pallas kernels, shards_by_columns(): local(column_kernel, (values(*atmos_state.shape), values(FIELDS, ROWS, LA...  1.44 us
    pallas_call x1, Pallas kernels, shards_by_columns(): local(tables_kernel, (values(TABLES, LANES), values(2 * LEVELS * LEVELS,...  1.08 us
    pallas_call x1, Pallas kernels, shards_by_columns(): local(returned_kernel, (values(*atmos_state.shape), values(FIELDS * 2 * R...  0.72 us
    pallas_call x1, Pallas kernels, shards_by_columns(): local(rows_kernel, values(*ocean_state.shape), [pltpu.VMEM] * 4)  0.62 us
  transfers between devices with their start and end apart: 10, of which 4 were waited for; matrix products, arithmetic and copies ran while one was open for 0% of the time, Pallas kernels for 7%

profile of v2, /device:TPU:0, one launch (start us, length us, event | category | flops | bytes accessed | tf_op | source)
XLA Modules:
  0.0 28.5 jit_solution(11264558677763039253)
XLA Ops:
  0.6 0.5 %collective-permute-start = (f32[4,16,128]{2,1,0:T(8,128)}, f32[4,16,128]{2,1,0:T(8,128)S(1)}, u32[]{:S(2)}, u32[]{:S(2)}) collective-permute-start(f32[4,16,128]{2,1,0:T(8,128)} %refs_4_.1), channel_id=1, source_target_pairs={{0,1},{1,0},{2,3},{3,2},{4,5},{5,4},{6,7},{7,6},{8,9},{9,8},{10,11... | collective-permute-start | bytes 98312 | tf_op jit(solution)/shard_map/ppermute | solution.py:441
  1.2 1.1 %shard_map.103 = (f32[96,128]{1,0:T(8,128)S(1)}, f32[128,128]{1,0:T(8,128)S(1)}, f32[4,16,128]{2,1,0:T(8,128)S(1)}, f32[16,128]{1,0:T(8,128)S(1)}) custom-call(f32[8,1,512]{2,1,0:T(1,128)} %refs_0_.1, s32[4,1,512]{2,1,0:T(1,128)} %refs_1_.1, f32[4,1,512]{2,1,0:T(1,128)} %refs_2_.1, s32[1,512]{1,0:T(1,128)} %refs_3_.1, f32[4,16,128]{2,1,0:T(8,128)} %refs_4_.1, ...), custom_call_target="tpu_custom_call" | custom-call | tf_op jit(solution)/shard_map/pallas_call | solution.py:473
  2.2 0.0 collective-permute-done.other_ref.own_other_ref
  2.3 0.1 shard_map.104.own_sheet_ref
  2.4 2.9 %collective-permute-start.1 = (f32[112,128]{1,0:T(8,128)S(1)}, f32[112,128]{1,0:T(8,128)S(1)}, u32[]{:S(2)}, u32[]{:S(2)}) collective-permute-start(f32[112,128]{1,0:T(8,128)S(1)} %shard_map.104.own_sheet_ref), channel_id=1, source_target_pairs={{0,2},{2,0},{1,3},{3,1},{4,6},{6,4},{5,7},{7,5},{8,10},{10,8},{9,1... | collective-permute-start | bytes 172040 | tf_op jit(solution)/shard_map/ppermute | solution.py:441
  5.2 0.1 collective-permute-start.3
  5.3 4.0 %collective-permute-done.3.beside_tables_ref.beside_ref = f32[96,128]{1,0:T(8,128)S(1)} collective-permute-done((f32[96,128]{1,0:T(8,128)S(1)}, f32[96,128]{1,0:T(8,128)S(1)}, u32[]{:S(2)}, u32[]{:S(2)}) %collective-permute-start.3) | collective-permute-done | bytes 49184 | tf_op jit(solution)/shard_map/ppermute | solution.py:441
  9.3 0.0 collective-permute-done.1.beside_sheet_ref.beside_ref
  9.3 1.6 %collective-permute-start.4 = (f32[80,128]{1,0:T(8,128)S(1)}, f32[80,128]{1,0:T(8,128)S(1)}, u32[]{:S(2)}, u32[]{:S(2)}) collective-permute-start(f32[80,128]{1,0:T(8,128)S(1)} %get-tuple-element.25), channel_id=1, source_target_pairs={{0,4},{4,0},{8,12},{12,8},{1,5},{5,1},{9,13},{13,9},{2,6},{6,2},{1... | collective-permute-start | bytes 122888 | tf_op jit(solution)/shard_map/ppermute | solution.py:441
  11.0 2.5 %collective-permute-start.5 = (f32[80,128]{1,0:T(8,128)S(1)}, f32[80,128]{1,0:T(8,128)S(1)}, u32[]{:S(2)}, u32[]{:S(2)}) collective-permute-start(f32[80,128]{1,0:T(8,128)S(1)} %get-tuple-element.26), channel_id=1, source_target_pairs={{0,12},{4,8},{8,4},{12,0},{1,13},{5,9},{9,5},{13,1},{2,14},{6,10},... | collective-permute-start | bytes 122888 | tf_op jit(solution)/shard_map/ppermute | solution.py:441
  13.5 0.1 collective-permute-start.6
  13.6 0.0 collective-permute-start.2
  13.6 0.0 collective-permute-done.4.one_ref
  13.6 3.2 %collective-permute-done.5.three_ref = f32[80,128]{1,0:T(8,128)S(1)} collective-permute-done((f32[80,128]{1,0:T(8,128)S(1)}, f32[80,128]{1,0:T(8,128)S(1)}, u32[]{:S(2)}, u32[]{:S(2)}) %collective-permute-start.5) | collective-permute-done | bytes 40992 | tf_op jit(solution)/shard_map/ppermute | solution.py:441
  16.8 2.0 %collective-permute-done.6.two_ref = f32[80,128]{1,0:T(8,128)S(1)} collective-permute-done((f32[80,128]{1,0:T(8,128)S(1)}, f32[80,128]{1,0:T(8,128)S(1)}, u32[]{:S(2)}, u32[]{:S(2)}) %collective-permute-start.6) | collective-permute-done | bytes 40992 | tf_op jit(solution)/shard_map/ppermute | solution.py:441
  18.8 0.3 shard_map.106
  19.1 0.0 collective-permute-done.2.beside_other_ref
  19.1 1.4 %shard_map.107 = (f32[4,16,128]{2,1,0:T(8,128)S(1)}, f32[8,8,128]{2,1,0:T(8,128)S(1)}, f32[8,128]{1,0:T(8,128)S(1)}, f32[8,128]{1,0:T(8,128)S(1)}, f32[8,128]{1,0:T(8,128)S(1)}, /*index=5*/f32[8,128]{1,0:T(8,128)S(1)}) custom-call(f32[128,128]{1,0:T(8,128)S(1)} %get-tuple-element.21.factors_ref, f32[4,16,128]{2,1,0:T(8,128)S(1)} %get-tuple-element.22.levels_ref.own_ref, ...), custom_call_target="tpu_custom_call" | custom-call | tf_op jit(solution)/shard_map/pallas_call | solution.py:493
  20.5 0.4 %collective-permute-start.7 = (f32[8,128]{1,0:T(8,128)S(1)}, f32[8,128]{1,0:T(8,128)S(1)}, u32[]{:S(2)}, u32[]{:S(2)}) collective-permute-start(f32[8,128]{1,0:T(8,128)S(1)} %get-tuple-element.35), channel_id=1, source_target_pairs={{0,4},{4,0},{8,12},{12,8},{1,5},{5,1},{9,13},{13,9},{2,6},{6,2},{1... | collective-permute-start | bytes 12296 | tf_op jit(solution)/shard_map/ppermute | solution.py:441
  20.9 1.6 %collective-permute-start.8 = (f32[8,128]{1,0:T(8,128)S(1)}, f32[8,128]{1,0:T(8,128)S(1)}, u32[]{:S(2)}, u32[]{:S(2)}) collective-permute-start(f32[8,128]{1,0:T(8,128)S(1)} %get-tuple-element.36), channel_id=1, source_target_pairs={{0,8},{4,12},{8,0},{12,4},{1,9},{5,13},{9,1},{13,5},{2,10},{6,14},... | collective-permute-start | bytes 12296 | tf_op jit(solution)/shard_map/ppermute | solution.py:441
  22.5 2.5 %collective-permute-start.9 = (f32[8,128]{1,0:T(8,128)S(1)}, f32[8,128]{1,0:T(8,128)S(1)}, u32[]{:S(2)}, u32[]{:S(2)}) collective-permute-start(f32[8,128]{1,0:T(8,128)S(1)} %get-tuple-element.37), channel_id=1, source_target_pairs={{0,12},{4,8},{8,4},{12,0},{1,13},{5,9},{9,5},{13,1},{2,14},{6,10},... | collective-permute-start | bytes 12296 | tf_op jit(solution)/shard_map/ppermute | solution.py:441
  25.0 0.7 %shard_map.108 = (f32[4,16,128]{2,1,0:T(8,128)}, f32[128,128]{1,0:T(8,128)}) custom-call(f32[4,16,128]{2,1,0:T(8,128)S(1)} %get-tuple-element.31.atmos_ref, f32[8,8,128]{2,1,0:T(8,128)S(1)} %get-tuple-element.32.final_ref, f32[4,3,8,128]{3,2,1,0:T(8,128)S(1)} %get-tuple-element.30.named_ref), custom_call_target="tpu_custom_call" | custom-call | tf_op jit(solution)/shard_map/pallas_call | solution.py:504
  25.7 0.0 collective-permute-done.7.one_ref
  25.7 0.0 collective-permute-done.8.two_ref
  25.7 2.2 %collective-permute-done.9.three_ref = f32[8,128]{1,0:T(8,128)S(1)} collective-permute-done((f32[8,128]{1,0:T(8,128)S(1)}, f32[8,128]{1,0:T(8,128)S(1)}, u32[]{:S(2)}, u32[]{:S(2)}) %collective-permute-start.9) | collective-permute-done | bytes 4128 | tf_op jit(solution)/shard_map/ppermute | solution.py:441
  27.9 0.6 %shard_map.109 = f32[8,1,512]{2,1,0:T(1,128)} custom-call(f32[8,128]{1,0:T(8,128)S(1)} %get-tuple-element.34.own_ref, f32[8,128]{1,0:T(8,128)S(1)} %collective-permute-done.7.one_ref, f32[8,128]{1,0:T(8,128)S(1)} %collective-permute-done.8.two_ref, f32[8,128]{1,0:T(8,128)S(1)} %collective-permute-done.9.three_ref), custom_call_target="tpu_custom_call" | custom-call | tf_op jit(solution)/shard_map/pallas_call | solution.py:509
  (2 shorter events, 0.0 us)
Async XLA Ops:
  0.6 1.6 %collective-permute-start = (f32[4,16,128]{2,1,0:T(8,128)}, f32[4,16,128]{2,1,0:T(8,128)S(1)}, u32[]{:S(2)}, u32[]{:S(2)}) collective-permute-start(f32[4,16,128]{2,1,0:T(8,128)} %refs_4_.1), channel_id=1, source_target_pairs={{0,1},{1,0},{2,3},{3,2},{4,5},{5,4},{6,7},{7,6},{8,9},{9,8},{10,11... | collective-permute-start | bytes 98312 | tf_op jit(solution)/shard_map/ppermute | solution.py:441
  2.4 7.0 %collective-permute-start.1 = (f32[112,128]{1,0:T(8,128)S(1)}, f32[112,128]{1,0:T(8,128)S(1)}, u32[]{:S(2)}, u32[]{:S(2)}) collective-permute-start(f32[112,128]{1,0:T(8,128)S(1)} %shard_map.104.own_sheet_ref), channel_id=1, source_target_pairs={{0,2},{2,0},{1,3},{3,1},{4,6},{6,4},{5,7},{7,5},{8,10},{10,8},{9,1... | collective-permute-start | bytes 172040 | tf_op jit(solution)/shard_map/ppermute | solution.py:441
  5.2 4.1 %collective-permute-start.3 = (f32[96,128]{1,0:T(8,128)S(1)}, f32[96,128]{1,0:T(8,128)S(1)}, u32[]{:S(2)}, u32[]{:S(2)}) collective-permute-start(f32[96,128]{1,0:T(8,128)S(1)} %get-tuple-element.24.own_tables_ref.own_ref), channel_id=1, source_target_pairs={{0,2},{2,0},{1,3},{3,1},{4,6},{6,4},{5,7},{7,5},{8,10},{10,8},{9,1... | collective-permute-start | bytes 147464 | tf_op jit(solution)/shard_map/ppermute | solution.py:441
  9.3 4.2 %collective-permute-start.4 = (f32[80,128]{1,0:T(8,128)S(1)}, f32[80,128]{1,0:T(8,128)S(1)}, u32[]{:S(2)}, u32[]{:S(2)}) collective-permute-start(f32[80,128]{1,0:T(8,128)S(1)} %get-tuple-element.25), channel_id=1, source_target_pairs={{0,4},{4,0},{8,12},{12,8},{1,5},{5,1},{9,13},{13,9},{2,6},{6,2},{1... | collective-permute-start | bytes 122888 | tf_op jit(solution)/shard_map/ppermute | solution.py:441
  11.0 5.8 %collective-permute-start.5 = (f32[80,128]{1,0:T(8,128)S(1)}, f32[80,128]{1,0:T(8,128)S(1)}, u32[]{:S(2)}, u32[]{:S(2)}) collective-permute-start(f32[80,128]{1,0:T(8,128)S(1)} %get-tuple-element.26), channel_id=1, source_target_pairs={{0,12},{4,8},{8,4},{12,0},{1,13},{5,9},{9,5},{13,1},{2,14},{6,10},... | collective-permute-start | bytes 122888 | tf_op jit(solution)/shard_map/ppermute | solution.py:441
  13.5 5.3 %collective-permute-start.6 = (f32[80,128]{1,0:T(8,128)S(1)}, f32[80,128]{1,0:T(8,128)S(1)}, u32[]{:S(2)}, u32[]{:S(2)}) collective-permute-start(f32[80,128]{1,0:T(8,128)S(1)} %get-tuple-element.27), channel_id=1, source_target_pairs={{0,8},{4,12},{8,0},{12,4},{1,9},{5,13},{9,1},{13,5},{2,10},{6,14},... | collective-permute-start | bytes 122888 | tf_op jit(solution)/shard_map/ppermute | solution.py:441
  13.6 5.5 %collective-permute-start.2 = (f32[64,128]{1,0:T(8,128)S(1)}, f32[64,128]{1,0:T(8,128)S(1)}, u32[]{:S(2)}, u32[]{:S(2)}) collective-permute-start(f32[64,128]{1,0:T(8,128)S(1)} %slice.4), channel_id=1, source_target_pairs={{0,1},{1,0},{2,3},{3,2},{4,5},{5,4},{6,7},{7,6},{8,9},{9,8},{10,11... | collective-permute-start | bytes 98312 | tf_op jit(solution)/shard_map/ppermute | solution.py:441
  20.5 5.2 %collective-permute-start.7 = (f32[8,128]{1,0:T(8,128)S(1)}, f32[8,128]{1,0:T(8,128)S(1)}, u32[]{:S(2)}, u32[]{:S(2)}) collective-permute-start(f32[8,128]{1,0:T(8,128)S(1)} %get-tuple-element.35), channel_id=1, source_target_pairs={{0,4},{4,0},{8,12},{12,8},{1,5},{5,1},{9,13},{13,9},{2,6},{6,2},{1... | collective-permute-start | bytes 12296 | tf_op jit(solution)/shard_map/ppermute | solution.py:441
  20.9 4.8 %collective-permute-start.8 = (f32[8,128]{1,0:T(8,128)S(1)}, f32[8,128]{1,0:T(8,128)S(1)}, u32[]{:S(2)}, u32[]{:S(2)}) collective-permute-start(f32[8,128]{1,0:T(8,128)S(1)} %get-tuple-element.36), channel_id=1, source_target_pairs={{0,8},{4,12},{8,0},{12,4},{1,9},{5,13},{9,1},{13,5},{2,10},{6,14},... | collective-permute-start | bytes 12296 | tf_op jit(solution)/shard_map/ppermute | solution.py:441
  22.5 5.4 %collective-permute-start.9 = (f32[8,128]{1,0:T(8,128)S(1)}, f32[8,128]{1,0:T(8,128)S(1)}, u32[]{:S(2)}, u32[]{:S(2)}) collective-permute-start(f32[8,128]{1,0:T(8,128)S(1)} %get-tuple-element.37), channel_id=1, source_target_pairs={{0,12},{4,8},{8,4},{12,0},{1,13},{5,9},{9,5},{13,1},{2,14},{6,10},... | collective-permute-start | bytes 12296 | tf_op jit(solution)/shard_map/ppermute | solution.py:441

commit v3 on v2

--- a/solution.py
+++ b/solution.py
@@ -114,13 +114,19 @@
 TABLE = 24
 PACKED = 16
 TABLES = 4 * TABLE
-AT_LEFT = 16
-AT_REQUEST = 32
-AT_LEVELS = 48
-SHEET = 112
-AT_EDGE = 2 * TABLE
-AT_ASKED = AT_EDGE + 16
+AT_EDGE = TABLE
+AT_ASKED = AT_EDGE + 8
 LETTER = AT_ASKED + 16
+AT_REQUEST = 64
+STRIP = AT_REQUEST + 16
+AT_HALO = 4 * TABLE
+AT_HALO_ASKED = AT_HALO + 8
+SHEET = AT_HALO_ASKED + 16
+OTHER_HALO = TABLE
+BESIDE_BLOCKS = OTHER_HALO + 8
+BESIDE_HALO = BESIDE_BLOCKS + 3 * TABLE
+OTHER_LEVELS = BESIDE_HALO + 8
+BESIDE_LEVELS = OTHER_LEVELS + 64
 EDGE = 16
 WIDE = 32
 VMEM_LIMIT = 4 * 1024 * 1024
@@ -157,7 +163,7 @@
 
 
 def tables_kernel(*refs):
-    arrays, (tables_ref, factors_ref, levels_ref, asked_ref), held, arrived = refs[:8], refs[8:12], refs[12:-1], refs[-1]
+    arrays, (letters_ref, factors_ref, strip_ref), held, arrived = refs[:8], refs[8:11], refs[11:-1], refs[-1]
     copies = [pltpu.make_async_copy(a, h, arrived.at[i]) for i, (a, h) in enumerate(zip(arrays, held))]
     for copy in copies:
         copy.start()
@@ -176,8 +182,7 @@
         return jnp.where(near[: beyond.shape[0]], jnp.where(wide < HALF, east, west), 0.0)
 
     def packed(cells):
-        spread = [jnp.where(row == i, turn(cells, EDGE * i), 0.0) for i in range(ROWS)]
-        return jnp.sum(sum(spread), axis=0, keepdims=True)
+        return jnp.sum(pltpu.roll(cells, 0, 1, stride=EDGE, stride_axis=0), axis=0, keepdims=True)
 
     def tiles_of(cells):
         return [cells[:, LANES * z : LANES * (z + 1)] for z in range(4)]
@@ -185,107 +190,74 @@
     ocean = tiles_of(ocean_ref[:, 0, :])
     table = tiles_of(jnp.concatenate([slot_ref[:, 0, :].astype(jnp.float32), weight_ref[:, 0, :]], 0))
     mask = tiles_of(mask_ref[...].astype(jnp.float32))
+    to_right = jnp.zeros((ROWS, LANES), jnp.float32)
+    to_left = jnp.zeros((ROWS, LANES), jnp.float32)
+    for group in range(LANES // EDGE):
+        tile = atmos_ref[group // 2, ROWS * (group % 2) : ROWS * (group % 2 + 1), :]
+        here = lane // EDGE == group
+        to_right = jnp.where(here, turn(tile, EDGE * (group + 1)), to_right)
+        to_left = jnp.where(here, turn(tile, EDGE * group), to_left)
+    edge = jnp.where(comp == 0, to_left, to_right)
+    requests = request_ref[0].astype(jnp.float32)
     for z in range(4):
-        base = (z ^ space) * TABLE
-        tables_ref[pl.ds(base, 8), :] = ocean[z]
-        tables_ref[pl.ds(base + 8, 8), :] = table[z]
+        k = z ^ space
+        letters_ref[k, :8, :] = ocean[z]
+        letters_ref[k, 8:16, :] = table[z]
         last = jnp.where(row == 0, packed(halo(ocean, z)), 0.0)
         last = jnp.where(row == 1, packed(halo(table, z)), last)
         last = jnp.where(row == 2, mask[z], last)
-        tables_ref[pl.ds(base + PACKED, 8), :] = jnp.where(row == 3, halo(mask, z), last)
+        letters_ref[k, PACKED:TABLE, :] = jnp.where(row == 3, halo(mask, z), last)
+        letters_ref[k, AT_EDGE:AT_ASKED, :] = edge
+        letters_ref[k, AT_ASKED : AT_ASKED + 8, :] = requests[:, :LANES]
+        letters_ref[k, AT_ASKED + 8 :, :] = requests[:, LANES:]
     for other in range(LEVELS):
         factors_ref[LEVELS * other : LEVELS * (other + 1), :] = jnp.broadcast_to(
-            mixing_ref[:, other : other + 1], (ROWS, LANES)
+            TENDENCY * mixing_ref[:, other : other + 1], (ROWS, LANES)
         )
     for field in range(FIELDS):
-        mine = [coupling_ref[:, FIELDS * i + field : FIELDS * i + field + 1] for i in range(2)]
+        other = [coupling_ref[:, FIELDS * i + field : FIELDS * i + field + 1] for i in range(2)]
         at = LEVELS * (LEVELS + field)
-        factors_ref[at : at + LEVELS, :] = jnp.broadcast_to(jnp.where(lev == 0, mine[0], mine[1]), (ROWS, LANES))
-    levels_ref[...] = atmos_ref[...]
-    requests = request_ref[0].astype(jnp.float32)
-    asked_ref[:ROWS, :] = requests[:, :LANES]
-    asked_ref[ROWS:, :] = requests[:, LANES:]
-
-
-def sheet_kernel(levels_ref, other_ref, asked_ref, sheet_ref):
+        factors_ref[at : at + LEVELS, :] = jnp.broadcast_to(jnp.where(lev == 0, other[1], other[0]), (ROWS, LANES))
+    for level in range(LEVELS // 2):
+        strip_ref[2 * ROWS * level : 2 * ROWS * (level + 1), :] = atmos_ref[level]
+    strip_ref[AT_REQUEST : AT_REQUEST + 8, :] = requests[:, :LANES]
+    strip_ref[AT_REQUEST + 8 :, :] = requests[:, LANES:]
+
+
+def sheet_kernel(own_ref, three_ref, two_ref, one_ref, sheet_ref):
     space, comp, lev = place()
-    lane = lane_of()
-    for block, ref in ((lev, levels_ref), (1 - lev, other_ref)):
-        to_right = jnp.zeros((ROWS, LANES), jnp.float32)
-        to_left = jnp.zeros((ROWS, LANES), jnp.float32)
-        for group in range(LANES // EDGE):
-            tile = ref[group // 2, ROWS * (group % 2) : ROWS * (group % 2 + 1), :]
-            here = lane // EDGE == group
-            to_right = jnp.where(here, turn(tile, EDGE * (group + 1)), to_right)
-            to_left = jnp.where(here, turn(tile, EDGE * group), to_left)
-        sheet_ref[pl.ds(ROWS * block, 8), :] = to_right
-        sheet_ref[pl.ds(AT_LEFT + ROWS * block, 8), :] = to_left
-    sheet_ref[AT_REQUEST:AT_LEVELS, :] = asked_ref[...]
-    for level in range(LEVELS // 2):
-        at = AT_LEVELS + 2 * ROWS * level
-        sheet_ref[at : at + 2 * ROWS, :] = levels_ref[level]
-
-
-def letter_kernel(own_tables_ref, own_sheet_ref, beside_tables_ref, beside_sheet_ref, *letter_refs):
+    for k, ref in enumerate((own_ref, one_ref, two_ref, three_ref)):
+        sheet_ref[TABLE * k : TABLE * (k + 1), :] = ref[:TABLE, :]
+    near = (space + comp) % 2 == 0
+    sheet_ref[AT_HALO:, :] = jnp.where(near, one_ref[AT_EDGE:, :], three_ref[AT_EDGE:, :])
+
+
+def margins_kernel(strip_ref, strip_beside_ref, own_ref, beside_ref, wet_ref, named_ref, rows_ref):
     space, comp, lev = place()
-    sheets = (own_sheet_ref, beside_sheet_ref)
-    for k in (1, 2, 3):
-        letter_ref = letter_refs[k - 1]
-        letter_ref[:TABLE, :] = own_tables_ref[TABLE * k : TABLE * (k + 1), :]
-        letter_ref[TABLE : 2 * TABLE, :] = beside_tables_ref[TABLE * k : TABLE * (k + 1), :]
-        east = (space ^ k) > space
-        mine = comp == jnp.where(east, 1, 0)
-        edges = [jnp.where(east, ref[:AT_LEFT, :], ref[AT_LEFT:AT_REQUEST, :]) for ref in sheets]
-        asked = [ref[AT_REQUEST:AT_LEVELS, :] for ref in sheets]
-        letter_ref[AT_EDGE:AT_ASKED, :] = jnp.where(mine, edges[0], edges[1])
-        letter_ref[AT_ASKED:LETTER, :] = jnp.where(mine, asked[0], asked[1])
-
-
-def margins_kernel(
-    own_ref,
-    beside_ref,
-    own_sheet_ref,
-    beside_sheet_ref,
-    one_ref,
-    two_ref,
-    three_ref,
-    ocean_ref,
-    wet_ref,
-    named_ref,
-    rows_ref,
-):
-    space, comp, lev = place()
-    strip = 2 * space + comp
     lane, row = lane_of(), row_of()
-    blocks = [(own_ref, 0), (beside_ref, 0)]
-    for ref in (one_ref, two_ref, three_ref):
-        blocks += [(ref, 0), (ref, TABLE)]
-    for m, (ref, start) in enumerate(blocks):
-        rows_ref[pl.ds((m ^ strip) * TABLE, TABLE), :] = ref[start : start + TABLE, :]
+    for k in range(4):
+        for ref, c in ((own_ref, comp), (beside_ref, 1 - comp)):
+            at = (2 * (space ^ k) + c) * TABLE
+            rows_ref[pl.ds(at, TABLE), :] = ref[TABLE * k : TABLE * (k + 1), :]
 
     def table_row(which):
         return rows_ref[pl.ds(which, ROWS, stride=TABLE), :]
 
-    ocean_halo = table_row(PACKED)
-    for field in range(FIELDS):
-        ocean_ref[field, :, :LANES] = table_row(field)
-        ocean_ref[field, :, LANES:] = turn(ocean_halo, -EDGE * field)
     near = (lane < EDGE // 2) | (lane >= LANES - EDGE // 2)
     wet_ref[:, :LANES] = table_row(PACKED + 2)
     wet_ref[:, LANES:] = jnp.where(near, table_row(PACKED + 3), 0.0)
 
-    even = space % 2 == 0
-    own = [own_sheet_ref[AT_REQUEST + 8 * i : AT_REQUEST + 8 * (i + 1), :] for i in range(2)]
-    beside = [beside_sheet_ref[AT_REQUEST + 8 * i : AT_REQUEST + 8 * (i + 1), :] for i in range(2)]
-    one = [one_ref[AT_ASKED + 8 * i : AT_ASKED + 8 * (i + 1), :] for i in range(2)]
-    three = [three_ref[AT_ASKED + 8 * i : AT_ASKED + 8 * (i + 1), :] for i in range(2)]
-
-    def either(first_is, first, second):
-        return [jnp.where(first_is, a, b) for a, b in zip(first, second)]
-
+    def halves(ref, at):
+        return [ref[at + 8 * i : at + 8 * (i + 1), :] for i in range(2)]
+
+    def by_comp(mine, theirs):
+        return [jnp.where(comp == 0, a, b) for a, b in zip(mine, theirs)]
+
+    strips = halves(strip_ref, AT_REQUEST), halves(strip_beside_ref, AT_REQUEST)
+    halos = halves(own_ref, AT_HALO_ASKED), halves(beside_ref, AT_HALO_ASKED)
     tables = (
-        (either(comp == 0, own, beside), either(comp == 0, beside, own)),
-        (either(even, one, three), either(even, three, one)),
+        (by_comp(*strips), by_comp(*strips[::-1])),
+        (by_comp(*halos), by_comp(*halos[::-1])),
     )
     first = ((2 * row - 1) * LANES + 2 * (lane & (HALF - 1))).astype(jnp.float32)
     parity = (lane & 1).astype(jnp.float32)
@@ -315,13 +287,11 @@
 
 def column_kernel(
     factors_ref,
+    strip_ref,
+    strip_beside_ref,
     own_ref,
-    own_other_ref,
     beside_ref,
-    beside_other_ref,
-    one_ref,
-    three_ref,
-    ocean_ref,
+    others_ref,
     wet_ref,
     named_ref,
     atmos_ref,
@@ -329,9 +299,9 @@
     first_ref,
     second_ref,
     third_ref,
-    fourth_ref,
     state_ref,
     flux_ref,
+    rows_ref,
     back_ref,
 ):
     space, comp, lev = place()
@@ -342,16 +312,18 @@
     theirs = pl.ds(pl.multiple_of((1 - comp) * LANES, LANES), LANES)
     for level in range(half):
         here, there = lev * half + level, (1 - lev) * half + level
-        state_ref[here, :, mine] = own_ref[level]
-        state_ref[there, :, mine] = own_other_ref[level]
         at = 2 * ROWS * level
-        state_ref[here, :, theirs] = beside_ref[AT_LEVELS + at : AT_LEVELS + at + 2 * ROWS, :]
-        state_ref[there, :, theirs] = beside_other_ref[at : at + 2 * ROWS, :]
-    even = space % 2 == 0
+        state_ref[here, :, mine] = strip_ref[at : at + 2 * ROWS, :]
+        state_ref[there, :, mine] = others_ref[OTHER_LEVELS + at : OTHER_LEVELS + at + 2 * ROWS, :]
+        state_ref[there, :, theirs] = strip_beside_ref[at : at + 2 * ROWS, :]
+        state_ref[here, :, theirs] = others_ref[BESIDE_LEVELS + at : BESIDE_LEVELS + at + 2 * ROWS, :]
     exists = jnp.where(lane < HALF, space + 1, 4 - space) < 4
-    for block in range(2):
-        one, three = [ref[AT_EDGE + ROWS * block : AT_EDGE + ROWS * (block + 1), :] for ref in (one_ref, three_ref)]
-        east, west = jnp.where(even, one, three), jnp.where(even, three, one)
+    halos = (
+        (lev, others_ref[OTHER_HALO:BESIDE_BLOCKS, :], beside_ref[AT_HALO:AT_HALO_ASKED, :]),
+        (1 - lev, own_ref[AT_HALO:AT_HALO_ASKED, :], others_ref[BESIDE_HALO:OTHER_LEVELS, :]),
+    )
+    for block, own, beside in halos:
+        east, west = jnp.where(comp == 0, own, beside), jnp.where(comp == 0, beside, own)
         for group in range(LANES // EDGE):
             tile = jnp.where(
                 lane < EDGE,
@@ -375,7 +347,7 @@
             cells = atmos[level]
             beside = turn(cells, 1) + turn(cells, -1) + rows_down(cells) + rows_up(cells)
             column = sum(factor(LEVELS * other + level) * shaded[other] for other in range(LEVELS))
-            cells = cells + DIFFUSE * (beside - 4.0 * cells) + TENDENCY * column
+            cells = DIFFUSE * (cells + beside) + column
             later.append(inside * cells)
         atmos = later
     for level in range(LEVELS):
@@ -389,6 +361,14 @@
             flux_ref[tile, WIDE * field : WIDE * field + 8, :] = jnp.zeros((ROWS, LANES), jnp.float32)
             flux_ref[tile, WIDE * field + 8 : WIDE * field + 24, :] = flux[:, LANES * tile : LANES * (tile + 1)]
             flux_ref[tile, WIDE * field + 24 : WIDE * field + 32, :] = jnp.zeros((ROWS, LANES), jnp.float32)
+
+    for k in range(4):
+        own, beside = 2 * (space ^ k) + comp, 2 * (space ^ k) + 1 - comp
+        block = slice(TABLE * k, TABLE * (k + 1))
+        came = slice(BESIDE_BLOCKS + TABLE * (k - 1), BESIDE_BLOCKS + TABLE * k)
+        rows_ref[pl.ds(own * TABLE, TABLE), :] = own_ref[block, :] if k else others_ref[:TABLE, :]
+        rows_ref[pl.ds(beside * TABLE, TABLE), :] = others_ref[came, :] if k else beside_ref[block, :]
+    ocean_halo = rows_ref[pl.ds(PACKED, ROWS, stride=TABLE), :]
 
     wetness = wet_ref[...]
     pairs = (2 * lane) & (LANES - 1)
@@ -403,17 +383,19 @@
             sums.append(pick_lanes(total + turn(total, -1), pairs))
         remapped = jnp.concatenate([jnp.where(lane < HALF, sums[0], sums[1]), sums[2]], 1)
         forcing.append(wetness * (FORCING * remapped))
-        ocean.append(ocean_ref[field])
+        main = rows_ref[pl.ds(field, ROWS, stride=TABLE), :]
+        ocean.append(jnp.concatenate([main, turn(ocean_halo, -EDGE * field)], 1))
+    spreading = OCEAN_MIX * wetness
     for substep in range(SUB):
         for field in range(FIELDS):
             cells = ocean[field]
             beside = turn(cells, 1) + turn(cells, -1) + rows_down(cells) + rows_up(cells)
-            ocean[field] = wetness * (cells + OCEAN_MIX * (beside - 4.0 * cells)) + forcing[field]
+            ocean[field] = spreading * (cells + beside) + forcing[field]
     for field in range(FIELDS):
         cells = ocean[field][:, :LANES]
-        final_ref[field] = cells
+        final_ref[ROWS * field : ROWS * (field + 1), :] = cells
         back_ref[pl.ds(field, ROWS, stride=FIELDS), :] = cells
-    for k, ref in enumerate((first_ref, second_ref, third_ref, fourth_ref)):
+    for k, ref in zip((1, 2, 3), (first_ref, second_ref, third_ref)):
         ref[...] = back_ref[pl.ds((2 * (space ^ k) + comp) * FIELDS, FIELDS), :]
 
 
@@ -424,21 +406,27 @@
     named = [jnp.where(comp == 0, named_ref[step, 0], named_ref[step, 1]) for step in range(4)]
     pairs = (lane >> 1) + HALF * comp
     for field in range(FIELDS):
-        spread = pick_lanes(final_ref[field], pairs)
+        spread = pick_lanes(final_ref[ROWS * field : ROWS * (field + 1), :], pairs)
         upper = named[1] * spread + rows_down(named[3] * spread)
         lower = named[2] * spread + rows_up(named[0] * spread)
         returned_ref[pl.ds(2 * ROWS * field, ROWS, stride=2), :] = upper
         returned_ref[pl.ds(2 * ROWS * field + 1, ROWS, stride=2), :] = lower
 
 
-def rows_kernel(own_ref, one_ref, two_ref, three_ref, ocean_ref):
+def rows_kernel(three_ref, two_ref, one_ref, final_ref, ocean_ref):
     space, comp, lev = place()
-    for k, ref in enumerate((own_ref, one_ref, two_ref, three_ref)):
-        ocean_ref[:, 0, pl.ds(pl.multiple_of((space ^ k) * LANES, LANES), LANES)] = ref[...]
+    own = final_ref[pl.ds(2 * space + comp, FIELDS, stride=ROWS), :]
+    for k, cells in enumerate((own, one_ref[...], two_ref[...], three_ref[...])):
+        ocean_ref[:, 0, pl.ds(pl.multiple_of((space ^ k) * LANES, LANES), LANES)] = cells
 
 
 def over(axis, k, array):
     return lax.ppermute(array, axis, [(i, i ^ k) for i in range(lax.axis_size(axis))])
+
+
+def across(axis, k, array):
+    pairs = [(2 * i + core, 2 * (i ^ k) + 1 - core) for i in range(lax.axis_size(axis)) for core in range(2)]
+    return lax.ppermute(array, (axis, "lev"), pairs)
 
 
 def local(kernel, out_shape, spaces, scratch=()):
@@ -469,44 +457,45 @@
 
     arrays = (ocean_state, margin_slot, margin_weight, sea_mask, atmos_state, request_cells)
     arrays += (vertical_mixing, flux_coupling.T)
-    own_other = over("lev", 1, atmos_state)
-    tables, factors, levels, asked = local(
+    letters, factors, strip = local(
         tables_kernel,
-        (values(TABLES, LANES), values(2 * LEVELS * LEVELS, LANES), values(*atmos_state.shape), values(2 * ROWS, LANES)),
+        (values(4, LETTER, LANES), values(2 * LEVELS * LEVELS, LANES), values(STRIP, LANES)),
         [pltpu.HBM] * 8,
         [pltpu.VMEM(a.shape, a.dtype) for a in arrays] + [pltpu.SemaphoreType.DMA((8,))],
     )(*(pltpu.with_memory_space_constraint(a, pltpu.HBM) for a in arrays))
-    tables_beside = over("comp", 1, tables)
-    sheet = local(sheet_kernel, values(SHEET, LANES), [pltpu.VMEM] * 3)(levels, own_other, asked)
-    sheet_beside = over("comp", 1, sheet)
-    letters = local(letter_kernel, (values(LETTER, LANES),) * 3, [pltpu.VMEM] * 4)(
-        tables, sheet, tables_beside, sheet_beside
-    )
-    one, two, three = (over("space", k, letter) for k, letter in zip((1, 2, 3), letters))
-    beside_other = over("lev", 1, sheet_beside[AT_LEVELS:])
-    ocean, wet, named = local(
+    one, three = (across("space", k, letters[k]) for k in (1, 3))
+    two = across("space", 2, letters[2, :TABLE])
+    strip_beside = across("comp", 1, strip)
+    sheet = local(sheet_kernel, values(SHEET, LANES), [pltpu.VMEM] * 4)(letters[0], three, two, one)
+    sheet_beside = across("comp", 1, sheet)
+    swapped = (sheet[:TABLE], sheet[AT_HALO:AT_HALO_ASKED], sheet_beside[TABLE:AT_HALO_ASKED])
+    swapped += (strip[:AT_REQUEST], strip_beside[:AT_REQUEST])
+    others = over("lev", 1, jnp.concatenate(swapped, 0))
+    wet, named = local(
         margins_kernel,
-        (values(FIELDS, ROWS, 2 * LANES), values(ROWS, 2 * LANES), values(4, 3, ROWS, LANES)),
-        [pltpu.VMEM] * 7,
+        (values(ROWS, 2 * LANES), values(4, 3, ROWS, LANES)),
+        [pltpu.VMEM] * 4,
         [pltpu.VMEM((ROWS * TABLE, LANES), jnp.float32)],
-    )(tables, tables_beside, sheet, sheet_beside, one, two, three)
+    )(strip, strip_beside, sheet, sheet_beside)
     atmos, final, *back = local(
         column_kernel,
-        (values(*atmos_state.shape), values(FIELDS, ROWS, LANES)) + (values(FIELDS, LANES),) * 4,
-        [pltpu.VMEM] * 10,
+        (values(*atmos_state.shape), values(FIELDS * ROWS, LANES)) + (values(FIELDS, LANES),) * 3,
+        [pltpu.VMEM] * 8,
         [
             pltpu.VMEM((LEVELS, 2 * ROWS, 3 * LANES), jnp.float32),
             pltpu.VMEM((3, FIELDS * WIDE, LANES), jnp.float32),
+            pltpu.VMEM((ROWS * TABLE, LANES), jnp.float32),
             pltpu.VMEM((ROWS * FIELDS, LANES), jnp.float32),
         ],
-    )(factors, levels, own_other, sheet_beside, beside_other, one, three, ocean, wet, named)
-    pieces = [over("space", k, piece) for k, piece in zip((1, 2, 3), back[1:])]
+    )(factors, strip, strip_beside, sheet, sheet_beside, others, wet, named)
+    one, two, three = (across("space", k, piece) for k, piece in zip((1, 2, 3), back))
+    final = over("lev", 1, final)
     atmos_next, returned = local(
         returned_kernel,
         (values(*atmos_state.shape), values(FIELDS * 2 * ROWS, LANES)),
         [pltpu.VMEM] * 3,
     )(atmos, final, named)
-    ocean_next = local(rows_kernel, values(*ocean_state.shape), [pltpu.VMEM] * 4)(back[0], *pieces)
+    ocean_next = local(rows_kernel, values(*ocean_state.shape), [pltpu.VMEM] * 4)(three, two, one, final)
     return (atmos_next, ocean_next, returned.reshape(FIELDS, 2 * ROWS, LANES))
 
 

time: 28.8 us -> 25 us (0.87)
  waiting for transfers between devices: 11.4 us -> 6.42 us
  starting transfers between devices: 12.2 us -> 13.5 us
    ppermute x0 -> x8, starting transfers between devices: none -> 12.4 us  [across(): return lax.ppermute(array, (axis, 'lev'), pairs)]
    ppermute x10 -> x2, starting transfers between devices: 12.2 us -> 1.06 us  [over(): lax.ppermute(array, axis, [(i, i ^ k) for i in range(lax.axis_size(axis))])]
    ppermute x10 -> x2, waiting for transfers between devices: 11.4 us -> 0.69 us  [over(): lax.ppermute(array, axis, [(i, i ^ k) for i in range(lax.axis_size(axis))])]
    ppermute x0 -> x8, waiting for transfers between devices: none -> 5.72 us  [across(): return lax.ppermute(array, (axis, 'lev'), pairs)]
    pallas_call x5 -> x4, Pallas kernels: 2.92 us -> 2.76 us  [the longest x1 1.42 us: shards_by_columns(): local(column_kernel, (values(*atmos_state.shape), values(FIELDS * ROWS, L...]
  transfers between devices with their start and end apart: 10 -> 10, of which waited for: 4 -> 6; matrix products, arithmetic and copies ran while one was open for 0% -> 0% of each run, Pallas kernels for 7% -> 4%
where the time goes in v3:
time: 25 us; the launch traced here: 24.7 us
  starting transfers between devices  13.5 us (54%)
  waiting for transfers between devices  6.42 us (26%)
  Pallas kernels  4.11 us (16%)
  between operations  0.7 us (3%)
    ppermute x8, starting transfers between devices, across(): return lax.ppermute(array, (axis, 'lev'), pairs)  12.4 us
    ppermute x8, waiting for transfers between devices, across(): return lax.ppermute(array, (axis, 'lev'), pairs)  5.72 us
    pallas_call x1, Pallas kernels, shards_by_columns(): local(column_kernel, (values(*atmos_state.shape), values(FIELDS * ROWS, L...  1.42 us
    ppermute x2, starting transfers between devices, over(): lax.ppermute(array, axis, [(i, i ^ k) for i in range(lax.axis_size(axis))])  1.06 us
    pallas_call x1, Pallas kernels, shards_by_columns(): local(tables_kernel, (values(4, LETTER, LANES), values(2 * LEVELS * LEVEL...  1.05 us
    pallas_call x1, Pallas kernels, shards_by_columns(): local(returned_kernel, (values(*atmos_state.shape), values(FIELDS * 2 * R...  0.72 us
    ppermute x2, waiting for transfers between devices, over(): lax.ppermute(array, axis, [(i, i ^ k) for i in range(lax.axis_size(axis))])  0.69 us
    pallas_call x1, Pallas kernels, shards_by_columns(): local(rows_kernel, values(*ocean_state.shape), [pltpu.VMEM] * 4)  0.63 us
  transfers between devices with their start and end apart: 10, of which 6 were waited for; matrix products, arithmetic and copies ran while one was open for 0% of the time, Pallas kernels for 4%

profile of v3, /device:TPU:0, one launch (start us, length us, event | category | flops | bytes accessed | tf_op | source)
XLA Modules:
  0.0 24.7 jit_solution(7146437779004910927)
XLA Ops:
  0.6 1.0 %shard_map.103 = (f32[4,48,128]{2,1,0:T(8,128)S(1)}, f32[128,128]{1,0:T(8,128)S(1)}, f32[80,128]{1,0:T(8,128)S(1)}) custom-call(f32[8,1,512]{2,1,0:T(1,128)} %refs_0_.1, s32[4,1,512]{2,1,0:T(1,128)} %refs_1_.1, f32[4,1,512]{2,1,0:T(1,128)} %refs_2_.1, s32[1,512]{1,0:T(1,128)} %refs_3_.1, f32[4,16,128]{2,1,0:T(8,128)} %refs_4_.1, s32[1,8,256]{2,1,0:T(8,128)} %refs_5_.1, ...), custom_call_target="tpu_custom_call" | custom-call | tf_op jit(solution)/shard_map/pallas_call | solution.py:460
  1.7 4.6 %collective-permute-start.1 = (f32[48,128]{1,0:T(8,128)S(1)}, f32[48,128]{1,0:T(8,128)S(1)}, u32[]{:S(2)}, u32[]{:S(2)}) collective-permute-start(f32[48,128]{1,0:T(8,128)S(1)} %get-tuple-element.28), channel_id=1, source_target_pairs={{0,13},{1,12},{4,9},{5,8},{8,5},{9,4},{12,1},{13,0},{2,15},{3,14},... | collective-permute-start | bytes 73736 | tf_op jit(solution)/shard_map/ppermute | solution.py:429
  6.3 0.0 collective-permute-start.3
  6.3 0.9 %collective-permute-start.2 = (f32[24,128]{1,0:T(8,128)S(1)}, f32[24,128]{1,0:T(8,128)S(1)}, u32[]{:S(2)}, u32[]{:S(2)}) collective-permute-start(f32[24,128]{1,0:T(8,128)S(1)} %slice_bitcast_fusion.3), channel_id=1, source_target_pairs={{0,9},{1,8},{4,13},{5,12},{8,1},{9,0},{12,5},{13,4},{2,11},{3,10},... | collective-permute-start | bytes 36872 | tf_op jit(solution)/shard_map/ppermute | solution.py:429
  7.2 1.4 %collective-permute-start = (f32[80,128]{1,0:T(8,128)S(1)}, f32[80,128]{1,0:T(8,128)S(1)}, u32[]{:S(2)}, u32[]{:S(2)}) collective-permute-start(f32[80,128]{1,0:T(8,128)S(1)} %get-tuple-element.16.strip_ref), channel_id=1, source_target_pairs={{0,3},{1,2},{2,1},{3,0},{4,7},{5,6},{6,5},{7,4},{8,11},{9,10},{10,... | collective-permute-start | bytes 122888 | tf_op jit(solution)/shard_map/ppermute | solution.py:429
  8.5 1.9 %collective-permute-done.2.two_ref = f32[24,128]{1,0:T(8,128)S(1)} collective-permute-done((f32[24,128]{1,0:T(8,128)S(1)}, f32[24,128]{1,0:T(8,128)S(1)}, u32[]{:S(2)}, u32[]{:S(2)}) %collective-permute-start.2) | collective-permute-done | bytes 12320 | tf_op jit(solution)/shard_map/ppermute | solution.py:429
  10.4 0.0 collective-permute-done.1.three_ref
  10.4 0.0 collective-permute-done.3.one_ref
  10.4 1.7 %collective-permute-start.4 = (f32[120,128]{1,0:T(8,128)S(1)}, f32[120,128]{1,0:T(8,128)S(1)}, u32[]{:S(2)}, u32[]{:S(2)}) collective-permute-start(f32[120,128]{1,0:T(8,128)S(1)} %shard_map.104.own_ref), channel_id=1, source_target_pairs={{0,3},{1,2},{2,1},{3,0},{4,7},{5,6},{6,5},{7,4},{8,11},{9,10},{10,... | collective-permute-start | bytes 184328 | tf_op jit(solution)/shard_map/ppermute | solution.py:429
  12.2 2.0 %collective-permute-done.4.beside_ref = f32[120,128]{1,0:T(8,128)S(1)} collective-permute-done((f32[120,128]{1,0:T(8,128)S(1)}, f32[120,128]{1,0:T(8,128)S(1)}, u32[]{:S(2)}, u32[]{:S(2)}) %collective-permute-start.4) | collective-permute-done | bytes 61472 | tf_op jit(solution)/shard_map/ppermute | solution.py:429
  14.2 0.0 collective-permute-done.strip_beside_ref
  14.2 0.6 %collective-permute-start.5 = (f32[240,128]{1,0:T(8,128)S(1)}, f32[240,128]{1,0:T(8,128)S(1)}, u32[]{:S(2)}, u32[]{:S(2)}) collective-permute-start(f32[240,128]{1,0:T(8,128)S(1)} %slice_dynamic-update-slice_fusion.1), channel_id=1, source_target_pairs={{0,1},{1,0},{2,3},{3,2},{4,5},{5,4},{6,7},{7,6},{8,9},{9,8},{10,11... | collective-permute-start | bytes 368648 | tf_op jit(solution)/shard_map/ppermute | solution.py:424
  14.8 0.3 %shard_map.105 = (f32[8,256]{1,0:T(8,128)S(1)}, f32[4,3,8,128]{3,2,1,0:T(8,128)S(1)}) custom-call(f32[80,128]{1,0:T(8,128)S(1)} %get-tuple-element.16.strip_ref, f32[80,128]{1,0:T(8,128)S(1)} %collective-permute-done.strip_beside_ref, f32[120,128]{1,0:T(8,128)S(1)} %shard_map.104.own_ref, f32[120,128]{1,0:T(8,128)S(1)} %collective-permute-done.4.beside_ref), custom_call_target="tpu_custom_call" | custom-call | tf_op jit(solution)/shard_map/pallas_call | solution.py:474
  15.1 0.7 %collective-permute-done.5.others_ref = f32[240,128]{1,0:T(8,128)S(1)} collective-permute-done((f32[240,128]{1,0:T(8,128)S(1)}, f32[240,128]{1,0:T(8,128)S(1)}, u32[]{:S(2)}, u32[]{:S(2)}) %collective-permute-start.5) | collective-permute-done | bytes 122912 | tf_op jit(solution)/shard_map/ppermute | solution.py:424
  15.8 1.4 %shard_map.106 = (f32[4,16,128]{2,1,0:T(8,128)S(1)}, f32[64,128]{1,0:T(8,128)S(1)}, f32[8,128]{1,0:T(8,128)S(1)}, f32[8,128]{1,0:T(8,128)S(1)}, f32[8,128]{1,0:T(8,128)S(1)}) custom-call(f32[128,128]{1,0:T(8,128)S(1)} %get-tuple-element.15.factors_ref, f32[80,128]{1,0:T(8,128)S(1)} %get-tuple-element.16.strip_ref, ...), custom_call_target="tpu_custom_call" | custom-call | tf_op jit(solution)/shard_map/pallas_call | solution.py:480
  17.2 0.4 %collective-permute-start.6 = (f32[64,128]{1,0:T(8,128)S(1)}, f32[64,128]{1,0:T(8,128)S(1)}, u32[]{:S(2)}, u32[]{:S(2)}) collective-permute-start(f32[64,128]{1,0:T(8,128)S(1)} %get-tuple-element.21), channel_id=1, source_target_pairs={{0,1},{1,0},{2,3},{3,2},{4,5},{5,4},{6,7},{7,6},{8,9},{9,8},{10,11... | collective-permute-start | bytes 98312 | tf_op jit(solution)/shard_map/ppermute | solution.py:424
  17.6 1.7 %collective-permute-start.7 = (f32[8,128]{1,0:T(8,128)S(1)}, f32[8,128]{1,0:T(8,128)S(1)}, u32[]{:S(2)}, u32[]{:S(2)}) collective-permute-start(f32[8,128]{1,0:T(8,128)S(1)} %get-tuple-element.23), channel_id=1, source_target_pairs={{0,13},{1,12},{4,9},{5,8},{8,5},{9,4},{12,1},{13,0},{2,15},{3,14},... | collective-permute-start | bytes 12296 | tf_op jit(solution)/shard_map/ppermute | solution.py:429
  19.4 1.7 %collective-permute-start.8 = (f32[8,128]{1,0:T(8,128)S(1)}, f32[8,128]{1,0:T(8,128)S(1)}, u32[]{:S(2)}, u32[]{:S(2)}) collective-permute-start(f32[8,128]{1,0:T(8,128)S(1)} %get-tuple-element.24), channel_id=1, source_target_pairs={{0,9},{1,8},{4,13},{5,12},{8,1},{9,0},{12,5},{13,4},{2,11},{3,10},... | collective-permute-start | bytes 12296 | tf_op jit(solution)/shard_map/ppermute | solution.py:429
  21.1 0.4 %collective-permute-start.9 = (f32[8,128]{1,0:T(8,128)S(1)}, f32[8,128]{1,0:T(8,128)S(1)}, u32[]{:S(2)}, u32[]{:S(2)}) collective-permute-start(f32[8,128]{1,0:T(8,128)S(1)} %get-tuple-element.25), channel_id=1, source_target_pairs={{0,5},{1,4},{4,1},{5,0},{8,13},{9,12},{12,9},{13,8},{2,7},{3,6},{6... | collective-permute-start | bytes 12296 | tf_op jit(solution)/shard_map/ppermute | solution.py:429
  21.5 0.0 collective-permute-done.6.final_ref
  21.5 0.7 %shard_map.107 = (f32[4,16,128]{2,1,0:T(8,128)}, f32[128,128]{1,0:T(8,128)}) custom-call(f32[4,16,128]{2,1,0:T(8,128)S(1)} %get-tuple-element.20.atmos_ref, f32[64,128]{1,0:T(8,128)S(1)} %collective-permute-done.6.final_ref, f32[4,3,8,128]{3,2,1,0:T(8,128)S(1)} %get-tuple-element.19.named_ref), custom_call_target="tpu_custom_call" | custom-call | tf_op jit(solution)/shard_map/pallas_call | solution.py:493
  22.2 0.2 collective-permute-done.7.three_ref
  22.5 0.8 %collective-permute-done.8.two_ref = f32[8,128]{1,0:T(8,128)S(1)} collective-permute-done((f32[8,128]{1,0:T(8,128)S(1)}, f32[8,128]{1,0:T(8,128)S(1)}, u32[]{:S(2)}, u32[]{:S(2)}) %collective-permute-start.8) | collective-permute-done | bytes 4128 | tf_op jit(solution)/shard_map/ppermute | solution.py:429
  23.3 0.8 %collective-permute-done.9.one_ref = f32[8,128]{1,0:T(8,128)S(1)} collective-permute-done((f32[8,128]{1,0:T(8,128)S(1)}, f32[8,128]{1,0:T(8,128)S(1)}, u32[]{:S(2)}, u32[]{:S(2)}) %collective-permute-start.9) | collective-permute-done | bytes 4128 | tf_op jit(solution)/shard_map/ppermute | solution.py:429
  24.1 0.6 %shard_map.108 = f32[8,1,512]{2,1,0:T(1,128)} custom-call(f32[8,128]{1,0:T(8,128)S(1)} %collective-permute-done.7.three_ref, f32[8,128]{1,0:T(8,128)S(1)} %collective-permute-done.8.two_ref, f32[8,128]{1,0:T(8,128)S(1)} %collective-permute-done.9.one_ref, f32[64,128]{1,0:T(8,128)S(1)} %collective-permute-done.6.final_ref), custom_call_target="tpu_custom_call" | custom-call | tf_op jit(solution)/shard_map/pallas_call | solution.py:498
  (8 shorter events, 0.0 us)
Async XLA Ops:
  1.7 8.7 %collective-permute-start.1 = (f32[48,128]{1,0:T(8,128)S(1)}, f32[48,128]{1,0:T(8,128)S(1)}, u32[]{:S(2)}, u32[]{:S(2)}) collective-permute-start(f32[48,128]{1,0:T(8,128)S(1)} %get-tuple-element.28), channel_id=1, source_target_pairs={{0,13},{1,12},{4,9},{5,8},{8,5},{9,4},{12,1},{13,0},{2,15},{3,14},... | collective-permute-start | bytes 73736 | tf_op jit(solution)/shard_map/ppermute | solution.py:429
  6.3 4.1 %collective-permute-start.3 = (f32[48,128]{1,0:T(8,128)S(1)}, f32[48,128]{1,0:T(8,128)S(1)}, u32[]{:S(2)}, u32[]{:S(2)}) collective-permute-start(f32[48,128]{1,0:T(8,128)S(1)} %get-tuple-element.27), channel_id=1, source_target_pairs={{0,5},{1,4},{4,1},{5,0},{8,13},{9,12},{12,9},{13,8},{2,7},{3,6},{6... | collective-permute-start | bytes 73736 | tf_op jit(solution)/shard_map/ppermute | solution.py:429
  6.3 4.1 %collective-permute-start.2 = (f32[24,128]{1,0:T(8,128)S(1)}, f32[24,128]{1,0:T(8,128)S(1)}, u32[]{:S(2)}, u32[]{:S(2)}) collective-permute-start(f32[24,128]{1,0:T(8,128)S(1)} %slice_bitcast_fusion.3), channel_id=1, source_target_pairs={{0,9},{1,8},{4,13},{5,12},{8,1},{9,0},{12,5},{13,4},{2,11},{3,10},... | collective-permute-start | bytes 36872 | tf_op jit(solution)/shard_map/ppermute | solution.py:429
  7.2 7.0 %collective-permute-start = (f32[80,128]{1,0:T(8,128)S(1)}, f32[80,128]{1,0:T(8,128)S(1)}, u32[]{:S(2)}, u32[]{:S(2)}) collective-permute-start(f32[80,128]{1,0:T(8,128)S(1)} %get-tuple-element.16.strip_ref), channel_id=1, source_target_pairs={{0,3},{1,2},{2,1},{3,0},{4,7},{5,6},{6,5},{7,4},{8,11},{9,10},{10,... | collective-permute-start | bytes 122888 | tf_op jit(solution)/shard_map/ppermute | solution.py:429
  10.4 3.7 %collective-permute-start.4 = (f32[120,128]{1,0:T(8,128)S(1)}, f32[120,128]{1,0:T(8,128)S(1)}, u32[]{:S(2)}, u32[]{:S(2)}) collective-permute-start(f32[120,128]{1,0:T(8,128)S(1)} %shard_map.104.own_ref), channel_id=1, source_target_pairs={{0,3},{1,2},{2,1},{3,0},{4,7},{5,6},{6,5},{7,4},{8,11},{9,10},{10,... | collective-permute-start | bytes 184328 | tf_op jit(solution)/shard_map/ppermute | solution.py:429
  14.2 1.6 %collective-permute-start.5 = (f32[240,128]{1,0:T(8,128)S(1)}, f32[240,128]{1,0:T(8,128)S(1)}, u32[]{:S(2)}, u32[]{:S(2)}) collective-permute-start(f32[240,128]{1,0:T(8,128)S(1)} %slice_dynamic-update-slice_fusion.1), channel_id=1, source_target_pairs={{0,1},{1,0},{2,3},{3,2},{4,5},{5,4},{6,7},{7,6},{8,9},{9,8},{10,11... | collective-permute-start | bytes 368648 | tf_op jit(solution)/shard_map/ppermute | solution.py:424
  17.2 4.3 %collective-permute-start.6 = (f32[64,128]{1,0:T(8,128)S(1)}, f32[64,128]{1,0:T(8,128)S(1)}, u32[]{:S(2)}, u32[]{:S(2)}) collective-permute-start(f32[64,128]{1,0:T(8,128)S(1)} %get-tuple-element.21), channel_id=1, source_target_pairs={{0,1},{1,0},{2,3},{3,2},{4,5},{5,4},{6,7},{7,6},{8,9},{9,8},{10,11... | collective-permute-start | bytes 98312 | tf_op jit(solution)/shard_map/ppermute | solution.py:424
  17.6 4.8 %collective-permute-start.7 = (f32[8,128]{1,0:T(8,128)S(1)}, f32[8,128]{1,0:T(8,128)S(1)}, u32[]{:S(2)}, u32[]{:S(2)}) collective-permute-start(f32[8,128]{1,0:T(8,128)S(1)} %get-tuple-element.23), channel_id=1, source_target_pairs={{0,13},{1,12},{4,9},{5,8},{8,5},{9,4},{12,1},{13,0},{2,15},{3,14},... | collective-permute-start | bytes 12296 | tf_op jit(solution)/shard_map/ppermute | solution.py:429
  19.4 3.9 %collective-permute-start.8 = (f32[8,128]{1,0:T(8,128)S(1)}, f32[8,128]{1,0:T(8,128)S(1)}, u32[]{:S(2)}, u32[]{:S(2)}) collective-permute-start(f32[8,128]{1,0:T(8,128)S(1)} %get-tuple-element.24), channel_id=1, source_target_pairs={{0,9},{1,8},{4,13},{5,12},{8,1},{9,0},{12,5},{13,4},{2,11},{3,10},... | collective-permute-start | bytes 12296 | tf_op jit(solution)/shard_map/ppermute | solution.py:429
  21.1 3.0 %collective-permute-start.9 = (f32[8,128]{1,0:T(8,128)S(1)}, f32[8,128]{1,0:T(8,128)S(1)}, u32[]{:S(2)}, u32[]{:S(2)}) collective-permute-start(f32[8,128]{1,0:T(8,128)S(1)} %get-tuple-element.25), channel_id=1, source_target_pairs={{0,5},{1,4},{4,1},{5,0},{8,13},{9,12},{12,9},{13,8},{2,7},{3,6},{6... | collective-permute-start | bytes 12296 | tf_op jit(solution)/shard_map/ppermute | solution.py:429

commit v4 on v3

--- a/solution.py
+++ b/solution.py
@@ -463,8 +463,7 @@
         [pltpu.HBM] * 8,
         [pltpu.VMEM(a.shape, a.dtype) for a in arrays] + [pltpu.SemaphoreType.DMA((8,))],
     )(*(pltpu.with_memory_space_constraint(a, pltpu.HBM) for a in arrays))
-    one, three = (across("space", k, letters[k]) for k in (1, 3))
-    two = across("space", 2, letters[2, :TABLE])
+    one, two, three = (across("space", k, letters[k]) for k in (1, 2, 3))
     strip_beside = across("comp", 1, strip)
     sheet = local(sheet_kernel, values(SHEET, LANES), [pltpu.VMEM] * 4)(letters[0], three, two, one)
     sheet_beside = across("comp", 1, sheet)

time: 25 us -> 24.3 us (0.972)
  waiting for transfers between devices: 6.42 us -> 5.97 us
  starting transfers between devices: 13.5 us -> 13.2 us
    ppermute x8, waiting for transfers between devices: 5.72 us -> 5.28 us  [across(): return lax.ppermute(array, (axis, 'lev'), pairs)]
  transfers between devices with their start and end apart: 10 -> 10, of which waited for: 6 -> 5; matrix products, arithmetic and copies ran while one was open for 0% -> 0% of each run, Pallas kernels for 4% -> 4%
where the time goes in v4:
time: 24.3 us; the launch traced here: 24 us
  starting transfers between devices  13.2 us (54%)
  waiting for transfers between devices  5.97 us (25%)
  Pallas kernels  4.11 us (17%)
  between operations  0.7 us (3%)
    ppermute x8, starting transfers between devices, across(): return lax.ppermute(array, (axis, 'lev'), pairs)  12.3 us
    ppermute x8, waiting for transfers between devices, across(): return lax.ppermute(array, (axis, 'lev'), pairs)  5.28 us
    pallas_call x1, Pallas kernels, shards_by_columns(): local(column_kernel, (values(*atmos_state.shape), values(FIELDS * ROWS, L...  1.42 us
    pallas_call x1, Pallas kernels, shards_by_columns(): local(tables_kernel, (values(4, LETTER, LANES), values(2 * LEVELS * LEVEL...  1.05 us
    ppermute x2, starting transfers between devices, over(): lax.ppermute(array, axis, [(i, i ^ k) for i in range(lax.axis_size(axis))])  0.91 us
    pallas_call x1, Pallas kernels, shards_by_columns(): local(returned_kernel, (values(*atmos_state.shape), values(FIELDS * 2 * R...  0.72 us
    ppermute x2, waiting for transfers between devices, over(): lax.ppermute(array, axis, [(i, i ^ k) for i in range(lax.axis_size(axis))])  0.69 us
    pallas_call x1, Pallas kernels, shards_by_columns(): local(rows_kernel, values(*ocean_state.shape), [pltpu.VMEM] * 4)  0.63 us
  transfers between devices with their start and end apart: 10, of which 5 were waited for; matrix products, arithmetic and copies ran while one was open for 0% of the time, Pallas kernels for 4%

profile of v4, /device:TPU:0, one launch (start us, length us, event | category | flops | bytes accessed | tf_op | source)
XLA Modules:
  0.0 24.0 jit_solution(3382915412017056527)
XLA Ops:
  0.6 1.0 %shard_map.103 = (f32[4,48,128]{2,1,0:T(8,128)S(1)}, f32[128,128]{1,0:T(8,128)S(1)}, f32[80,128]{1,0:T(8,128)S(1)}) custom-call(f32[8,1,512]{2,1,0:T(1,128)} %refs_0_.1, s32[4,1,512]{2,1,0:T(1,128)} %refs_1_.1, f32[4,1,512]{2,1,0:T(1,128)} %refs_2_.1, s32[1,512]{1,0:T(1,128)} %refs_3_.1, f32[4,16,128]{2,1,0:T(8,128)} %refs_4_.1, s32[1,8,256]{2,1,0:T(8,128)} %refs_5_.1, ...), custom_call_target="tpu_custom_call" | custom-call | tf_op jit(solution)/shard_map/pallas_call | solution.py:460
  1.7 4.6 %collective-permute-start.1 = (f32[48,128]{1,0:T(8,128)S(1)}, f32[48,128]{1,0:T(8,128)S(1)}, u32[]{:S(2)}, u32[]{:S(2)}) collective-permute-start(f32[48,128]{1,0:T(8,128)S(1)} %get-tuple-element.29), channel_id=1, source_target_pairs={{0,13},{1,12},{4,9},{5,8},{8,5},{9,4},{12,1},{13,0},{2,15},{3,14},... | collective-permute-start | bytes 73736 | tf_op jit(solution)/shard_map/ppermute | solution.py:429
  6.3 0.0 collective-permute-start.2
  6.3 0.9 %collective-permute-start.3 = (f32[48,128]{1,0:T(8,128)S(1)}, f32[48,128]{1,0:T(8,128)S(1)}, u32[]{:S(2)}, u32[]{:S(2)}) collective-permute-start(f32[48,128]{1,0:T(8,128)S(1)} %get-tuple-element.27), channel_id=1, source_target_pairs={{0,5},{1,4},{4,1},{5,0},{8,13},{9,12},{12,9},{13,8},{2,7},{3,6},{6... | collective-permute-start | bytes 73736 | tf_op jit(solution)/shard_map/ppermute | solution.py:429
  7.2 1.4 %collective-permute-start = (f32[80,128]{1,0:T(8,128)S(1)}, f32[80,128]{1,0:T(8,128)S(1)}, u32[]{:S(2)}, u32[]{:S(2)}) collective-permute-start(f32[80,128]{1,0:T(8,128)S(1)} %get-tuple-element.16.strip_ref), channel_id=1, source_target_pairs={{0,3},{1,2},{2,1},{3,0},{4,7},{5,6},{6,5},{7,4},{8,11},{9,10},{10,... | collective-permute-start | bytes 122888 | tf_op jit(solution)/shard_map/ppermute | solution.py:429
  8.5 0.0 collective-permute-done.1.three_ref
  8.5 2.1 %collective-permute-done.2.two_ref = f32[48,128]{1,0:T(8,128)S(1)} collective-permute-done((f32[48,128]{1,0:T(8,128)S(1)}, f32[48,128]{1,0:T(8,128)S(1)}, u32[]{:S(2)}, u32[]{:S(2)}) %collective-permute-start.2) | collective-permute-done | bytes 24608 | tf_op jit(solution)/shard_map/ppermute | solution.py:429
  10.6 0.0 collective-permute-done.3.one_ref
  10.7 1.6 %collective-permute-start.4 = (f32[120,128]{1,0:T(8,128)S(1)}, f32[120,128]{1,0:T(8,128)S(1)}, u32[]{:S(2)}, u32[]{:S(2)}) collective-permute-start(f32[120,128]{1,0:T(8,128)S(1)} %shard_map.104.own_ref), channel_id=1, source_target_pairs={{0,3},{1,2},{2,1},{3,0},{4,7},{5,6},{6,5},{7,4},{8,11},{9,10},{10,... | collective-permute-start | bytes 184328 | tf_op jit(solution)/shard_map/ppermute | solution.py:429
  12.3 2.1 %collective-permute-done.4.beside_ref = f32[120,128]{1,0:T(8,128)S(1)} collective-permute-done((f32[120,128]{1,0:T(8,128)S(1)}, f32[120,128]{1,0:T(8,128)S(1)}, u32[]{:S(2)}, u32[]{:S(2)}) %collective-permute-start.4) | collective-permute-done | bytes 61472 | tf_op jit(solution)/shard_map/ppermute | solution.py:429
  14.4 0.0 collective-permute-done.strip_beside_ref
  14.5 0.5 %collective-permute-start.5 = (f32[240,128]{1,0:T(8,128)S(1)}, f32[240,128]{1,0:T(8,128)S(1)}, u32[]{:S(2)}, u32[]{:S(2)}) collective-permute-start(f32[240,128]{1,0:T(8,128)S(1)} %slice_dynamic-update-slice_fusion.1), channel_id=1, source_target_pairs={{0,1},{1,0},{2,3},{3,2},{4,5},{5,4},{6,7},{7,6},{8,9},{9,8},{10,11... | collective-permute-start | bytes 368648 | tf_op jit(solution)/shard_map/ppermute | solution.py:424
  14.9 0.3 %shard_map.105 = (f32[8,256]{1,0:T(8,128)S(1)}, f32[4,3,8,128]{3,2,1,0:T(8,128)S(1)}) custom-call(f32[80,128]{1,0:T(8,128)S(1)} %get-tuple-element.16.strip_ref, f32[80,128]{1,0:T(8,128)S(1)} %collective-permute-done.strip_beside_ref, f32[120,128]{1,0:T(8,128)S(1)} %shard_map.104.own_ref, f32[120,128]{1,0:T(8,128)S(1)} %collective-permute-done.4.beside_ref), custom_call_target="tpu_custom_call" | custom-call | tf_op jit(solution)/shard_map/pallas_call | solution.py:473
  15.2 0.7 %collective-permute-done.5.others_ref = f32[240,128]{1,0:T(8,128)S(1)} collective-permute-done((f32[240,128]{1,0:T(8,128)S(1)}, f32[240,128]{1,0:T(8,128)S(1)}, u32[]{:S(2)}, u32[]{:S(2)}) %collective-permute-start.5) | collective-permute-done | bytes 122912 | tf_op jit(solution)/shard_map/ppermute | solution.py:424
  15.9 1.4 %shard_map.106 = (f32[4,16,128]{2,1,0:T(8,128)S(1)}, f32[64,128]{1,0:T(8,128)S(1)}, f32[8,128]{1,0:T(8,128)S(1)}, f32[8,128]{1,0:T(8,128)S(1)}, f32[8,128]{1,0:T(8,128)S(1)}) custom-call(f32[128,128]{1,0:T(8,128)S(1)} %get-tuple-element.15.factors_ref, f32[80,128]{1,0:T(8,128)S(1)} %get-tuple-element.16.strip_ref, ...), custom_call_target="tpu_custom_call" | custom-call | tf_op jit(solution)/shard_map/pallas_call | solution.py:479
  17.3 0.4 %collective-permute-start.6 = (f32[64,128]{1,0:T(8,128)S(1)}, f32[64,128]{1,0:T(8,128)S(1)}, u32[]{:S(2)}, u32[]{:S(2)}) collective-permute-start(f32[64,128]{1,0:T(8,128)S(1)} %get-tuple-element.21), channel_id=1, source_target_pairs={{0,1},{1,0},{2,3},{3,2},{4,5},{5,4},{6,7},{7,6},{8,9},{9,8},{10,11... | collective-permute-start | bytes 98312 | tf_op jit(solution)/shard_map/ppermute | solution.py:424
  17.8 1.7 %collective-permute-start.7 = (f32[8,128]{1,0:T(8,128)S(1)}, f32[8,128]{1,0:T(8,128)S(1)}, u32[]{:S(2)}, u32[]{:S(2)}) collective-permute-start(f32[8,128]{1,0:T(8,128)S(1)} %get-tuple-element.23), channel_id=1, source_target_pairs={{0,13},{1,12},{4,9},{5,8},{8,5},{9,4},{12,1},{13,0},{2,15},{3,14},... | collective-permute-start | bytes 12296 | tf_op jit(solution)/shard_map/ppermute | solution.py:429
  19.5 0.6 %collective-permute-start.8 = (f32[8,128]{1,0:T(8,128)S(1)}, f32[8,128]{1,0:T(8,128)S(1)}, u32[]{:S(2)}, u32[]{:S(2)}) collective-permute-start(f32[8,128]{1,0:T(8,128)S(1)} %get-tuple-element.24), channel_id=1, source_target_pairs={{0,9},{1,8},{4,13},{5,12},{8,1},{9,0},{12,5},{13,4},{2,11},{3,10},... | collective-permute-start | bytes 12296 | tf_op jit(solution)/shard_map/ppermute | solution.py:429
  20.1 1.6 %collective-permute-start.9 = (f32[8,128]{1,0:T(8,128)S(1)}, f32[8,128]{1,0:T(8,128)S(1)}, u32[]{:S(2)}, u32[]{:S(2)}) collective-permute-start(f32[8,128]{1,0:T(8,128)S(1)} %get-tuple-element.25), channel_id=1, source_target_pairs={{0,5},{1,4},{4,1},{5,0},{8,13},{9,12},{12,9},{13,8},{2,7},{3,6},{6... | collective-permute-start | bytes 12296 | tf_op jit(solution)/shard_map/ppermute | solution.py:429
  21.6 0.0 collective-permute-done.6.final_ref
  21.6 0.7 %shard_map.107 = (f32[4,16,128]{2,1,0:T(8,128)}, f32[128,128]{1,0:T(8,128)}) custom-call(f32[4,16,128]{2,1,0:T(8,128)S(1)} %get-tuple-element.20.atmos_ref, f32[64,128]{1,0:T(8,128)S(1)} %collective-permute-done.6.final_ref, f32[4,3,8,128]{3,2,1,0:T(8,128)S(1)} %get-tuple-element.19.named_ref), custom_call_target="tpu_custom_call" | custom-call | tf_op jit(solution)/shard_map/pallas_call | solution.py:492
  22.4 0.2 collective-permute-done.7.three_ref
  22.6 0.8 %collective-permute-done.8.two_ref = f32[8,128]{1,0:T(8,128)S(1)} collective-permute-done((f32[8,128]{1,0:T(8,128)S(1)}, f32[8,128]{1,0:T(8,128)S(1)}, u32[]{:S(2)}, u32[]{:S(2)}) %collective-permute-start.8) | collective-permute-done | bytes 4128 | tf_op jit(solution)/shard_map/ppermute | solution.py:429
  23.4 0.0 collective-permute-done.9.one_ref
  23.4 0.6 %shard_map.108 = f32[8,1,512]{2,1,0:T(1,128)} custom-call(f32[8,128]{1,0:T(8,128)S(1)} %collective-permute-done.7.three_ref, f32[8,128]{1,0:T(8,128)S(1)} %collective-permute-done.8.two_ref, f32[8,128]{1,0:T(8,128)S(1)} %collective-permute-done.9.one_ref, f32[64,128]{1,0:T(8,128)S(1)} %collective-permute-done.6.final_ref), custom_call_target="tpu_custom_call" | custom-call | tf_op jit(solution)/shard_map/pallas_call | solution.py:497
  (7 shorter events, 0.0 us)
Async XLA Ops:
  1.7 6.8 %collective-permute-start.1 = (f32[48,128]{1,0:T(8,128)S(1)}, f32[48,128]{1,0:T(8,128)S(1)}, u32[]{:S(2)}, u32[]{:S(2)}) collective-permute-start(f32[48,128]{1,0:T(8,128)S(1)} %get-tuple-element.29), channel_id=1, source_target_pairs={{0,13},{1,12},{4,9},{5,8},{8,5},{9,4},{12,1},{13,0},{2,15},{3,14},... | collective-permute-start | bytes 73736 | tf_op jit(solution)/shard_map/ppermute | solution.py:429
  6.3 4.4 %collective-permute-start.2 = (f32[48,128]{1,0:T(8,128)S(1)}, f32[48,128]{1,0:T(8,128)S(1)}, u32[]{:S(2)}, u32[]{:S(2)}) collective-permute-start(f32[48,128]{1,0:T(8,128)S(1)} %get-tuple-element.28), channel_id=1, source_target_pairs={{0,9},{1,8},{4,13},{5,12},{8,1},{9,0},{12,5},{13,4},{2,11},{3,10},... | collective-permute-start | bytes 73736 | tf_op jit(solution)/shard_map/ppermute | solution.py:429
  6.3 4.4 %collective-permute-start.3 = (f32[48,128]{1,0:T(8,128)S(1)}, f32[48,128]{1,0:T(8,128)S(1)}, u32[]{:S(2)}, u32[]{:S(2)}) collective-permute-start(f32[48,128]{1,0:T(8,128)S(1)} %get-tuple-element.27), channel_id=1, source_target_pairs={{0,5},{1,4},{4,1},{5,0},{8,13},{9,12},{12,9},{13,8},{2,7},{3,6},{6... | collective-permute-start | bytes 73736 | tf_op jit(solution)/shard_map/ppermute | solution.py:429
  7.2 7.3 %collective-permute-start = (f32[80,128]{1,0:T(8,128)S(1)}, f32[80,128]{1,0:T(8,128)S(1)}, u32[]{:S(2)}, u32[]{:S(2)}) collective-permute-start(f32[80,128]{1,0:T(8,128)S(1)} %get-tuple-element.16.strip_ref), channel_id=1, source_target_pairs={{0,3},{1,2},{2,1},{3,0},{4,7},{5,6},{6,5},{7,4},{8,11},{9,10},{10,... | collective-permute-start | bytes 122888 | tf_op jit(solution)/shard_map/ppermute | solution.py:429
  10.7 3.8 %collective-permute-start.4 = (f32[120,128]{1,0:T(8,128)S(1)}, f32[120,128]{1,0:T(8,128)S(1)}, u32[]{:S(2)}, u32[]{:S(2)}) collective-permute-start(f32[120,128]{1,0:T(8,128)S(1)} %shard_map.104.own_ref), channel_id=1, source_target_pairs={{0,3},{1,2},{2,1},{3,0},{4,7},{5,6},{6,5},{7,4},{8,11},{9,10},{10,... | collective-permute-start | bytes 184328 | tf_op jit(solution)/shard_map/ppermute | solution.py:429
  14.5 1.5 %collective-permute-start.5 = (f32[240,128]{1,0:T(8,128)S(1)}, f32[240,128]{1,0:T(8,128)S(1)}, u32[]{:S(2)}, u32[]{:S(2)}) collective-permute-start(f32[240,128]{1,0:T(8,128)S(1)} %slice_dynamic-update-slice_fusion.1), channel_id=1, source_target_pairs={{0,1},{1,0},{2,3},{3,2},{4,5},{5,4},{6,7},{7,6},{8,9},{9,8},{10,11... | collective-permute-start | bytes 368648 | tf_op jit(solution)/shard_map/ppermute | solution.py:424
  17.3 4.3 %collective-permute-start.6 = (f32[64,128]{1,0:T(8,128)S(1)}, f32[64,128]{1,0:T(8,128)S(1)}, u32[]{:S(2)}, u32[]{:S(2)}) collective-permute-start(f32[64,128]{1,0:T(8,128)S(1)} %get-tuple-element.21), channel_id=1, source_target_pairs={{0,1},{1,0},{2,3},{3,2},{4,5},{5,4},{6,7},{7,6},{8,9},{9,8},{10,11... | collective-permute-start | bytes 98312 | tf_op jit(solution)/shard_map/ppermute | solution.py:424
  17.8 4.8 %collective-permute-start.7 = (f32[8,128]{1,0:T(8,128)S(1)}, f32[8,128]{1,0:T(8,128)S(1)}, u32[]{:S(2)}, u32[]{:S(2)}) collective-permute-start(f32[8,128]{1,0:T(8,128)S(1)} %get-tuple-element.23), channel_id=1, source_target_pairs={{0,13},{1,12},{4,9},{5,8},{8,5},{9,4},{12,1},{13,0},{2,15},{3,14},... | collective-permute-start | bytes 12296 | tf_op jit(solution)/shard_map/ppermute | solution.py:429
  19.5 3.9 %collective-permute-start.8 = (f32[8,128]{1,0:T(8,128)S(1)}, f32[8,128]{1,0:T(8,128)S(1)}, u32[]{:S(2)}, u32[]{:S(2)}) collective-permute-start(f32[8,128]{1,0:T(8,128)S(1)} %get-tuple-element.24), channel_id=1, source_target_pairs={{0,9},{1,8},{4,13},{5,12},{8,1},{9,0},{12,5},{13,4},{2,11},{3,10},... | collective-permute-start | bytes 12296 | tf_op jit(solution)/shard_map/ppermute | solution.py:429
  20.1 3.3 %collective-permute-start.9 = (f32[8,128]{1,0:T(8,128)S(1)}, f32[8,128]{1,0:T(8,128)S(1)}, u32[]{:S(2)}, u32[]{:S(2)}) collective-permute-start(f32[8,128]{1,0:T(8,128)S(1)} %get-tuple-element.25), channel_id=1, source_target_pairs={{0,5},{1,4},{4,1},{5,0},{8,13},{9,12},{12,9},{13,8},{2,7},{3,6},{6... | collective-permute-start | bytes 12296 | tf_op jit(solution)/shard_map/ppermute | solution.py:429

commit v5 on v4

--- a/solution.py
+++ b/solution.py
@@ -162,6 +162,19 @@
     return lax.axis_index("space"), lax.axis_index("comp"), lax.axis_index("lev")
 
 
+FIRST = (1, 3, 0, 2)
+SECOND = (3, 2, 1, 0)
+LAST = (2, 0, 3, 1)
+
+
+def at_end(space):
+    return (space == 0) | (space == 3)
+
+
+def letter_of(k, space):
+    return jnp.where((k == 1) | (k == 2), jnp.where(at_end(space), k, 3 - k), k)
+
+
 def tables_kernel(*refs):
     arrays, (letters_ref, factors_ref, strip_ref), held, arrived = refs[:8], refs[8:11], refs[11:-1], refs[-1]
     copies = [pltpu.make_async_copy(a, h, arrived.at[i]) for i, (a, h) in enumerate(zip(arrays, held))]
@@ -200,7 +213,7 @@
     edge = jnp.where(comp == 0, to_left, to_right)
     requests = request_ref[0].astype(jnp.float32)
     for z in range(4):
-        k = z ^ space
+        k = letter_of(z ^ space, space)
         letters_ref[k, :8, :] = ocean[z]
         letters_ref[k, 8:16, :] = table[z]
         last = jnp.where(row == 0, packed(halo(ocean, z)), 0.0)
@@ -224,12 +237,16 @@
     strip_ref[AT_REQUEST + 8 :, :] = requests[:, LANES:]
 
 
-def sheet_kernel(own_ref, three_ref, two_ref, one_ref, sheet_ref):
+def sheet_kernel(own_ref, first_ref, second_ref, last_ref, sheet_ref):
     space, comp, lev = place()
-    for k, ref in enumerate((own_ref, one_ref, two_ref, three_ref)):
-        sheet_ref[TABLE * k : TABLE * (k + 1), :] = ref[:TABLE, :]
+    end = at_end(space)
+    sheet_ref[:TABLE, :] = own_ref[:TABLE, :]
+    sheet_ref[pl.ds(jnp.where(end, 2, 1) * TABLE, TABLE), :] = first_ref[:TABLE, :]
+    sheet_ref[pl.ds(jnp.where(end, 1, 2) * TABLE, TABLE), :] = last_ref[:TABLE, :]
+    sheet_ref[3 * TABLE : 4 * TABLE, :] = second_ref[:TABLE, :]
     near = (space + comp) % 2 == 0
-    sheet_ref[AT_HALO:, :] = jnp.where(near, one_ref[AT_EDGE:, :], three_ref[AT_EDGE:, :])
+    one = jnp.where(end, last_ref[AT_EDGE:, :], first_ref[AT_EDGE:, :])
+    sheet_ref[AT_HALO:, :] = jnp.where(near, one, second_ref[AT_EDGE:, :])
 
 
 def margins_kernel(strip_ref, strip_beside_ref, own_ref, beside_ref, wet_ref, named_ref, rows_ref):
@@ -424,8 +441,8 @@
     return lax.ppermute(array, axis, [(i, i ^ k) for i in range(lax.axis_size(axis))])
 
 
-def across(axis, k, array):
-    pairs = [(2 * i + core, 2 * (i ^ k) + 1 - core) for i in range(lax.axis_size(axis)) for core in range(2)]
+def across(axis, targets, array):
+    pairs = [(2 * i + core, 2 * target + 1 - core) for i, target in enumerate(targets) for core in range(2)]
     return lax.ppermute(array, (axis, "lev"), pairs)
 
 
@@ -463,10 +480,10 @@
         [pltpu.HBM] * 8,
         [pltpu.VMEM(a.shape, a.dtype) for a in arrays] + [pltpu.SemaphoreType.DMA((8,))],
     )(*(pltpu.with_memory_space_constraint(a, pltpu.HBM) for a in arrays))
-    one, two, three = (across("space", k, letters[k]) for k in (1, 2, 3))
-    strip_beside = across("comp", 1, strip)
-    sheet = local(sheet_kernel, values(SHEET, LANES), [pltpu.VMEM] * 4)(letters[0], three, two, one)
-    sheet_beside = across("comp", 1, sheet)
+    first, second, last = (across("space", turns, letters[at]) for at, turns in ((1, FIRST), (3, SECOND), (2, LAST)))
+    strip_beside = across("comp", (1, 0), strip)
+    sheet = local(sheet_kernel, values(SHEET, LANES), [pltpu.VMEM] * 4)(letters[0], first, second, last)
+    sheet_beside = across("comp", (1, 0), sheet)
     swapped = (sheet[:TABLE], sheet[AT_HALO:AT_HALO_ASKED], sheet_beside[TABLE:AT_HALO_ASKED])
     swapped += (strip[:AT_REQUEST], strip_beside[:AT_REQUEST])
     others = over("lev", 1, jnp.concatenate(swapped, 0))
@@ -487,7 +504,7 @@
             pltpu.VMEM((ROWS * FIELDS, LANES), jnp.float32),
         ],
     )(factors, strip, strip_beside, sheet, sheet_beside, others, wet, named)
-    one, two, three = (across("space", k, piece) for k, piece in zip((1, 2, 3), back))
+    one, two, three = (across("space", [z ^ k for z in range(4)], piece) for k, piece in zip((1, 2, 3), back))
     final = over("lev", 1, final)
     atmos_next, returned = local(
         returned_kernel,

time: 24.3 us -> 24.1 us (level)
  waiting for transfers between devices: 5.97 us -> 5.18 us
  starting transfers between devices: 13.2 us -> 13.8 us
    ppermute x8, starting transfers between devices: 12.3 us -> 13.4 us  [across(): return lax.ppermute(array, (axis, 'lev'), pairs)]
    ppermute x8, waiting for transfers between devices: 5.28 us -> 4.24 us  [across(): return lax.ppermute(array, (axis, 'lev'), pairs)]
    ppermute x2, starting transfers between devices: 0.91 us -> 0.4 us  [over(): lax.ppermute(array, axis, [(i, i ^ k) for i in range(lax.axis_size(axis))])]
    ppermute x2, waiting for transfers between devices: 0.69 us -> 0.94 us  [over(): lax.ppermute(array, axis, [(i, i ^ k) for i in range(lax.axis_size(axis))])]
where the time goes in v5:
time: 24.1 us; the launch traced here: 23.8 us
  starting transfers between devices  13.8 us (57%)
  waiting for transfers between devices  5.18 us (21%)
  Pallas kernels  4.11 us (17%)
  between operations  0.69 us (3%)
    ppermute x8, starting transfers between devices, across(): return lax.ppermute(array, (axis, 'lev'), pairs)  13.4 us
    ppermute x8, waiting for transfers between devices, across(): return lax.ppermute(array, (axis, 'lev'), pairs)  4.24 us
    pallas_call x1, Pallas kernels, shards_by_columns(): local(column_kernel, (values(*atmos_state.shape), values(FIELDS * ROWS, L...  1.42 us
    pallas_call x1, Pallas kernels, shards_by_columns(): local(tables_kernel, (values(4, LETTER, LANES), values(2 * LEVELS * LEVEL...  1.05 us
    ppermute x2, waiting for transfers between devices, over(): lax.ppermute(array, axis, [(i, i ^ k) for i in range(lax.axis_size(axis))])  0.94 us
    pallas_call x1, Pallas kernels, shards_by_columns(): local(returned_kernel, (values(*atmos_state.shape), values(FIELDS * 2 * R...  0.72 us
    pallas_call x1, Pallas kernels, shards_by_columns(): local(rows_kernel, values(*ocean_state.shape), [pltpu.VMEM] * 4)  0.63 us
  transfers between devices with their start and end apart: 10, of which 5 were waited for; matrix products, arithmetic and copies ran while one was open for 0% of the time, Pallas kernels for 4%

profile of v5, /device:TPU:0, one launch (start us, length us, event | category | flops | bytes accessed | tf_op | source)
XLA Modules:
  0.0 23.8 jit_solution(15519409262617438528)
XLA Ops:
  0.6 1.0 %shard_map.103 = (f32[4,48,128]{2,1,0:T(8,128)S(1)}, f32[128,128]{1,0:T(8,128)S(1)}, f32[80,128]{1,0:T(8,128)S(1)}) custom-call(f32[8,1,512]{2,1,0:T(1,128)} %refs_0_.1, s32[4,1,512]{2,1,0:T(1,128)} %refs_1_.1, f32[4,1,512]{2,1,0:T(1,128)} %refs_2_.1, s32[1,512]{1,0:T(1,128)} %refs_3_.1, f32[4,16,128]{2,1,0:T(8,128)} %refs_4_.1, s32[1,8,256]{2,1,0:T(8,128)} %refs_5_.1, ...), custom_call_target="tpu_custom_call" | custom-call | tf_op jit(solution)/shard_map/pallas_call | solution.py:477
  1.7 2.5 %collective-permute-start.1 = (f32[48,128]{1,0:T(8,128)S(1)}, f32[48,128]{1,0:T(8,128)S(1)}, u32[]{:S(2)}, u32[]{:S(2)}) collective-permute-start(f32[48,128]{1,0:T(8,128)S(1)} %get-tuple-element.29), channel_id=1, source_target_pairs={{0,5},{1,4},{4,13},{5,12},{8,1},{9,0},{12,9},{13,8},{2,7},{3,6},{6... | collective-permute-start | bytes 73736 | tf_op jit(solution)/shard_map/ppermute | solution.py:446
  4.2 2.8 %collective-permute-start.2 = (f32[48,128]{1,0:T(8,128)S(1)}, f32[48,128]{1,0:T(8,128)S(1)}, u32[]{:S(2)}, u32[]{:S(2)}) collective-permute-start(f32[48,128]{1,0:T(8,128)S(1)} %get-tuple-element.28), channel_id=1, source_target_pairs={{0,13},{1,12},{4,9},{5,8},{8,5},{9,4},{12,1},{13,0},{2,15},{3,14},... | collective-permute-start | bytes 73736 | tf_op jit(solution)/shard_map/ppermute | solution.py:446
  7.0 1.0 %collective-permute-start.3 = (f32[48,128]{1,0:T(8,128)S(1)}, f32[48,128]{1,0:T(8,128)S(1)}, u32[]{:S(2)}, u32[]{:S(2)}) collective-permute-start(f32[48,128]{1,0:T(8,128)S(1)} %get-tuple-element.27), channel_id=1, source_target_pairs={{0,9},{1,8},{4,1},{5,0},{8,13},{9,12},{12,5},{13,4},{2,11},{3,10},... | collective-permute-start | bytes 73736 | tf_op jit(solution)/shard_map/ppermute | solution.py:446
  8.0 1.8 %collective-permute-start = (f32[80,128]{1,0:T(8,128)S(1)}, f32[80,128]{1,0:T(8,128)S(1)}, u32[]{:S(2)}, u32[]{:S(2)}) collective-permute-start(f32[80,128]{1,0:T(8,128)S(1)} %get-tuple-element.16.strip_ref), channel_id=1, source_target_pairs={{0,3},{1,2},{2,1},{3,0},{4,7},{5,6},{6,5},{7,4},{8,11},{9,10},{10,... | collective-permute-start | bytes 122888 | tf_op jit(solution)/shard_map/ppermute | solution.py:446
  9.8 0.0 collective-permute-done.1.first_ref
  9.8 0.0 collective-permute-done.2.second_ref
  9.8 0.8 %collective-permute-done.3.last_ref = f32[48,128]{1,0:T(8,128)S(1)} collective-permute-done((f32[48,128]{1,0:T(8,128)S(1)}, f32[48,128]{1,0:T(8,128)S(1)}, u32[]{:S(2)}, u32[]{:S(2)}) %collective-permute-start.3) | collective-permute-done | bytes 24608 | tf_op jit(solution)/shard_map/ppermute | solution.py:446
  10.6 1.3 %collective-permute-start.4 = (f32[120,128]{1,0:T(8,128)S(1)}, f32[120,128]{1,0:T(8,128)S(1)}, u32[]{:S(2)}, u32[]{:S(2)}) collective-permute-start(f32[120,128]{1,0:T(8,128)S(1)} %shard_map.104.own_ref), channel_id=1, source_target_pairs={{0,3},{1,2},{2,1},{3,0},{4,7},{5,6},{6,5},{7,4},{8,11},{9,10},{10,... | collective-permute-start | bytes 184328 | tf_op jit(solution)/shard_map/ppermute | solution.py:446
  11.9 2.8 %collective-permute-done.4.beside_ref = f32[120,128]{1,0:T(8,128)S(1)} collective-permute-done((f32[120,128]{1,0:T(8,128)S(1)}, f32[120,128]{1,0:T(8,128)S(1)}, u32[]{:S(2)}, u32[]{:S(2)}) %collective-permute-start.4) | collective-permute-done | bytes 61472 | tf_op jit(solution)/shard_map/ppermute | solution.py:446
  14.7 0.0 collective-permute-done.strip_beside_ref
  14.7 0.2 collective-permute-start.5
  14.9 0.3 %shard_map.105 = (f32[8,256]{1,0:T(8,128)S(1)}, f32[4,3,8,128]{3,2,1,0:T(8,128)S(1)}) custom-call(f32[80,128]{1,0:T(8,128)S(1)} %get-tuple-element.16.strip_ref, f32[80,128]{1,0:T(8,128)S(1)} %collective-permute-done.strip_beside_ref, f32[120,128]{1,0:T(8,128)S(1)} %shard_map.104.own_ref, f32[120,128]{1,0:T(8,128)S(1)} %collective-permute-done.4.beside_ref), custom_call_target="tpu_custom_call" | custom-call | tf_op jit(solution)/shard_map/pallas_call | solution.py:490
  15.2 0.9 %collective-permute-done.5.others_ref = f32[240,128]{1,0:T(8,128)S(1)} collective-permute-done((f32[240,128]{1,0:T(8,128)S(1)}, f32[240,128]{1,0:T(8,128)S(1)}, u32[]{:S(2)}, u32[]{:S(2)}) %collective-permute-start.5) | collective-permute-done | bytes 122912 | tf_op jit(solution)/shard_map/ppermute | solution.py:441
  16.1 1.4 %shard_map.106 = (f32[4,16,128]{2,1,0:T(8,128)S(1)}, f32[64,128]{1,0:T(8,128)S(1)}, f32[8,128]{1,0:T(8,128)S(1)}, f32[8,128]{1,0:T(8,128)S(1)}, f32[8,128]{1,0:T(8,128)S(1)}) custom-call(f32[128,128]{1,0:T(8,128)S(1)} %get-tuple-element.15.factors_ref, f32[80,128]{1,0:T(8,128)S(1)} %get-tuple-element.16.strip_ref, ...), custom_call_target="tpu_custom_call" | custom-call | tf_op jit(solution)/shard_map/pallas_call | solution.py:496
  17.6 0.2 collective-permute-start.6
  17.8 1.3 %collective-permute-start.7 = (f32[8,128]{1,0:T(8,128)S(1)}, f32[8,128]{1,0:T(8,128)S(1)}, u32[]{:S(2)}, u32[]{:S(2)}) collective-permute-start(f32[8,128]{1,0:T(8,128)S(1)} %get-tuple-element.23), channel_id=1, source_target_pairs={{0,13},{1,12},{4,9},{5,8},{8,5},{9,4},{12,1},{13,0},{2,15},{3,14},... | collective-permute-start | bytes 12296 | tf_op jit(solution)/shard_map/ppermute | solution.py:446
  19.0 1.0 %collective-permute-start.8 = (f32[8,128]{1,0:T(8,128)S(1)}, f32[8,128]{1,0:T(8,128)S(1)}, u32[]{:S(2)}, u32[]{:S(2)}) collective-permute-start(f32[8,128]{1,0:T(8,128)S(1)} %get-tuple-element.24), channel_id=1, source_target_pairs={{0,9},{1,8},{4,13},{5,12},{8,1},{9,0},{12,5},{13,4},{2,11},{3,10},... | collective-permute-start | bytes 12296 | tf_op jit(solution)/shard_map/ppermute | solution.py:446
  20.1 1.8 %collective-permute-start.9 = (f32[8,128]{1,0:T(8,128)S(1)}, f32[8,128]{1,0:T(8,128)S(1)}, u32[]{:S(2)}, u32[]{:S(2)}) collective-permute-start(f32[8,128]{1,0:T(8,128)S(1)} %get-tuple-element.25), channel_id=1, source_target_pairs={{0,5},{1,4},{4,1},{5,0},{8,13},{9,12},{12,9},{13,8},{2,7},{3,6},{6... | collective-permute-start | bytes 12296 | tf_op jit(solution)/shard_map/ppermute | solution.py:446
  21.9 0.0 collective-permute-done.6.final_ref
  21.9 0.7 %shard_map.107 = (f32[4,16,128]{2,1,0:T(8,128)}, f32[128,128]{1,0:T(8,128)}) custom-call(f32[4,16,128]{2,1,0:T(8,128)S(1)} %get-tuple-element.20.atmos_ref, f32[64,128]{1,0:T(8,128)S(1)} %collective-permute-done.6.final_ref, f32[4,3,8,128]{3,2,1,0:T(8,128)S(1)} %get-tuple-element.19.named_ref), custom_call_target="tpu_custom_call" | custom-call | tf_op jit(solution)/shard_map/pallas_call | solution.py:509
  22.6 0.0 collective-permute-done.7.three_ref
  22.6 0.3 %collective-permute-done.8.two_ref = f32[8,128]{1,0:T(8,128)S(1)} collective-permute-done((f32[8,128]{1,0:T(8,128)S(1)}, f32[8,128]{1,0:T(8,128)S(1)}, u32[]{:S(2)}, u32[]{:S(2)}) %collective-permute-start.8) | collective-permute-done | bytes 4128 | tf_op jit(solution)/shard_map/ppermute | solution.py:446
  23.0 0.2 collective-permute-done.9.one_ref
  23.2 0.6 %shard_map.108 = f32[8,1,512]{2,1,0:T(1,128)} custom-call(f32[8,128]{1,0:T(8,128)S(1)} %collective-permute-done.7.three_ref, f32[8,128]{1,0:T(8,128)S(1)} %collective-permute-done.8.two_ref, f32[8,128]{1,0:T(8,128)S(1)} %collective-permute-done.9.one_ref, f32[64,128]{1,0:T(8,128)S(1)} %collective-permute-done.6.final_ref), custom_call_target="tpu_custom_call" | custom-call | tf_op jit(solution)/shard_map/pallas_call | solution.py:514
  (7 shorter events, 0.0 us)
Async XLA Ops:
  1.7 8.1 %collective-permute-start.1 = (f32[48,128]{1,0:T(8,128)S(1)}, f32[48,128]{1,0:T(8,128)S(1)}, u32[]{:S(2)}, u32[]{:S(2)}) collective-permute-start(f32[48,128]{1,0:T(8,128)S(1)} %get-tuple-element.29), channel_id=1, source_target_pairs={{0,5},{1,4},{4,13},{5,12},{8,1},{9,0},{12,9},{13,8},{2,7},{3,6},{6... | collective-permute-start | bytes 73736 | tf_op jit(solution)/shard_map/ppermute | solution.py:446
  4.2 5.5 %collective-permute-start.2 = (f32[48,128]{1,0:T(8,128)S(1)}, f32[48,128]{1,0:T(8,128)S(1)}, u32[]{:S(2)}, u32[]{:S(2)}) collective-permute-start(f32[48,128]{1,0:T(8,128)S(1)} %get-tuple-element.28), channel_id=1, source_target_pairs={{0,13},{1,12},{4,9},{5,8},{8,5},{9,4},{12,1},{13,0},{2,15},{3,14},... | collective-permute-start | bytes 73736 | tf_op jit(solution)/shard_map/ppermute | solution.py:446
  7.0 3.6 %collective-permute-start.3 = (f32[48,128]{1,0:T(8,128)S(1)}, f32[48,128]{1,0:T(8,128)S(1)}, u32[]{:S(2)}, u32[]{:S(2)}) collective-permute-start(f32[48,128]{1,0:T(8,128)S(1)} %get-tuple-element.27), channel_id=1, source_target_pairs={{0,9},{1,8},{4,1},{5,0},{8,13},{9,12},{12,5},{13,4},{2,11},{3,10},... | collective-permute-start | bytes 73736 | tf_op jit(solution)/shard_map/ppermute | solution.py:446
  8.0 6.7 %collective-permute-start = (f32[80,128]{1,0:T(8,128)S(1)}, f32[80,128]{1,0:T(8,128)S(1)}, u32[]{:S(2)}, u32[]{:S(2)}) collective-permute-start(f32[80,128]{1,0:T(8,128)S(1)} %get-tuple-element.16.strip_ref), channel_id=1, source_target_pairs={{0,3},{1,2},{2,1},{3,0},{4,7},{5,6},{6,5},{7,4},{8,11},{9,10},{10,... | collective-permute-start | bytes 122888 | tf_op jit(solution)/shard_map/ppermute | solution.py:446
  10.6 4.1 %collective-permute-start.4 = (f32[120,128]{1,0:T(8,128)S(1)}, f32[120,128]{1,0:T(8,128)S(1)}, u32[]{:S(2)}, u32[]{:S(2)}) collective-permute-start(f32[120,128]{1,0:T(8,128)S(1)} %shard_map.104.own_ref), channel_id=1, source_target_pairs={{0,3},{1,2},{2,1},{3,0},{4,7},{5,6},{6,5},{7,4},{8,11},{9,10},{10,... | collective-permute-start | bytes 184328 | tf_op jit(solution)/shard_map/ppermute | solution.py:446
  14.7 1.4 %collective-permute-start.5 = (f32[240,128]{1,0:T(8,128)S(1)}, f32[240,128]{1,0:T(8,128)S(1)}, u32[]{:S(2)}, u32[]{:S(2)}) collective-permute-start(f32[240,128]{1,0:T(8,128)S(1)} %slice_dynamic-update-slice_fusion.1), channel_id=1, source_target_pairs={{0,1},{1,0},{2,3},{3,2},{4,5},{5,4},{6,7},{7,6},{8,9},{9,8},{10,11... | collective-permute-start | bytes 368648 | tf_op jit(solution)/shard_map/ppermute | solution.py:441
  17.6 4.3 %collective-permute-start.6 = (f32[64,128]{1,0:T(8,128)S(1)}, f32[64,128]{1,0:T(8,128)S(1)}, u32[]{:S(2)}, u32[]{:S(2)}) collective-permute-start(f32[64,128]{1,0:T(8,128)S(1)} %get-tuple-element.21), channel_id=1, source_target_pairs={{0,1},{1,0},{2,3},{3,2},{4,5},{5,4},{6,7},{7,6},{8,9},{9,8},{10,11... | collective-permute-start | bytes 98312 | tf_op jit(solution)/shard_map/ppermute | solution.py:441
  17.8 4.8 %collective-permute-start.7 = (f32[8,128]{1,0:T(8,128)S(1)}, f32[8,128]{1,0:T(8,128)S(1)}, u32[]{:S(2)}, u32[]{:S(2)}) collective-permute-start(f32[8,128]{1,0:T(8,128)S(1)} %get-tuple-element.23), channel_id=1, source_target_pairs={{0,13},{1,12},{4,9},{5,8},{8,5},{9,4},{12,1},{13,0},{2,15},{3,14},... | collective-permute-start | bytes 12296 | tf_op jit(solution)/shard_map/ppermute | solution.py:446
  19.0 3.9 %collective-permute-start.8 = (f32[8,128]{1,0:T(8,128)S(1)}, f32[8,128]{1,0:T(8,128)S(1)}, u32[]{:S(2)}, u32[]{:S(2)}) collective-permute-start(f32[8,128]{1,0:T(8,128)S(1)} %get-tuple-element.24), channel_id=1, source_target_pairs={{0,9},{1,8},{4,13},{5,12},{8,1},{9,0},{12,5},{13,4},{2,11},{3,10},... | collective-permute-start | bytes 12296 | tf_op jit(solution)/shard_map/ppermute | solution.py:446
  20.1 3.1 %collective-permute-start.9 = (f32[8,128]{1,0:T(8,128)S(1)}, f32[8,128]{1,0:T(8,128)S(1)}, u32[]{:S(2)}, u32[]{:S(2)}) collective-permute-start(f32[8,128]{1,0:T(8,128)S(1)} %get-tuple-element.25), channel_id=1, source_target_pairs={{0,5},{1,4},{4,1},{5,0},{8,13},{9,12},{12,9},{13,8},{2,7},{3,6},{6... | collective-permute-start | bytes 12296 | tf_op jit(solution)/shard_map/ppermute | solution.py:446

commit v6 on v5

--- a/solution.py
+++ b/solution.py
@@ -117,16 +117,14 @@
 AT_EDGE = TABLE
 AT_ASKED = AT_EDGE + 8
 LETTER = AT_ASKED + 16
-AT_REQUEST = 64
+AT_LEVELS = TABLE
+AT_REQUEST = AT_LEVELS + 64
 STRIP = AT_REQUEST + 16
-AT_HALO = 4 * TABLE
+AT_HALO = 3 * TABLE
 AT_HALO_ASKED = AT_HALO + 8
-SHEET = AT_HALO_ASKED + 16
-OTHER_HALO = TABLE
-BESIDE_BLOCKS = OTHER_HALO + 8
-BESIDE_HALO = BESIDE_BLOCKS + 3 * TABLE
-OTHER_LEVELS = BESIDE_HALO + 8
-BESIDE_LEVELS = OTHER_LEVELS + 64
+AT_MORE_LEVELS = AT_HALO_ASKED + 16
+SHEET = AT_MORE_LEVELS + 64
+OTHER_HALO = AT_REQUEST
 EDGE = 16
 WIDE = 32
 VMEM_LIMIT = 4 * 1024 * 1024
@@ -232,30 +230,36 @@
         at = LEVELS * (LEVELS + field)
         factors_ref[at : at + LEVELS, :] = jnp.broadcast_to(jnp.where(lev == 0, other[1], other[0]), (ROWS, LANES))
     for level in range(LEVELS // 2):
-        strip_ref[2 * ROWS * level : 2 * ROWS * (level + 1), :] = atmos_ref[level]
+        strip_ref[AT_LEVELS + 2 * ROWS * level : AT_LEVELS + 2 * ROWS * (level + 1), :] = atmos_ref[level]
+    strip_ref[:TABLE, :] = letters_ref[0, :TABLE, :]
     strip_ref[AT_REQUEST : AT_REQUEST + 8, :] = requests[:, :LANES]
     strip_ref[AT_REQUEST + 8 :, :] = requests[:, LANES:]
 
 
-def sheet_kernel(own_ref, first_ref, second_ref, last_ref, sheet_ref):
+def sheet_kernel(strip_ref, last_ref, second_ref, first_ref, sheet_ref):
     space, comp, lev = place()
     end = at_end(space)
-    sheet_ref[:TABLE, :] = own_ref[:TABLE, :]
-    sheet_ref[pl.ds(jnp.where(end, 2, 1) * TABLE, TABLE), :] = first_ref[:TABLE, :]
-    sheet_ref[pl.ds(jnp.where(end, 1, 2) * TABLE, TABLE), :] = last_ref[:TABLE, :]
-    sheet_ref[3 * TABLE : 4 * TABLE, :] = second_ref[:TABLE, :]
+    sheet_ref[pl.ds(jnp.where(end, 1, 0) * TABLE, TABLE), :] = first_ref[:TABLE, :]
+    sheet_ref[pl.ds(jnp.where(end, 0, 1) * TABLE, TABLE), :] = last_ref[:TABLE, :]
+    sheet_ref[2 * TABLE : 3 * TABLE, :] = second_ref[:TABLE, :]
     near = (space + comp) % 2 == 0
     one = jnp.where(end, last_ref[AT_EDGE:, :], first_ref[AT_EDGE:, :])
-    sheet_ref[AT_HALO:, :] = jnp.where(near, one, second_ref[AT_EDGE:, :])
+    sheet_ref[AT_HALO:AT_MORE_LEVELS, :] = jnp.where(near, one, second_ref[AT_EDGE:, :])
+    sheet_ref[AT_MORE_LEVELS:, :] = strip_ref[AT_LEVELS:AT_REQUEST, :]
+
+
+def gather_rows(rows_ref, own, beside):
+    space, comp, lev = place()
+    for k in range(4):
+        for (start_ref, came_ref), c in ((own, comp), (beside, 1 - comp)):
+            block = came_ref[TABLE * (k - 1) : TABLE * k, :] if k else start_ref[:TABLE, :]
+            rows_ref[pl.ds((2 * (space ^ k) + c) * TABLE, TABLE), :] = block
 
 
 def margins_kernel(strip_ref, strip_beside_ref, own_ref, beside_ref, wet_ref, named_ref, rows_ref):
     space, comp, lev = place()
     lane, row = lane_of(), row_of()
-    for k in range(4):
-        for ref, c in ((own_ref, comp), (beside_ref, 1 - comp)):
-            at = (2 * (space ^ k) + c) * TABLE
-            rows_ref[pl.ds(at, TABLE), :] = ref[TABLE * k : TABLE * (k + 1), :]
+    gather_rows(rows_ref, (strip_ref, own_ref), (strip_beside_ref, beside_ref))
 
     def table_row(which):
         return rows_ref[pl.ds(which, ROWS, stride=TABLE), :]
@@ -308,7 +312,8 @@
     strip_beside_ref,
     own_ref,
     beside_ref,
-    others_ref,
+    other_ref,
+    halo_beside_ref,
     wet_ref,
     named_ref,
     atmos_ref,
@@ -330,14 +335,15 @@
     for level in range(half):
         here, there = lev * half + level, (1 - lev) * half + level
         at = 2 * ROWS * level
-        state_ref[here, :, mine] = strip_ref[at : at + 2 * ROWS, :]
-        state_ref[there, :, mine] = others_ref[OTHER_LEVELS + at : OTHER_LEVELS + at + 2 * ROWS, :]
-        state_ref[there, :, theirs] = strip_beside_ref[at : at + 2 * ROWS, :]
-        state_ref[here, :, theirs] = others_ref[BESIDE_LEVELS + at : BESIDE_LEVELS + at + 2 * ROWS, :]
+        rows = slice(AT_LEVELS + at, AT_LEVELS + at + 2 * ROWS)
+        state_ref[here, :, mine] = strip_ref[rows, :]
+        state_ref[there, :, mine] = other_ref[rows, :]
+        state_ref[there, :, theirs] = strip_beside_ref[rows, :]
+        state_ref[here, :, theirs] = beside_ref[AT_MORE_LEVELS + at : AT_MORE_LEVELS + at + 2 * ROWS, :]
     exists = jnp.where(lane < HALF, space + 1, 4 - space) < 4
     halos = (
-        (lev, others_ref[OTHER_HALO:BESIDE_BLOCKS, :], beside_ref[AT_HALO:AT_HALO_ASKED, :]),
-        (1 - lev, own_ref[AT_HALO:AT_HALO_ASKED, :], others_ref[BESIDE_HALO:OTHER_LEVELS, :]),
+        (lev, other_ref[OTHER_HALO:, :], halo_beside_ref[...]),
+        (1 - lev, own_ref[AT_HALO:AT_HALO_ASKED, :], beside_ref[AT_HALO:AT_HALO_ASKED, :]),
     )
     for block, own, beside in halos:
         east, west = jnp.where(comp == 0, own, beside), jnp.where(comp == 0, beside, own)
@@ -379,12 +385,7 @@
             flux_ref[tile, WIDE * field + 8 : WIDE * field + 24, :] = flux[:, LANES * tile : LANES * (tile + 1)]
             flux_ref[tile, WIDE * field + 24 : WIDE * field + 32, :] = jnp.zeros((ROWS, LANES), jnp.float32)
 
-    for k in range(4):
-        own, beside = 2 * (space ^ k) + comp, 2 * (space ^ k) + 1 - comp
-        block = slice(TABLE * k, TABLE * (k + 1))
-        came = slice(BESIDE_BLOCKS + TABLE * (k - 1), BESIDE_BLOCKS + TABLE * k)
-        rows_ref[pl.ds(own * TABLE, TABLE), :] = own_ref[block, :] if k else others_ref[:TABLE, :]
-        rows_ref[pl.ds(beside * TABLE, TABLE), :] = others_ref[came, :] if k else beside_ref[block, :]
+    gather_rows(rows_ref, (other_ref, own_ref), (strip_beside_ref, beside_ref))
     ocean_halo = rows_ref[pl.ds(PACKED, ROWS, stride=TABLE), :]
 
     wetness = wet_ref[...]
@@ -482,11 +483,11 @@
     )(*(pltpu.with_memory_space_constraint(a, pltpu.HBM) for a in arrays))
     first, second, last = (across("space", turns, letters[at]) for at, turns in ((1, FIRST), (3, SECOND), (2, LAST)))
     strip_beside = across("comp", (1, 0), strip)
-    sheet = local(sheet_kernel, values(SHEET, LANES), [pltpu.VMEM] * 4)(letters[0], first, second, last)
-    sheet_beside = across("comp", (1, 0), sheet)
-    swapped = (sheet[:TABLE], sheet[AT_HALO:AT_HALO_ASKED], sheet_beside[TABLE:AT_HALO_ASKED])
-    swapped += (strip[:AT_REQUEST], strip_beside[:AT_REQUEST])
-    others = over("lev", 1, jnp.concatenate(swapped, 0))
+    sheet = local(sheet_kernel, values(SHEET, LANES), [pltpu.VMEM] * 4)(strip, last, second, first)
+    sheet_beside = over("comp", 1, sheet)
+    halo = sheet[AT_HALO:AT_HALO_ASKED]
+    halo_beside = lax.ppermute(halo, ("comp", "lev"), [(0, 3), (3, 0), (1, 2), (2, 1)])
+    other = over("lev", 1, jnp.concatenate([strip[:AT_REQUEST], halo], 0))
     wet, named = local(
         margins_kernel,
         (values(ROWS, 2 * LANES), values(4, 3, ROWS, LANES)),
@@ -496,14 +497,14 @@
     atmos, final, *back = local(
         column_kernel,
         (values(*atmos_state.shape), values(FIELDS * ROWS, LANES)) + (values(FIELDS, LANES),) * 3,
-        [pltpu.VMEM] * 8,
+        [pltpu.VMEM] * 9,
         [
             pltpu.VMEM((LEVELS, 2 * ROWS, 3 * LANES), jnp.float32),
             pltpu.VMEM((3, FIELDS * WIDE, LANES), jnp.float32),
             pltpu.VMEM((ROWS * TABLE, LANES), jnp.float32),
             pltpu.VMEM((ROWS * FIELDS, LANES), jnp.float32),
         ],
-    )(factors, strip, strip_beside, sheet, sheet_beside, others, wet, named)
+    )(factors, strip, strip_beside, sheet, sheet_beside, other, halo_beside, wet, named)
     one, two, three = (across("space", [z ^ k for z in range(4)], piece) for k, piece in zip((1, 2, 3), back))
     final = over("lev", 1, final)
     atmos_next, returned = local(

time: 24.1 us -> 23.7 us (0.983)
  waiting for transfers between devices: 5.18 us -> 4.03 us
  starting transfers between devices: 13.8 us -> 14.6 us
    ppermute x8 -> x7, waiting for transfers between devices: 4.24 us -> 1.7 us  [across(): return lax.ppermute(array, (axis, 'lev'), pairs)]
    ppermute x2 -> x3, starting transfers between devices: 0.4 us -> 1.9 us  [over(): lax.ppermute(array, axis, [(i, i ^ k) for i in range(lax.axis_size(axis))])]
    ppermute x8 -> x7, starting transfers between devices: 13.4 us -> 12 us  [across(): return lax.ppermute(array, (axis, 'lev'), pairs)]
    ppermute x2 -> x3, waiting for transfers between devices: 0.94 us -> 2.32 us  [over(): lax.ppermute(array, axis, [(i, i ^ k) for i in range(lax.axis_size(axis))])]
    ppermute x0 -> x1, starting transfers between devices: none -> 0.65 us  [shards_by_columns(): lax.ppermute(halo, ('comp', 'lev'), [(0, 3), (3, 0), (1, 2), (2, 1)])]
  transfers between devices with their start and end apart: 10 -> 11, of which waited for: 5 -> 4; matrix products, arithmetic and copies ran while one was open for 0% -> 0% of each run, Pallas kernels for 4% -> 4%
where the time goes in v6:
time: 23.7 us; the launch traced here: 23.4 us
  starting transfers between devices  14.6 us (62%)
  Pallas kernels  4.13 us (17%)
  waiting for transfers between devices  4.03 us (17%)
  between operations  0.7 us (3%)
    ppermute x7, starting transfers between devices, across(): return lax.ppermute(array, (axis, 'lev'), pairs)  12 us
    ppermute x3, waiting for transfers between devices, over(): lax.ppermute(array, axis, [(i, i ^ k) for i in range(lax.axis_size(axis))])  2.32 us
    ppermute x3, starting transfers between devices, over(): lax.ppermute(array, axis, [(i, i ^ k) for i in range(lax.axis_size(axis))])  1.9 us
    ppermute x7, waiting for transfers between devices, across(): return lax.ppermute(array, (axis, 'lev'), pairs)  1.7 us
    pallas_call x1, Pallas kernels, shards_by_columns(): local(column_kernel, (values(*atmos_state.shape), values(FIELDS * ROWS, L...  1.44 us
    pallas_call x1, Pallas kernels, shards_by_columns(): local(tables_kernel, (values(4, LETTER, LANES), values(2 * LEVELS * LEVEL...  1.05 us
    pallas_call x1, Pallas kernels, shards_by_columns(): local(returned_kernel, (values(*atmos_state.shape), values(FIELDS * 2 * R...  0.72 us
    ppermute x1, starting transfers between devices, shards_by_columns(): lax.ppermute(halo, ('comp', 'lev'), [(0, 3), (3, 0), (1, 2), (2, 1)])  0.65 us
  transfers between devices with their start and end apart: 11, of which 4 were waited for; matrix products, arithmetic and copies ran while one was open for 0% of the time, Pallas kernels for 4%

profile of v6, /device:TPU:0, one launch (start us, length us, event | category | flops | bytes accessed | tf_op | source)
XLA Modules:
  0.0 23.4 jit_solution(11421009364856851827)
XLA Ops:
  0.6 1.0 %shard_map.103 = (f32[4,48,128]{2,1,0:T(8,128)S(1)}, f32[128,128]{1,0:T(8,128)S(1)}, f32[104,128]{1,0:T(8,128)S(1)}) custom-call(f32[8,1,512]{2,1,0:T(1,128)} %refs_0_.1, s32[4,1,512]{2,1,0:T(1,128)} %refs_1_.1, f32[4,1,512]{2,1,0:T(1,128)} %refs_2_.1, s32[1,512]{1,0:T(1,128)} %refs_3_.1, f32[4,16,128]{2,1,0:T(8,128)} %refs_4_.1, s32[1,8,256]{2,1,0:T(8,128)} %refs_5_.1, ...), custom_call_target="tpu_custom_call" | custom-call | tf_op jit(solution)/shard_map/pallas_call | solution.py:478
  1.7 2.5 %collective-permute-start.3 = (f32[48,128]{1,0:T(8,128)S(1)}, f32[48,128]{1,0:T(8,128)S(1)}, u32[]{:S(2)}, u32[]{:S(2)}) collective-permute-start(f32[48,128]{1,0:T(8,128)S(1)} %get-tuple-element.27), channel_id=1, source_target_pairs={{0,5},{1,4},{4,13},{5,12},{8,1},{9,0},{12,9},{13,8},{2,7},{3,6},{6... | collective-permute-start | bytes 73736 | tf_op jit(solution)/shard_map/ppermute | solution.py:447
  4.2 2.8 %collective-permute-start.2 = (f32[48,128]{1,0:T(8,128)S(1)}, f32[48,128]{1,0:T(8,128)S(1)}, u32[]{:S(2)}, u32[]{:S(2)}) collective-permute-start(f32[48,128]{1,0:T(8,128)S(1)} %get-tuple-element.28), channel_id=1, source_target_pairs={{0,13},{1,12},{4,9},{5,8},{8,5},{9,4},{12,1},{13,0},{2,15},{3,14},... | collective-permute-start | bytes 73736 | tf_op jit(solution)/shard_map/ppermute | solution.py:447
  7.0 1.0 %collective-permute-start.1 = (f32[48,128]{1,0:T(8,128)S(1)}, f32[48,128]{1,0:T(8,128)S(1)}, u32[]{:S(2)}, u32[]{:S(2)}) collective-permute-start(f32[48,128]{1,0:T(8,128)S(1)} %get-tuple-element.29), channel_id=1, source_target_pairs={{0,9},{1,8},{4,1},{5,0},{8,13},{9,12},{12,5},{13,4},{2,11},{3,10},... | collective-permute-start | bytes 73736 | tf_op jit(solution)/shard_map/ppermute | solution.py:447
  8.0 1.8 %collective-permute-start = (f32[104,128]{1,0:T(8,128)S(1)}, f32[104,128]{1,0:T(8,128)S(1)}, u32[]{:S(2)}, u32[]{:S(2)}) collective-permute-start(f32[104,128]{1,0:T(8,128)S(1)} %get-tuple-element.16.strip_ref), channel_id=1, source_target_pairs={{0,3},{1,2},{2,1},{3,0},{4,7},{5,6},{6,5},{7,4},{8,11},{9,10},{10,... | collective-permute-start | bytes 159752 | tf_op jit(solution)/shard_map/ppermute | solution.py:447
  9.8 0.0 collective-permute-done.3.first_ref
  9.8 0.0 collective-permute-done.2.second_ref
  9.8 0.8 %collective-permute-done.1.last_ref = f32[48,128]{1,0:T(8,128)S(1)} collective-permute-done((f32[48,128]{1,0:T(8,128)S(1)}, f32[48,128]{1,0:T(8,128)S(1)}, u32[]{:S(2)}, u32[]{:S(2)}) %collective-permute-start.1) | collective-permute-done | bytes 24608 | tf_op jit(solution)/shard_map/ppermute | solution.py:447
  10.6 1.6 %collective-permute-start.4 = (f32[160,128]{1,0:T(8,128)S(1)}, f32[160,128]{1,0:T(8,128)S(1)}, u32[]{:S(2)}, u32[]{:S(2)}) collective-permute-start(f32[160,128]{1,0:T(8,128)S(1)} %shard_map.104.own_ref), channel_id=1, source_target_pairs={{0,2},{2,0},{1,3},{3,1},{4,6},{6,4},{5,7},{7,5},{8,10},{10,8},{9,1... | collective-permute-start | bytes 245768 | tf_op jit(solution)/shard_map/ppermute | solution.py:442
  12.2 0.0 collective-permute-start.5
  12.2 0.6 %collective-permute-start.6 = (f32[8,128]{1,0:T(8,128)S(1)}, f32[8,128]{1,0:T(8,128)S(1)}, u32[]{:S(2)}, u32[]{:S(2)}) collective-permute-start(f32[8,128]{1,0:T(8,128)S(1)} %slice.20), channel_id=1, source_target_pairs={{0,3},{3,0},{1,2},{2,1},{4,7},{7,4},{5,6},{6,5},{8,11},{11,8},{9,1... | collective-permute-start | bytes 12296 | tf_op jit(solution)/shard_map/ppermute | solution.py:489
  12.9 0.0 collective-permute-done.strip_beside_ref
  12.9 2.3 %collective-permute-done.4.beside_ref = f32[160,128]{1,0:T(8,128)S(1)} collective-permute-done((f32[160,128]{1,0:T(8,128)S(1)}, f32[160,128]{1,0:T(8,128)S(1)}, u32[]{:S(2)}, u32[]{:S(2)}) %collective-permute-start.4) | collective-permute-done | bytes 81952 | tf_op jit(solution)/shard_map/ppermute | solution.py:442
  15.2 0.3 %shard_map.105 = (f32[8,256]{1,0:T(8,128)S(1)}, f32[4,3,8,128]{3,2,1,0:T(8,128)S(1)}) custom-call(f32[104,128]{1,0:T(8,128)S(1)} %get-tuple-element.16.strip_ref, f32[104,128]{1,0:T(8,128)S(1)} %collective-permute-done.strip_beside_ref, f32[160,128]{1,0:T(8,128)S(1)} %shard_map.104.own_ref, f32[160,128]{1,0:T(8,128)S(1)} %collective-permute-done.4.beside_ref), custom_call_target="tpu_custom_call" | custom-call | tf_op jit(solution)/shard_map/pallas_call | solution.py:491
  15.5 0.0 collective-permute-done.6.halo_beside_ref
  15.5 0.0 collective-permute-done.5.other_ref
  15.5 1.4 %shard_map.106 = (f32[4,16,128]{2,1,0:T(8,128)S(1)}, f32[64,128]{1,0:T(8,128)S(1)}, f32[8,128]{1,0:T(8,128)S(1)}, f32[8,128]{1,0:T(8,128)S(1)}, f32[8,128]{1,0:T(8,128)S(1)}) custom-call(f32[128,128]{1,0:T(8,128)S(1)} %get-tuple-element.15.factors_ref, f32[104,128]{1,0:T(8,128)S(1)} %get-tuple-element.16.strip_ref, ...), custom_call_target="tpu_custom_call" | custom-call | tf_op jit(solution)/shard_map/pallas_call | solution.py:497
  16.9 0.3 %collective-permute-start.7 = (f32[64,128]{1,0:T(8,128)S(1)}, f32[64,128]{1,0:T(8,128)S(1)}, u32[]{:S(2)}, u32[]{:S(2)}) collective-permute-start(f32[64,128]{1,0:T(8,128)S(1)} %get-tuple-element.21), channel_id=1, source_target_pairs={{0,1},{1,0},{2,3},{3,2},{4,5},{5,4},{6,7},{7,6},{8,9},{9,8},{10,11... | collective-permute-start | bytes 98312 | tf_op jit(solution)/shard_map/ppermute | solution.py:442
  17.3 1.6 %collective-permute-start.8 = (f32[8,128]{1,0:T(8,128)S(1)}, f32[8,128]{1,0:T(8,128)S(1)}, u32[]{:S(2)}, u32[]{:S(2)}) collective-permute-start(f32[8,128]{1,0:T(8,128)S(1)} %get-tuple-element.23), channel_id=1, source_target_pairs={{0,13},{1,12},{4,9},{5,8},{8,5},{9,4},{12,1},{13,0},{2,15},{3,14},... | collective-permute-start | bytes 12296 | tf_op jit(solution)/shard_map/ppermute | solution.py:447
  18.9 0.6 %collective-permute-start.9 = (f32[8,128]{1,0:T(8,128)S(1)}, f32[8,128]{1,0:T(8,128)S(1)}, u32[]{:S(2)}, u32[]{:S(2)}) collective-permute-start(f32[8,128]{1,0:T(8,128)S(1)} %get-tuple-element.24), channel_id=1, source_target_pairs={{0,9},{1,8},{4,13},{5,12},{8,1},{9,0},{12,5},{13,4},{2,11},{3,10},... | collective-permute-start | bytes 12296 | tf_op jit(solution)/shard_map/ppermute | solution.py:447
  19.4 1.8 %collective-permute-start.10 = (f32[8,128]{1,0:T(8,128)S(1)}, f32[8,128]{1,0:T(8,128)S(1)}, u32[]{:S(2)}, u32[]{:S(2)}) collective-permute-start(f32[8,128]{1,0:T(8,128)S(1)} %get-tuple-element.25), channel_id=1, source_target_pairs={{0,5},{1,4},{4,1},{5,0},{8,13},{9,12},{12,9},{13,8},{2,7},{3,6},{6... | collective-permute-start | bytes 12296 | tf_op jit(solution)/shard_map/ppermute | solution.py:447
  21.2 0.0 collective-permute-done.7.final_ref
  21.2 0.7 %shard_map.107 = (f32[4,16,128]{2,1,0:T(8,128)}, f32[128,128]{1,0:T(8,128)}) custom-call(f32[4,16,128]{2,1,0:T(8,128)S(1)} %get-tuple-element.20.atmos_ref, f32[64,128]{1,0:T(8,128)S(1)} %collective-permute-done.7.final_ref, f32[4,3,8,128]{3,2,1,0:T(8,128)S(1)} %get-tuple-element.19.named_ref), custom_call_target="tpu_custom_call" | custom-call | tf_op jit(solution)/shard_map/pallas_call | solution.py:510
  21.9 0.2 collective-permute-done.8.three_ref
  22.1 0.7 %collective-permute-done.9.two_ref = f32[8,128]{1,0:T(8,128)S(1)} collective-permute-done((f32[8,128]{1,0:T(8,128)S(1)}, f32[8,128]{1,0:T(8,128)S(1)}, u32[]{:S(2)}, u32[]{:S(2)}) %collective-permute-start.9) | collective-permute-done | bytes 4128 | tf_op jit(solution)/shard_map/ppermute | solution.py:447
  22.8 0.0 collective-permute-done.10.one_ref
  22.8 0.6 %shard_map.108 = f32[8,1,512]{2,1,0:T(1,128)} custom-call(f32[8,128]{1,0:T(8,128)S(1)} %collective-permute-done.8.three_ref, f32[8,128]{1,0:T(8,128)S(1)} %collective-permute-done.9.two_ref, f32[8,128]{1,0:T(8,128)S(1)} %collective-permute-done.10.one_ref, f32[64,128]{1,0:T(8,128)S(1)} %collective-permute-done.7.final_ref), custom_call_target="tpu_custom_call" | custom-call | tf_op jit(solution)/shard_map/pallas_call | solution.py:515
  (5 shorter events, 0.0 us)
Async XLA Ops:
  1.7 8.1 %collective-permute-start.3 = (f32[48,128]{1,0:T(8,128)S(1)}, f32[48,128]{1,0:T(8,128)S(1)}, u32[]{:S(2)}, u32[]{:S(2)}) collective-permute-start(f32[48,128]{1,0:T(8,128)S(1)} %get-tuple-element.27), channel_id=1, source_target_pairs={{0,5},{1,4},{4,13},{5,12},{8,1},{9,0},{12,9},{13,8},{2,7},{3,6},{6... | collective-permute-start | bytes 73736 | tf_op jit(solution)/shard_map/ppermute | solution.py:447
  4.2 5.6 %collective-permute-start.2 = (f32[48,128]{1,0:T(8,128)S(1)}, f32[48,128]{1,0:T(8,128)S(1)}, u32[]{:S(2)}, u32[]{:S(2)}) collective-permute-start(f32[48,128]{1,0:T(8,128)S(1)} %get-tuple-element.28), channel_id=1, source_target_pairs={{0,13},{1,12},{4,9},{5,8},{8,5},{9,4},{12,1},{13,0},{2,15},{3,14},... | collective-permute-start | bytes 73736 | tf_op jit(solution)/shard_map/ppermute | solution.py:447
  7.0 3.6 %collective-permute-start.1 = (f32[48,128]{1,0:T(8,128)S(1)}, f32[48,128]{1,0:T(8,128)S(1)}, u32[]{:S(2)}, u32[]{:S(2)}) collective-permute-start(f32[48,128]{1,0:T(8,128)S(1)} %get-tuple-element.29), channel_id=1, source_target_pairs={{0,9},{1,8},{4,1},{5,0},{8,13},{9,12},{12,5},{13,4},{2,11},{3,10},... | collective-permute-start | bytes 73736 | tf_op jit(solution)/shard_map/ppermute | solution.py:447
  8.0 4.9 %collective-permute-start = (f32[104,128]{1,0:T(8,128)S(1)}, f32[104,128]{1,0:T(8,128)S(1)}, u32[]{:S(2)}, u32[]{:S(2)}) collective-permute-start(f32[104,128]{1,0:T(8,128)S(1)} %get-tuple-element.16.strip_ref), channel_id=1, source_target_pairs={{0,3},{1,2},{2,1},{3,0},{4,7},{5,6},{6,5},{7,4},{8,11},{9,10},{10,... | collective-permute-start | bytes 159752 | tf_op jit(solution)/shard_map/ppermute | solution.py:447
  10.6 4.5 %collective-permute-start.4 = (f32[160,128]{1,0:T(8,128)S(1)}, f32[160,128]{1,0:T(8,128)S(1)}, u32[]{:S(2)}, u32[]{:S(2)}) collective-permute-start(f32[160,128]{1,0:T(8,128)S(1)} %shard_map.104.own_ref), channel_id=1, source_target_pairs={{0,2},{2,0},{1,3},{3,1},{4,6},{6,4},{5,7},{7,5},{8,10},{10,8},{9,1... | collective-permute-start | bytes 245768 | tf_op jit(solution)/shard_map/ppermute | solution.py:442
  12.2 3.3 %collective-permute-start.5 = (f32[96,128]{1,0:T(8,128)S(1)}, f32[96,128]{1,0:T(8,128)S(1)}, u32[]{:S(2)}, u32[]{:S(2)}) collective-permute-start(f32[96,128]{1,0:T(8,128)S(1)} %pad_maximum_fusion), channel_id=1, source_target_pairs={{0,1},{1,0},{2,3},{3,2},{4,5},{5,4},{6,7},{7,6},{8,9},{9,8},{10,11... | collective-permute-start | bytes 147464 | tf_op jit(solution)/shard_map/ppermute | solution.py:442
  12.2 3.3 %collective-permute-start.6 = (f32[8,128]{1,0:T(8,128)S(1)}, f32[8,128]{1,0:T(8,128)S(1)}, u32[]{:S(2)}, u32[]{:S(2)}) collective-permute-start(f32[8,128]{1,0:T(8,128)S(1)} %slice.20), channel_id=1, source_target_pairs={{0,3},{3,0},{1,2},{2,1},{4,7},{7,4},{5,6},{6,5},{8,11},{11,8},{9,1... | collective-permute-start | bytes 12296 | tf_op jit(solution)/shard_map/ppermute | solution.py:489
  16.9 4.3 %collective-permute-start.7 = (f32[64,128]{1,0:T(8,128)S(1)}, f32[64,128]{1,0:T(8,128)S(1)}, u32[]{:S(2)}, u32[]{:S(2)}) collective-permute-start(f32[64,128]{1,0:T(8,128)S(1)} %get-tuple-element.21), channel_id=1, source_target_pairs={{0,1},{1,0},{2,3},{3,2},{4,5},{5,4},{6,7},{7,6},{8,9},{9,8},{10,11... | collective-permute-start | bytes 98312 | tf_op jit(solution)/shard_map/ppermute | solution.py:442
  17.3 4.8 %collective-permute-start.8 = (f32[8,128]{1,0:T(8,128)S(1)}, f32[8,128]{1,0:T(8,128)S(1)}, u32[]{:S(2)}, u32[]{:S(2)}) collective-permute-start(f32[8,128]{1,0:T(8,128)S(1)} %get-tuple-element.23), channel_id=1, source_target_pairs={{0,13},{1,12},{4,9},{5,8},{8,5},{9,4},{12,1},{13,0},{2,15},{3,14},... | collective-permute-start | bytes 12296 | tf_op jit(solution)/shard_map/ppermute | solution.py:447
  18.9 3.9 %collective-permute-start.9 = (f32[8,128]{1,0:T(8,128)S(1)}, f32[8,128]{1,0:T(8,128)S(1)}, u32[]{:S(2)}, u32[]{:S(2)}) collective-permute-start(f32[8,128]{1,0:T(8,128)S(1)} %get-tuple-element.24), channel_id=1, source_target_pairs={{0,9},{1,8},{4,13},{5,12},{8,1},{9,0},{12,5},{13,4},{2,11},{3,10},... | collective-permute-start | bytes 12296 | tf_op jit(solution)/shard_map/ppermute | solution.py:447
  19.4 3.4 %collective-permute-start.10 = (f32[8,128]{1,0:T(8,128)S(1)}, f32[8,128]{1,0:T(8,128)S(1)}, u32[]{:S(2)}, u32[]{:S(2)}) collective-permute-start(f32[8,128]{1,0:T(8,128)S(1)} %get-tuple-element.25), channel_id=1, source_target_pairs={{0,5},{1,4},{4,1},{5,0},{8,13},{9,12},{12,9},{13,8},{2,7},{3,6},{6... | collective-permute-start | bytes 12296 | tf_op jit(solution)/shard_map/ppermute | solution.py:447

commit v7 on v6

--- a/solution.py
+++ b/solution.py
@@ -174,7 +174,7 @@
 
 
 def tables_kernel(*refs):
-    arrays, (letters_ref, factors_ref, strip_ref), held, arrived = refs[:8], refs[8:11], refs[11:-1], refs[-1]
+    arrays, (letters_ref, strip_ref, mixed_ref, coupled_ref), held, arrived = refs[:8], refs[8:12], refs[12:-1], refs[-1]
     copies = [pltpu.make_async_copy(a, h, arrived.at[i]) for i, (a, h) in enumerate(zip(arrays, held))]
     for copy in copies:
         copy.start()
@@ -221,6 +221,17 @@
         letters_ref[k, AT_EDGE:AT_ASKED, :] = edge
         letters_ref[k, AT_ASKED : AT_ASKED + 8, :] = requests[:, :LANES]
         letters_ref[k, AT_ASKED + 8 :, :] = requests[:, LANES:]
+    mixed_ref[...] = mixing_ref[...]
+    coupled_ref[...] = coupling_ref[...]
+    for level in range(LEVELS // 2):
+        strip_ref[AT_LEVELS + 2 * ROWS * level : AT_LEVELS + 2 * ROWS * (level + 1), :] = atmos_ref[level]
+    strip_ref[:TABLE, :] = letters_ref[0, :TABLE, :]
+    strip_ref[AT_REQUEST : AT_REQUEST + 8, :] = requests[:, :LANES]
+    strip_ref[AT_REQUEST + 8 :, :] = requests[:, LANES:]
+
+
+def factors_kernel(mixing_ref, coupling_ref, factors_ref):
+    space, comp, lev = place()
     for other in range(LEVELS):
         factors_ref[LEVELS * other : LEVELS * (other + 1), :] = jnp.broadcast_to(
             TENDENCY * mixing_ref[:, other : other + 1], (ROWS, LANES)
@@ -229,11 +240,6 @@
         other = [coupling_ref[:, FIELDS * i + field : FIELDS * i + field + 1] for i in range(2)]
         at = LEVELS * (LEVELS + field)
         factors_ref[at : at + LEVELS, :] = jnp.broadcast_to(jnp.where(lev == 0, other[1], other[0]), (ROWS, LANES))
-    for level in range(LEVELS // 2):
-        strip_ref[AT_LEVELS + 2 * ROWS * level : AT_LEVELS + 2 * ROWS * (level + 1), :] = atmos_ref[level]
-    strip_ref[:TABLE, :] = letters_ref[0, :TABLE, :]
-    strip_ref[AT_REQUEST : AT_REQUEST + 8, :] = requests[:, :LANES]
-    strip_ref[AT_REQUEST + 8 :, :] = requests[:, LANES:]
 
 
 def sheet_kernel(strip_ref, last_ref, second_ref, first_ref, sheet_ref):
@@ -475,9 +481,9 @@
 
     arrays = (ocean_state, margin_slot, margin_weight, sea_mask, atmos_state, request_cells)
     arrays += (vertical_mixing, flux_coupling.T)
-    letters, factors, strip = local(
+    letters, strip, mixing, coupling = local(
         tables_kernel,
-        (values(4, LETTER, LANES), values(2 * LEVELS * LEVELS, LANES), values(STRIP, LANES)),
+        (values(4, LETTER, LANES), values(STRIP, LANES), values(LEVELS, LEVELS), values(LEVELS, 2 * FIELDS)),
         [pltpu.HBM] * 8,
         [pltpu.VMEM(a.shape, a.dtype) for a in arrays] + [pltpu.SemaphoreType.DMA((8,))],
     )(*(pltpu.with_memory_space_constraint(a, pltpu.HBM) for a in arrays))
@@ -488,6 +494,7 @@
     halo = sheet[AT_HALO:AT_HALO_ASKED]
     halo_beside = lax.ppermute(halo, ("comp", "lev"), [(0, 3), (3, 0), (1, 2), (2, 1)])
     other = over("lev", 1, jnp.concatenate([strip[:AT_REQUEST], halo], 0))
+    factors = local(factors_kernel, values(2 * LEVELS * LEVELS, LANES), [pltpu.VMEM] * 2)(mixing, coupling)
     wet, named = local(
         margins_kernel,
         (values(ROWS, 2 * LANES), values(4, 3, ROWS, LANES)),

time: 23.7 us -> 23.6 us (level)
    pallas_call x1 -> x2, Pallas kernels: 1.05 us -> 1.15 us  [the longest x1 1.01 us: shards_by_columns(): local(tables_kernel, (values(4, LETTER, LANES), values(STRIP, LANES), val...]
  transfers between devices with their start and end apart: 11 -> 11, of which waited for: 4 -> 4; matrix products, arithmetic and copies ran while one was open for 0% -> 0% of each run, Pallas kernels for 4% -> 5%
where the time goes in v7:
time: 23.6 us; the launch traced here: 23.4 us
  starting transfers between devices  14.6 us (62%)
  Pallas kernels  4.22 us (18%)
  waiting for transfers between devices  3.88 us (16%)
  between operations  0.71 us (3%)
    ppermute x7, starting transfers between devices, across(): return lax.ppermute(array, (axis, 'lev'), pairs)  12 us
    ppermute x3, waiting for transfers between devices, over(): lax.ppermute(array, axis, [(i, i ^ k) for i in range(lax.axis_size(axis))])  2.17 us
    ppermute x3, starting transfers between devices, over(): lax.ppermute(array, axis, [(i, i ^ k) for i in range(lax.axis_size(axis))])  1.9 us
    ppermute x7, waiting for transfers between devices, across(): return lax.ppermute(array, (axis, 'lev'), pairs)  1.7 us
    pallas_call x1, Pallas kernels, shards_by_columns(): local(column_kernel, (values(*atmos_state.shape), values(FIELDS * ROWS, L...  1.43 us
    pallas_call x1, Pallas kernels, shards_by_columns(): local(tables_kernel, (values(4, LETTER, LANES), values(STRIP, LANES), val...  1.01 us
    pallas_call x1, Pallas kernels, shards_by_columns(): local(returned_kernel, (values(*atmos_state.shape), values(FIELDS * 2 * R...  0.72 us
    ppermute x1, starting transfers between devices, shards_by_columns(): lax.ppermute(halo, ('comp', 'lev'), [(0, 3), (3, 0), (1, 2), (2, 1)])  0.65 us
  transfers between devices with their start and end apart: 11, of which 4 were waited for; matrix products, arithmetic and copies ran while one was open for 0% of the time, Pallas kernels for 5%

profile of v7, /device:TPU:0, one launch (start us, length us, event | category | flops | bytes accessed | tf_op | source)
XLA Modules:
  0.0 23.4 jit_solution(13213081476061898712)
XLA Ops:
  0.6 1.0 %shard_map.103 = (f32[4,48,128]{2,1,0:T(8,128)S(1)}, f32[104,128]{1,0:T(8,128)S(1)}, f32[8,8]{1,0:T(8,128)S(1)}, f32[8,16]{1,0:T(8,128)S(1)}) custom-call(f32[8,1,512]{2,1,0:T(1,128)} %refs_0_.1, s32[4,1,512]{2,1,0:T(1,128)} %refs_1_.1, f32[4,1,512]{2,1,0:T(1,128)} %refs_2_.1, s32[1,512]{1,0:T(1,128)} %refs_3_.1, f32[4,16,128]{2,1,0:T(8,128)} %refs_4_.1, ...), custom_call_target="tpu_custom_call" | custom-call | tf_op jit(solution)/shard_map/pallas_call | solution.py:484
  1.7 2.5 %collective-permute-start.3 = (f32[48,128]{1,0:T(8,128)S(1)}, f32[48,128]{1,0:T(8,128)S(1)}, u32[]{:S(2)}, u32[]{:S(2)}) collective-permute-start(f32[48,128]{1,0:T(8,128)S(1)} %get-tuple-element.29), channel_id=1, source_target_pairs={{0,5},{1,4},{4,13},{5,12},{8,1},{9,0},{12,9},{13,8},{2,7},{3,6},{6... | collective-permute-start | bytes 73736 | tf_op jit(solution)/shard_map/ppermute | solution.py:453
  4.2 2.8 %collective-permute-start.2 = (f32[48,128]{1,0:T(8,128)S(1)}, f32[48,128]{1,0:T(8,128)S(1)}, u32[]{:S(2)}, u32[]{:S(2)}) collective-permute-start(f32[48,128]{1,0:T(8,128)S(1)} %get-tuple-element.30), channel_id=1, source_target_pairs={{0,13},{1,12},{4,9},{5,8},{8,5},{9,4},{12,1},{13,0},{2,15},{3,14},... | collective-permute-start | bytes 73736 | tf_op jit(solution)/shard_map/ppermute | solution.py:453
  6.9 1.0 %collective-permute-start.1 = (f32[48,128]{1,0:T(8,128)S(1)}, f32[48,128]{1,0:T(8,128)S(1)}, u32[]{:S(2)}, u32[]{:S(2)}) collective-permute-start(f32[48,128]{1,0:T(8,128)S(1)} %get-tuple-element.31), channel_id=1, source_target_pairs={{0,9},{1,8},{4,1},{5,0},{8,13},{9,12},{12,5},{13,4},{2,11},{3,10},... | collective-permute-start | bytes 73736 | tf_op jit(solution)/shard_map/ppermute | solution.py:453
  8.0 1.8 %collective-permute-start = (f32[104,128]{1,0:T(8,128)S(1)}, f32[104,128]{1,0:T(8,128)S(1)}, u32[]{:S(2)}, u32[]{:S(2)}) collective-permute-start(f32[104,128]{1,0:T(8,128)S(1)} %get-tuple-element.18.strip_ref), channel_id=1, source_target_pairs={{0,3},{1,2},{2,1},{3,0},{4,7},{5,6},{6,5},{7,4},{8,11},{9,10},{10,... | collective-permute-start | bytes 159752 | tf_op jit(solution)/shard_map/ppermute | solution.py:453
  9.7 0.0 collective-permute-done.3.first_ref
  9.7 0.0 collective-permute-done.2.second_ref
  9.7 0.8 %collective-permute-done.1.last_ref = f32[48,128]{1,0:T(8,128)S(1)} collective-permute-done((f32[48,128]{1,0:T(8,128)S(1)}, f32[48,128]{1,0:T(8,128)S(1)}, u32[]{:S(2)}, u32[]{:S(2)}) %collective-permute-start.1) | collective-permute-done | bytes 24608 | tf_op jit(solution)/shard_map/ppermute | solution.py:453
  10.6 1.6 %collective-permute-start.4 = (f32[160,128]{1,0:T(8,128)S(1)}, f32[160,128]{1,0:T(8,128)S(1)}, u32[]{:S(2)}, u32[]{:S(2)}) collective-permute-start(f32[160,128]{1,0:T(8,128)S(1)} %shard_map.105.own_ref), channel_id=1, source_target_pairs={{0,2},{2,0},{1,3},{3,1},{4,6},{6,4},{5,7},{7,5},{8,10},{10,8},{9,1... | collective-permute-start | bytes 245768 | tf_op jit(solution)/shard_map/ppermute | solution.py:448
  12.2 0.0 collective-permute-start.5
  12.2 0.6 %collective-permute-start.6 = (f32[8,128]{1,0:T(8,128)S(1)}, f32[8,128]{1,0:T(8,128)S(1)}, u32[]{:S(2)}, u32[]{:S(2)}) collective-permute-start(f32[8,128]{1,0:T(8,128)S(1)} %slice.20), channel_id=1, source_target_pairs={{0,3},{3,0},{1,2},{2,1},{4,7},{7,4},{5,6},{6,5},{8,11},{11,8},{9,1... | collective-permute-start | bytes 12296 | tf_op jit(solution)/shard_map/ppermute | solution.py:495
  12.8 0.1 shard_map.104.factors_ref
  13.0 0.0 collective-permute-done.strip_beside_ref
  13.0 2.2 %collective-permute-done.4.beside_ref = f32[160,128]{1,0:T(8,128)S(1)} collective-permute-done((f32[160,128]{1,0:T(8,128)S(1)}, f32[160,128]{1,0:T(8,128)S(1)}, u32[]{:S(2)}, u32[]{:S(2)}) %collective-permute-start.4) | collective-permute-done | bytes 81952 | tf_op jit(solution)/shard_map/ppermute | solution.py:448
  15.1 0.3 %shard_map.106 = (f32[8,256]{1,0:T(8,128)S(1)}, f32[4,3,8,128]{3,2,1,0:T(8,128)S(1)}) custom-call(f32[104,128]{1,0:T(8,128)S(1)} %get-tuple-element.18.strip_ref, f32[104,128]{1,0:T(8,128)S(1)} %collective-permute-done.strip_beside_ref, f32[160,128]{1,0:T(8,128)S(1)} %shard_map.105.own_ref, f32[160,128]{1,0:T(8,128)S(1)} %collective-permute-done.4.beside_ref), custom_call_target="tpu_custom_call" | custom-call | tf_op jit(solution)/shard_map/pallas_call | solution.py:498
  15.4 0.0 collective-permute-done.6.halo_beside_ref
  15.4 0.0 collective-permute-done.5.other_ref
  15.4 1.4 %shard_map.107 = (f32[4,16,128]{2,1,0:T(8,128)S(1)}, f32[64,128]{1,0:T(8,128)S(1)}, f32[8,128]{1,0:T(8,128)S(1)}, f32[8,128]{1,0:T(8,128)S(1)}, f32[8,128]{1,0:T(8,128)S(1)}) custom-call(f32[128,128]{1,0:T(8,128)S(1)} %shard_map.104.factors_ref, f32[104,128]{1,0:T(8,128)S(1)} %get-tuple-element.18.strip_ref, ...), custom_call_target="tpu_custom_call" | custom-call | tf_op jit(solution)/shard_map/pallas_call | solution.py:504
  16.9 0.3 %collective-permute-start.7 = (f32[64,128]{1,0:T(8,128)S(1)}, f32[64,128]{1,0:T(8,128)S(1)}, u32[]{:S(2)}, u32[]{:S(2)}) collective-permute-start(f32[64,128]{1,0:T(8,128)S(1)} %get-tuple-element.23), channel_id=1, source_target_pairs={{0,1},{1,0},{2,3},{3,2},{4,5},{5,4},{6,7},{7,6},{8,9},{9,8},{10,11... | collective-permute-start | bytes 98312 | tf_op jit(solution)/shard_map/ppermute | solution.py:448
  17.2 1.6 %collective-permute-start.8 = (f32[8,128]{1,0:T(8,128)S(1)}, f32[8,128]{1,0:T(8,128)S(1)}, u32[]{:S(2)}, u32[]{:S(2)}) collective-permute-start(f32[8,128]{1,0:T(8,128)S(1)} %get-tuple-element.25), channel_id=1, source_target_pairs={{0,13},{1,12},{4,9},{5,8},{8,5},{9,4},{12,1},{13,0},{2,15},{3,14},... | collective-permute-start | bytes 12296 | tf_op jit(solution)/shard_map/ppermute | solution.py:453
  18.8 0.6 %collective-permute-start.9 = (f32[8,128]{1,0:T(8,128)S(1)}, f32[8,128]{1,0:T(8,128)S(1)}, u32[]{:S(2)}, u32[]{:S(2)}) collective-permute-start(f32[8,128]{1,0:T(8,128)S(1)} %get-tuple-element.26), channel_id=1, source_target_pairs={{0,9},{1,8},{4,13},{5,12},{8,1},{9,0},{12,5},{13,4},{2,11},{3,10},... | collective-permute-start | bytes 12296 | tf_op jit(solution)/shard_map/ppermute | solution.py:453
  19.4 1.8 %collective-permute-start.10 = (f32[8,128]{1,0:T(8,128)S(1)}, f32[8,128]{1,0:T(8,128)S(1)}, u32[]{:S(2)}, u32[]{:S(2)}) collective-permute-start(f32[8,128]{1,0:T(8,128)S(1)} %get-tuple-element.27), channel_id=1, source_target_pairs={{0,5},{1,4},{4,1},{5,0},{8,13},{9,12},{12,9},{13,8},{2,7},{3,6},{6... | collective-permute-start | bytes 12296 | tf_op jit(solution)/shard_map/ppermute | solution.py:453
  21.2 0.0 collective-permute-done.7.final_ref
  21.2 0.7 %shard_map.108 = (f32[4,16,128]{2,1,0:T(8,128)}, f32[128,128]{1,0:T(8,128)}) custom-call(f32[4,16,128]{2,1,0:T(8,128)S(1)} %get-tuple-element.22.atmos_ref, f32[64,128]{1,0:T(8,128)S(1)} %collective-permute-done.7.final_ref, f32[4,3,8,128]{3,2,1,0:T(8,128)S(1)} %get-tuple-element.21.named_ref), custom_call_target="tpu_custom_call" | custom-call | tf_op jit(solution)/shard_map/pallas_call | solution.py:517
  21.9 0.2 collective-permute-done.8.three_ref
  22.0 0.7 %collective-permute-done.9.two_ref = f32[8,128]{1,0:T(8,128)S(1)} collective-permute-done((f32[8,128]{1,0:T(8,128)S(1)}, f32[8,128]{1,0:T(8,128)S(1)}, u32[]{:S(2)}, u32[]{:S(2)}) %collective-permute-start.9) | collective-permute-done | bytes 4128 | tf_op jit(solution)/shard_map/ppermute | solution.py:453
  22.8 0.0 collective-permute-done.10.one_ref
  22.8 0.6 %shard_map.109 = f32[8,1,512]{2,1,0:T(1,128)} custom-call(f32[8,128]{1,0:T(8,128)S(1)} %collective-permute-done.8.three_ref, f32[8,128]{1,0:T(8,128)S(1)} %collective-permute-done.9.two_ref, f32[8,128]{1,0:T(8,128)S(1)} %collective-permute-done.10.one_ref, f32[64,128]{1,0:T(8,128)S(1)} %collective-permute-done.7.final_ref), custom_call_target="tpu_custom_call" | custom-call | tf_op jit(solution)/shard_map/pallas_call | solution.py:522
  (5 shorter events, 0.0 us)
Async XLA Ops:
  1.7 8.1 %collective-permute-start.3 = (f32[48,128]{1,0:T(8,128)S(1)}, f32[48,128]{1,0:T(8,128)S(1)}, u32[]{:S(2)}, u32[]{:S(2)}) collective-permute-start(f32[48,128]{1,0:T(8,128)S(1)} %get-tuple-element.29), channel_id=1, source_target_pairs={{0,5},{1,4},{4,13},{5,12},{8,1},{9,0},{12,9},{13,8},{2,7},{3,6},{6... | collective-permute-start | bytes 73736 | tf_op jit(solution)/shard_map/ppermute | solution.py:453
  4.2 5.6 %collective-permute-start.2 = (f32[48,128]{1,0:T(8,128)S(1)}, f32[48,128]{1,0:T(8,128)S(1)}, u32[]{:S(2)}, u32[]{:S(2)}) collective-permute-start(f32[48,128]{1,0:T(8,128)S(1)} %get-tuple-element.30), channel_id=1, source_target_pairs={{0,13},{1,12},{4,9},{5,8},{8,5},{9,4},{12,1},{13,0},{2,15},{3,14},... | collective-permute-start | bytes 73736 | tf_op jit(solution)/shard_map/ppermute | solution.py:453
  6.9 3.6 %collective-permute-start.1 = (f32[48,128]{1,0:T(8,128)S(1)}, f32[48,128]{1,0:T(8,128)S(1)}, u32[]{:S(2)}, u32[]{:S(2)}) collective-permute-start(f32[48,128]{1,0:T(8,128)S(1)} %get-tuple-element.31), channel_id=1, source_target_pairs={{0,9},{1,8},{4,1},{5,0},{8,13},{9,12},{12,5},{13,4},{2,11},{3,10},... | collective-permute-start | bytes 73736 | tf_op jit(solution)/shard_map/ppermute | solution.py:453
  8.0 5.0 %collective-permute-start = (f32[104,128]{1,0:T(8,128)S(1)}, f32[104,128]{1,0:T(8,128)S(1)}, u32[]{:S(2)}, u32[]{:S(2)}) collective-permute-start(f32[104,128]{1,0:T(8,128)S(1)} %get-tuple-element.18.strip_ref), channel_id=1, source_target_pairs={{0,3},{1,2},{2,1},{3,0},{4,7},{5,6},{6,5},{7,4},{8,11},{9,10},{10,... | collective-permute-start | bytes 159752 | tf_op jit(solution)/shard_map/ppermute | solution.py:453
  10.6 4.5 %collective-permute-start.4 = (f32[160,128]{1,0:T(8,128)S(1)}, f32[160,128]{1,0:T(8,128)S(1)}, u32[]{:S(2)}, u32[]{:S(2)}) collective-permute-start(f32[160,128]{1,0:T(8,128)S(1)} %shard_map.105.own_ref), channel_id=1, source_target_pairs={{0,2},{2,0},{1,3},{3,1},{4,6},{6,4},{5,7},{7,5},{8,10},{10,8},{9,1... | collective-permute-start | bytes 245768 | tf_op jit(solution)/shard_map/ppermute | solution.py:448
  12.2 3.3 %collective-permute-start.5 = (f32[96,128]{1,0:T(8,128)S(1)}, f32[96,128]{1,0:T(8,128)S(1)}, u32[]{:S(2)}, u32[]{:S(2)}) collective-permute-start(f32[96,128]{1,0:T(8,128)S(1)} %pad_maximum_fusion), channel_id=1, source_target_pairs={{0,1},{1,0},{2,3},{3,2},{4,5},{5,4},{6,7},{7,6},{8,9},{9,8},{10,11... | collective-permute-start | bytes 147464 | tf_op jit(solution)/shard_map/ppermute | solution.py:448
  12.2 3.3 %collective-permute-start.6 = (f32[8,128]{1,0:T(8,128)S(1)}, f32[8,128]{1,0:T(8,128)S(1)}, u32[]{:S(2)}, u32[]{:S(2)}) collective-permute-start(f32[8,128]{1,0:T(8,128)S(1)} %slice.20), channel_id=1, source_target_pairs={{0,3},{3,0},{1,2},{2,1},{4,7},{7,4},{5,6},{6,5},{8,11},{11,8},{9,1... | collective-permute-start | bytes 12296 | tf_op jit(solution)/shard_map/ppermute | solution.py:495
  16.9 4.3 %collective-permute-start.7 = (f32[64,128]{1,0:T(8,128)S(1)}, f32[64,128]{1,0:T(8,128)S(1)}, u32[]{:S(2)}, u32[]{:S(2)}) collective-permute-start(f32[64,128]{1,0:T(8,128)S(1)} %get-tuple-element.23), channel_id=1, source_target_pairs={{0,1},{1,0},{2,3},{3,2},{4,5},{5,4},{6,7},{7,6},{8,9},{9,8},{10,11... | collective-permute-start | bytes 98312 | tf_op jit(solution)/shard_map/ppermute | solution.py:448
  17.2 4.8 %collective-permute-start.8 = (f32[8,128]{1,0:T(8,128)S(1)}, f32[8,128]{1,0:T(8,128)S(1)}, u32[]{:S(2)}, u32[]{:S(2)}) collective-permute-start(f32[8,128]{1,0:T(8,128)S(1)} %get-tuple-element.25), channel_id=1, source_target_pairs={{0,13},{1,12},{4,9},{5,8},{8,5},{9,4},{12,1},{13,0},{2,15},{3,14},... | collective-permute-start | bytes 12296 | tf_op jit(solution)/shard_map/ppermute | solution.py:453
  18.8 3.9 %collective-permute-start.9 = (f32[8,128]{1,0:T(8,128)S(1)}, f32[8,128]{1,0:T(8,128)S(1)}, u32[]{:S(2)}, u32[]{:S(2)}) collective-permute-start(f32[8,128]{1,0:T(8,128)S(1)} %get-tuple-element.26), channel_id=1, source_target_pairs={{0,9},{1,8},{4,13},{5,12},{8,1},{9,0},{12,5},{13,4},{2,11},{3,10},... | collective-permute-start | bytes 12296 | tf_op jit(solution)/shard_map/ppermute | solution.py:453
  19.4 3.4 %collective-permute-start.10 = (f32[8,128]{1,0:T(8,128)S(1)}, f32[8,128]{1,0:T(8,128)S(1)}, u32[]{:S(2)}, u32[]{:S(2)}) collective-permute-start(f32[8,128]{1,0:T(8,128)S(1)} %get-tuple-element.27), channel_id=1, source_target_pairs={{0,5},{1,4},{4,1},{5,0},{8,13},{9,12},{12,9},{13,8},{2,7},{3,6},{6... | collective-permute-start | bytes 12296 | tf_op jit(solution)/shard_map/ppermute | solution.py:453

commit v8 on v7

--- a/solution.py
+++ b/solution.py
@@ -312,8 +312,24 @@
             named_ref[step, tile] = named[step][tile]
 
 
+def mixing_kernel(factors_ref, strip_ref, other_ref, mixed_ref, shaded_ref):
+    space, comp, lev = place()
+    half = LEVELS // 2
+    for level in range(half):
+        at = AT_LEVELS + 2 * ROWS * level
+        shaded_ref[lev * half + level] = jnp.tanh(strip_ref[at : at + 2 * ROWS, :])
+        shaded_ref[(1 - lev) * half + level] = jnp.tanh(other_ref[at : at + 2 * ROWS, :])
+    for level in range(LEVELS):
+        mixed_ref[level] = sum(
+            jnp.broadcast_to(factors_ref[LEVELS * other + level : LEVELS * other + level + 1, :], (2 * ROWS, LANES))
+            * shaded_ref[other]
+            for other in range(LEVELS)
+        )
+
+
 def column_kernel(
     factors_ref,
+    mixed_own_ref,
     strip_ref,
     strip_beside_ref,
     own_ref,
@@ -331,6 +347,7 @@
     flux_ref,
     rows_ref,
     back_ref,
+    mixed_ref,
 ):
     space, comp, lev = place()
     lane, row = lane_of(), row_of()
@@ -365,17 +382,26 @@
     edge_inside = jnp.where(jnp.concatenate([exists] * 2, 0), 1.0, 0.0)
     inside = jnp.concatenate([jnp.ones((2 * ROWS, 2 * LANES), jnp.float32), edge_inside], 1)
 
-    def factor(which):
-        return jnp.broadcast_to(jnp.concatenate([factors_ref[which : which + 1, :]] * 3, 1), (2 * ROWS, 3 * LANES))
-
+    def factor(which, tiles=3):
+        return jnp.broadcast_to(jnp.concatenate([factors_ref[which : which + 1, :]] * tiles, 1), (2 * ROWS, tiles * LANES))
+
+    rest = [jnp.tanh(jnp.concatenate([state_ref[i, :, theirs], state_ref[i, :, 2 * LANES :]], 1)) for i in range(LEVELS)]
+    for level in range(LEVELS):
+        column = sum(factor(LEVELS * other + level, 2) * rest[other] for other in range(LEVELS))
+        mixed_ref[level, :, mine] = mixed_own_ref[level]
+        mixed_ref[level, :, theirs] = column[:, :LANES]
+        mixed_ref[level, :, 2 * LANES :] = column[:, LANES:]
     atmos = [state_ref[level] for level in range(LEVELS)]
     for substep in range(ASUB):
-        shaded = [jnp.tanh(cells) for cells in atmos]
+        shaded = [jnp.tanh(cells) for cells in atmos] if substep else None
         later = []
         for level in range(LEVELS):
             cells = atmos[level]
             beside = turn(cells, 1) + turn(cells, -1) + rows_down(cells) + rows_up(cells)
-            column = sum(factor(LEVELS * other + level) * shaded[other] for other in range(LEVELS))
+            if substep:
+                column = sum(factor(LEVELS * other + level) * shaded[other] for other in range(LEVELS))
+            else:
+                column = mixed_ref[level]
             cells = DIFFUSE * (cells + beside) + column
             later.append(inside * cells)
         atmos = later
@@ -495,6 +521,12 @@
     halo_beside = lax.ppermute(halo, ("comp", "lev"), [(0, 3), (3, 0), (1, 2), (2, 1)])
     other = over("lev", 1, jnp.concatenate([strip[:AT_REQUEST], halo], 0))
     factors = local(factors_kernel, values(2 * LEVELS * LEVELS, LANES), [pltpu.VMEM] * 2)(mixing, coupling)
+    mixed = local(
+        mixing_kernel,
+        values(LEVELS, 2 * ROWS, LANES),
+        [pltpu.VMEM] * 3,
+        [pltpu.VMEM((LEVELS, 2 * ROWS, LANES), jnp.float32)],
+    )(factors, strip, other)
     wet, named = local(
         margins_kernel,
         (values(ROWS, 2 * LANES), values(4, 3, ROWS, LANES)),
@@ -504,14 +536,15 @@
     atmos, final, *back = local(
         column_kernel,
         (values(*atmos_state.shape), values(FIELDS * ROWS, LANES)) + (values(FIELDS, LANES),) * 3,
-        [pltpu.VMEM] * 9,
+        [pltpu.VMEM] * 10,
         [
             pltpu.VMEM((LEVELS, 2 * ROWS, 3 * LANES), jnp.float32),
             pltpu.VMEM((3, FIELDS * WIDE, LANES), jnp.float32),
             pltpu.VMEM((ROWS * TABLE, LANES), jnp.float32),
             pltpu.VMEM((ROWS * FIELDS, LANES), jnp.float32),
+            pltpu.VMEM((LEVELS, 2 * ROWS, 3 * LANES), jnp.float32),
         ],
-    )(factors, strip, strip_beside, sheet, sheet_beside, other, halo_beside, wet, named)
+    )(factors, mixed, strip, strip_beside, sheet, sheet_beside, other, halo_beside, wet, named)
     one, two, three = (across("space", [z ^ k for z in range(4)], piece) for k, piece in zip((1, 2, 3), back))
     final = over("lev", 1, final)
     atmos_next, returned = local(

time: 23.6 us -> 23.6 us (level)
  transfers between devices with their start and end apart: 11 -> 11, of which waited for: 4 -> 5; matrix products, arithmetic and copies ran while one was open for 0% -> 0% of each run, Pallas kernels for 5% -> 5%
where the time goes in v8:
time: 23.6 us; the launch traced here: 23.3 us
  starting transfers between devices  14.6 us (62%)
  Pallas kernels  4.23 us (18%)
  waiting for transfers between devices  3.81 us (16%)
  between operations  0.7 us (3%)
    ppermute x7, starting transfers between devices, across(): return lax.ppermute(array, (axis, 'lev'), pairs)  12 us
    ppermute x3, waiting for transfers between devices, over(): lax.ppermute(array, axis, [(i, i ^ k) for i in range(lax.axis_size(axis))])  2.11 us
    ppermute x3, starting transfers between devices, over(): lax.ppermute(array, axis, [(i, i ^ k) for i in range(lax.axis_size(axis))])  1.9 us
    ppermute x7, waiting for transfers between devices, across(): return lax.ppermute(array, (axis, 'lev'), pairs)  1.7 us
    pallas_call x1, Pallas kernels, shards_by_columns(): local(column_kernel, (values(*atmos_state.shape), values(FIELDS * ROWS, L...  1.38 us
    pallas_call x1, Pallas kernels, shards_by_columns(): local(tables_kernel, (values(4, LETTER, LANES), values(STRIP, LANES), val...  1.01 us
    pallas_call x1, Pallas kernels, shards_by_columns(): local(returned_kernel, (values(*atmos_state.shape), values(FIELDS * 2 * R...  0.72 us
    ppermute x1, starting transfers between devices, shards_by_columns(): lax.ppermute(halo, ('comp', 'lev'), [(0, 3), (3, 0), (1, 2), (2, 1)])  0.65 us
  transfers between devices with their start and end apart: 11, of which 5 were waited for; matrix products, arithmetic and copies ran while one was open for 0% of the time, Pallas kernels for 5%

profile of v8, /device:TPU:0, one launch (start us, length us, event | category | flops | bytes accessed | tf_op | source)
XLA Modules:
  0.0 23.3 jit_solution(7450999743925491383)
XLA Ops:
  0.6 1.0 %shard_map.103 = (f32[4,48,128]{2,1,0:T(8,128)S(1)}, f32[104,128]{1,0:T(8,128)S(1)}, f32[8,8]{1,0:T(8,128)S(1)}, f32[8,16]{1,0:T(8,128)S(1)}) custom-call(f32[8,1,512]{2,1,0:T(1,128)} %refs_0_.1, s32[4,1,512]{2,1,0:T(1,128)} %refs_1_.1, f32[4,1,512]{2,1,0:T(1,128)} %refs_2_.1, s32[1,512]{1,0:T(1,128)} %refs_3_.1, f32[4,16,128]{2,1,0:T(8,128)} %refs_4_.1, ...), custom_call_target="tpu_custom_call" | custom-call | tf_op jit(solution)/shard_map/pallas_call | solution.py:510
  1.7 2.5 %collective-permute-start.2 = (f32[48,128]{1,0:T(8,128)S(1)}, f32[48,128]{1,0:T(8,128)S(1)}, u32[]{:S(2)}, u32[]{:S(2)}) collective-permute-start(f32[48,128]{1,0:T(8,128)S(1)} %get-tuple-element.29), channel_id=1, source_target_pairs={{0,5},{1,4},{4,13},{5,12},{8,1},{9,0},{12,9},{13,8},{2,7},{3,6},{6... | collective-permute-start | bytes 73736 | tf_op jit(solution)/shard_map/ppermute | solution.py:479
  4.2 2.8 %collective-permute-start.1 = (f32[48,128]{1,0:T(8,128)S(1)}, f32[48,128]{1,0:T(8,128)S(1)}, u32[]{:S(2)}, u32[]{:S(2)}) collective-permute-start(f32[48,128]{1,0:T(8,128)S(1)} %get-tuple-element.30), channel_id=1, source_target_pairs={{0,13},{1,12},{4,9},{5,8},{8,5},{9,4},{12,1},{13,0},{2,15},{3,14},... | collective-permute-start | bytes 73736 | tf_op jit(solution)/shard_map/ppermute | solution.py:479
  6.9 1.0 %collective-permute-start = (f32[48,128]{1,0:T(8,128)S(1)}, f32[48,128]{1,0:T(8,128)S(1)}, u32[]{:S(2)}, u32[]{:S(2)}) collective-permute-start(f32[48,128]{1,0:T(8,128)S(1)} %get-tuple-element.31), channel_id=1, source_target_pairs={{0,9},{1,8},{4,1},{5,0},{8,13},{9,12},{12,5},{13,4},{2,11},{3,10},... | collective-permute-start | bytes 73736 | tf_op jit(solution)/shard_map/ppermute | solution.py:479
  8.0 1.8 %collective-permute-start.4 = (f32[104,128]{1,0:T(8,128)S(1)}, f32[104,128]{1,0:T(8,128)S(1)}, u32[]{:S(2)}, u32[]{:S(2)}) collective-permute-start(f32[104,128]{1,0:T(8,128)S(1)} %get-tuple-element.18.strip_ref), channel_id=1, source_target_pairs={{0,3},{1,2},{2,1},{3,0},{4,7},{5,6},{6,5},{7,4},{8,11},{9,10},{10,... | collective-permute-start | bytes 159752 | tf_op jit(solution)/shard_map/ppermute | solution.py:479
  9.7 0.0 collective-permute-done.2.first_ref
  9.7 0.0 collective-permute-done.1.second_ref
  9.7 0.8 %collective-permute-done.last_ref = f32[48,128]{1,0:T(8,128)S(1)} collective-permute-done((f32[48,128]{1,0:T(8,128)S(1)}, f32[48,128]{1,0:T(8,128)S(1)}, u32[]{:S(2)}, u32[]{:S(2)}) %collective-permute-start) | collective-permute-done | bytes 24608 | tf_op jit(solution)/shard_map/ppermute | solution.py:479
  10.6 1.6 %collective-permute-start.5 = (f32[160,128]{1,0:T(8,128)S(1)}, f32[160,128]{1,0:T(8,128)S(1)}, u32[]{:S(2)}, u32[]{:S(2)}) collective-permute-start(f32[160,128]{1,0:T(8,128)S(1)} %shard_map.105.own_ref), channel_id=1, source_target_pairs={{0,2},{2,0},{1,3},{3,1},{4,6},{6,4},{5,7},{7,5},{8,10},{10,8},{9,1... | collective-permute-start | bytes 245768 | tf_op jit(solution)/shard_map/ppermute | solution.py:474
  12.2 0.0 collective-permute-start.3
  12.2 0.6 %collective-permute-start.6 = (f32[8,128]{1,0:T(8,128)S(1)}, f32[8,128]{1,0:T(8,128)S(1)}, u32[]{:S(2)}, u32[]{:S(2)}) collective-permute-start(f32[8,128]{1,0:T(8,128)S(1)} %slice.20), channel_id=1, source_target_pairs={{0,3},{3,0},{1,2},{2,1},{4,7},{7,4},{5,6},{6,5},{8,11},{11,8},{9,1... | collective-permute-start | bytes 12296 | tf_op jit(solution)/shard_map/ppermute | solution.py:521
  12.8 0.1 shard_map.104.factors_ref
  13.0 0.4 %collective-permute-done.3.other_ref = f32[96,128]{1,0:T(8,128)S(1)} collective-permute-done((f32[96,128]{1,0:T(8,128)S(1)}, f32[96,128]{1,0:T(8,128)S(1)}, u32[]{:S(2)}, u32[]{:S(2)}) %collective-permute-start.3) | collective-permute-done | bytes 49184 | tf_op jit(solution)/shard_map/ppermute | solution.py:474
  13.4 0.1 shard_map.106.mixed_own_ref
  13.5 0.0 collective-permute-done.4.strip_beside_ref
  13.5 1.7 %collective-permute-done.5.beside_ref = f32[160,128]{1,0:T(8,128)S(1)} collective-permute-done((f32[160,128]{1,0:T(8,128)S(1)}, f32[160,128]{1,0:T(8,128)S(1)}, u32[]{:S(2)}, u32[]{:S(2)}) %collective-permute-start.5) | collective-permute-done | bytes 81952 | tf_op jit(solution)/shard_map/ppermute | solution.py:474
  15.1 0.3 %shard_map.107 = (f32[8,256]{1,0:T(8,128)S(1)}, f32[4,3,8,128]{3,2,1,0:T(8,128)S(1)}) custom-call(f32[104,128]{1,0:T(8,128)S(1)} %get-tuple-element.18.strip_ref, f32[104,128]{1,0:T(8,128)S(1)} %collective-permute-done.4.strip_beside_ref, f32[160,128]{1,0:T(8,128)S(1)} %shard_map.105.own_ref, f32[160,128]{1,0:T(8,128)S(1)} %collective-permute-done.5.beside_ref), custom_call_target="tpu_custom_call" | custom-call | tf_op jit(solution)/shard_map/pallas_call | solution.py:530
  15.4 0.0 collective-permute-done.6.halo_beside_ref
  15.4 1.4 %shard_map.108 = (f32[4,16,128]{2,1,0:T(8,128)S(1)}, f32[64,128]{1,0:T(8,128)S(1)}, f32[8,128]{1,0:T(8,128)S(1)}, f32[8,128]{1,0:T(8,128)S(1)}, f32[8,128]{1,0:T(8,128)S(1)}) custom-call(f32[128,128]{1,0:T(8,128)S(1)} %shard_map.104.factors_ref, f32[8,16,128]{2,1,0:T(8,128)S(1)} %shard_map.106.mixed_own_ref, f32[104,128]{1,0:T(8,128)S(1)} %get-tuple-element.18.strip_ref, ...), custom_call_target="tpu_custom_call" | custom-call | tf_op jit(solution)/shard_map/pallas_call | solution.py:536
  16.8 0.3 %collective-permute-start.7 = (f32[64,128]{1,0:T(8,128)S(1)}, f32[64,128]{1,0:T(8,128)S(1)}, u32[]{:S(2)}, u32[]{:S(2)}) collective-permute-start(f32[64,128]{1,0:T(8,128)S(1)} %get-tuple-element.23), channel_id=1, source_target_pairs={{0,1},{1,0},{2,3},{3,2},{4,5},{5,4},{6,7},{7,6},{8,9},{9,8},{10,11... | collective-permute-start | bytes 98312 | tf_op jit(solution)/shard_map/ppermute | solution.py:474
  17.1 1.6 %collective-permute-start.8 = (f32[8,128]{1,0:T(8,128)S(1)}, f32[8,128]{1,0:T(8,128)S(1)}, u32[]{:S(2)}, u32[]{:S(2)}) collective-permute-start(f32[8,128]{1,0:T(8,128)S(1)} %get-tuple-element.25), channel_id=1, source_target_pairs={{0,13},{1,12},{4,9},{5,8},{8,5},{9,4},{12,1},{13,0},{2,15},{3,14},... | collective-permute-start | bytes 12296 | tf_op jit(solution)/shard_map/ppermute | solution.py:479
  18.8 0.6 %collective-permute-start.9 = (f32[8,128]{1,0:T(8,128)S(1)}, f32[8,128]{1,0:T(8,128)S(1)}, u32[]{:S(2)}, u32[]{:S(2)}) collective-permute-start(f32[8,128]{1,0:T(8,128)S(1)} %get-tuple-element.26), channel_id=1, source_target_pairs={{0,9},{1,8},{4,13},{5,12},{8,1},{9,0},{12,5},{13,4},{2,11},{3,10},... | collective-permute-start | bytes 12296 | tf_op jit(solution)/shard_map/ppermute | solution.py:479
  19.3 1.8 %collective-permute-start.10 = (f32[8,128]{1,0:T(8,128)S(1)}, f32[8,128]{1,0:T(8,128)S(1)}, u32[]{:S(2)}, u32[]{:S(2)}) collective-permute-start(f32[8,128]{1,0:T(8,128)S(1)} %get-tuple-element.27), channel_id=1, source_target_pairs={{0,5},{1,4},{4,1},{5,0},{8,13},{9,12},{12,9},{13,8},{2,7},{3,6},{6... | collective-permute-start | bytes 12296 | tf_op jit(solution)/shard_map/ppermute | solution.py:479
  21.1 0.0 collective-permute-done.7.final_ref
  21.1 0.7 %shard_map.109 = (f32[4,16,128]{2,1,0:T(8,128)}, f32[128,128]{1,0:T(8,128)}) custom-call(f32[4,16,128]{2,1,0:T(8,128)S(1)} %get-tuple-element.22.atmos_ref, f32[64,128]{1,0:T(8,128)S(1)} %collective-permute-done.7.final_ref, f32[4,3,8,128]{3,2,1,0:T(8,128)S(1)} %get-tuple-element.21.named_ref), custom_call_target="tpu_custom_call" | custom-call | tf_op jit(solution)/shard_map/pallas_call | solution.py:550
  21.8 0.2 collective-permute-done.8.three_ref
  22.0 0.7 %collective-permute-done.9.two_ref = f32[8,128]{1,0:T(8,128)S(1)} collective-permute-done((f32[8,128]{1,0:T(8,128)S(1)}, f32[8,128]{1,0:T(8,128)S(1)}, u32[]{:S(2)}, u32[]{:S(2)}) %collective-permute-start.9) | collective-permute-done | bytes 4128 | tf_op jit(solution)/shard_map/ppermute | solution.py:479
  22.7 0.0 collective-permute-done.10.one_ref
  22.7 0.6 %shard_map.110 = f32[8,1,512]{2,1,0:T(1,128)} custom-call(f32[8,128]{1,0:T(8,128)S(1)} %collective-permute-done.8.three_ref, f32[8,128]{1,0:T(8,128)S(1)} %collective-permute-done.9.two_ref, f32[8,128]{1,0:T(8,128)S(1)} %collective-permute-done.10.one_ref, f32[64,128]{1,0:T(8,128)S(1)} %collective-permute-done.7.final_ref), custom_call_target="tpu_custom_call" | custom-call | tf_op jit(solution)/shard_map/pallas_call | solution.py:555
  (5 shorter events, 0.0 us)
Async XLA Ops:
  1.7 8.1 %collective-permute-start.2 = (f32[48,128]{1,0:T(8,128)S(1)}, f32[48,128]{1,0:T(8,128)S(1)}, u32[]{:S(2)}, u32[]{:S(2)}) collective-permute-start(f32[48,128]{1,0:T(8,128)S(1)} %get-tuple-element.29), channel_id=1, source_target_pairs={{0,5},{1,4},{4,13},{5,12},{8,1},{9,0},{12,9},{13,8},{2,7},{3,6},{6... | collective-permute-start | bytes 73736 | tf_op jit(solution)/shard_map/ppermute | solution.py:479
  4.2 5.6 %collective-permute-start.1 = (f32[48,128]{1,0:T(8,128)S(1)}, f32[48,128]{1,0:T(8,128)S(1)}, u32[]{:S(2)}, u32[]{:S(2)}) collective-permute-start(f32[48,128]{1,0:T(8,128)S(1)} %get-tuple-element.30), channel_id=1, source_target_pairs={{0,13},{1,12},{4,9},{5,8},{8,5},{9,4},{12,1},{13,0},{2,15},{3,14},... | collective-permute-start | bytes 73736 | tf_op jit(solution)/shard_map/ppermute | solution.py:479
  6.9 3.6 %collective-permute-start = (f32[48,128]{1,0:T(8,128)S(1)}, f32[48,128]{1,0:T(8,128)S(1)}, u32[]{:S(2)}, u32[]{:S(2)}) collective-permute-start(f32[48,128]{1,0:T(8,128)S(1)} %get-tuple-element.31), channel_id=1, source_target_pairs={{0,9},{1,8},{4,1},{5,0},{8,13},{9,12},{12,5},{13,4},{2,11},{3,10},... | collective-permute-start | bytes 73736 | tf_op jit(solution)/shard_map/ppermute | solution.py:479
  8.0 5.5 %collective-permute-start.4 = (f32[104,128]{1,0:T(8,128)S(1)}, f32[104,128]{1,0:T(8,128)S(1)}, u32[]{:S(2)}, u32[]{:S(2)}) collective-permute-start(f32[104,128]{1,0:T(8,128)S(1)} %get-tuple-element.18.strip_ref), channel_id=1, source_target_pairs={{0,3},{1,2},{2,1},{3,0},{4,7},{5,6},{6,5},{7,4},{8,11},{9,10},{10,... | collective-permute-start | bytes 159752 | tf_op jit(solution)/shard_map/ppermute | solution.py:479
  10.6 4.5 %collective-permute-start.5 = (f32[160,128]{1,0:T(8,128)S(1)}, f32[160,128]{1,0:T(8,128)S(1)}, u32[]{:S(2)}, u32[]{:S(2)}) collective-permute-start(f32[160,128]{1,0:T(8,128)S(1)} %shard_map.105.own_ref), channel_id=1, source_target_pairs={{0,2},{2,0},{1,3},{3,1},{4,6},{6,4},{5,7},{7,5},{8,10},{10,8},{9,1... | collective-permute-start | bytes 245768 | tf_op jit(solution)/shard_map/ppermute | solution.py:474
  12.2 1.2 %collective-permute-start.3 = (f32[96,128]{1,0:T(8,128)S(1)}, f32[96,128]{1,0:T(8,128)S(1)}, u32[]{:S(2)}, u32[]{:S(2)}) collective-permute-start(f32[96,128]{1,0:T(8,128)S(1)} %pad_maximum_fusion), channel_id=1, source_target_pairs={{0,1},{1,0},{2,3},{3,2},{4,5},{5,4},{6,7},{7,6},{8,9},{9,8},{10,11... | collective-permute-start | bytes 147464 | tf_op jit(solution)/shard_map/ppermute | solution.py:474
  12.2 3.3 %collective-permute-start.6 = (f32[8,128]{1,0:T(8,128)S(1)}, f32[8,128]{1,0:T(8,128)S(1)}, u32[]{:S(2)}, u32[]{:S(2)}) collective-permute-start(f32[8,128]{1,0:T(8,128)S(1)} %slice.20), channel_id=1, source_target_pairs={{0,3},{3,0},{1,2},{2,1},{4,7},{7,4},{5,6},{6,5},{8,11},{11,8},{9,1... | collective-permute-start | bytes 12296 | tf_op jit(solution)/shard_map/ppermute | solution.py:521
  16.8 4.3 %collective-permute-start.7 = (f32[64,128]{1,0:T(8,128)S(1)}, f32[64,128]{1,0:T(8,128)S(1)}, u32[]{:S(2)}, u32[]{:S(2)}) collective-permute-start(f32[64,128]{1,0:T(8,128)S(1)} %get-tuple-element.23), channel_id=1, source_target_pairs={{0,1},{1,0},{2,3},{3,2},{4,5},{5,4},{6,7},{7,6},{8,9},{9,8},{10,11... | collective-permute-start | bytes 98312 | tf_op jit(solution)/shard_map/ppermute | solution.py:474
  17.1 4.8 %collective-permute-start.8 = (f32[8,128]{1,0:T(8,128)S(1)}, f32[8,128]{1,0:T(8,128)S(1)}, u32[]{:S(2)}, u32[]{:S(2)}) collective-permute-start(f32[8,128]{1,0:T(8,128)S(1)} %get-tuple-element.25), channel_id=1, source_target_pairs={{0,13},{1,12},{4,9},{5,8},{8,5},{9,4},{12,1},{13,0},{2,15},{3,14},... | collective-permute-start | bytes 12296 | tf_op jit(solution)/shard_map/ppermute | solution.py:479
  18.8 3.9 %collective-permute-start.9 = (f32[8,128]{1,0:T(8,128)S(1)}, f32[8,128]{1,0:T(8,128)S(1)}, u32[]{:S(2)}, u32[]{:S(2)}) collective-permute-start(f32[8,128]{1,0:T(8,128)S(1)} %get-tuple-element.26), channel_id=1, source_target_pairs={{0,9},{1,8},{4,13},{5,12},{8,1},{9,0},{12,5},{13,4},{2,11},{3,10},... | collective-permute-start | bytes 12296 | tf_op jit(solution)/shard_map/ppermute | solution.py:479
  19.3 3.4 %collective-permute-start.10 = (f32[8,128]{1,0:T(8,128)S(1)}, f32[8,128]{1,0:T(8,128)S(1)}, u32[]{:S(2)}, u32[]{:S(2)}) collective-permute-start(f32[8,128]{1,0:T(8,128)S(1)} %get-tuple-element.27), channel_id=1, source_target_pairs={{0,5},{1,4},{4,1},{5,0},{8,13},{9,12},{12,9},{13,8},{2,7},{3,6},{6... | collective-permute-start | bytes 12296 | tf_op jit(solution)/shard_map/ppermute | solution.py:479
